TPU v7x, 512 devices: a whole 4x4x16 slice. The times are simulated.
512 devices in a mesh: seq: 64 (over z, x_hi, core), head: 8 (over y, x_lo).
Axes of the slice: x: 4 (x_hi: 2, x_lo: 2; x = x_hi * 2 + x_lo), y: 4, z: 16, core: 2. Of those that a mesh axis runs over, the one named last changes fastest.
Arguments:
- stream_in: bfloat16 [64, 256, 2048], P('seq', None, 'head'), may hold values from -6 to 6
- row_query: bfloat16 [64, 256, 2048], P('seq', None, 'head'), may hold values from -240 to 240
- row_key: bfloat16 [64, 256, 2048], P('seq', None, 'head'), may hold values from -6 to 6
- row_value: bfloat16 [64, 256, 2048], P('seq', None, 'head'), may hold values from -6 to 6
- out_weight: bfloat16 [2048, 2048], P('head'), may hold values from -0.1875 to 0.1875
- norm_gain: float32 [2048], replicated, may hold values from 0.1 to 1.9
- qkv_weight: bfloat16 [2048, 3, 2048], P('seq', None, 'head'), may hold values from -5 to 5
Outputs:
- stream_out: bfloat16 [64, 256, 2048], P('seq', None, 'head')
- column_mixed: bfloat16 [64, 256, 2048], P('seq', None, 'head')
All inputs are finite; a program needn't handle non-finite values.
Results may differ from a plain program's by a relative error of at most 0.01295.
Values may be sent and summed in bfloat16 or wider, within the bound.
No kernel may reach another device: no remote copies, remote signals or barrier semaphores. Data moves between devices by JAX's collectives and lax.ppermute only.
A program may use at most 64 MiB of HBM per device.

v0:
```python
import jax
import jax.numpy as jnp
from jax import lax
from jax.sharding import PartitionSpec as P

HEAD = 128


STABILITY_FLOOR = 1e-05


def attend(query_rows, key_matrix_rows, value_rows, layout):
    if layout == "rows":
        score_form = "bqhe,bkhe->bhqk"
        mix_form = "bhqk,bkhe->bqhe"
        signal_length = query_rows.shape[1]
    else:
        score_form = "qbhe,kbhe->bhqk"
        mix_form = "bhqk,kbhe->qbhe"
        signal_length = query_rows.shape[0]
    logit_scores = jnp.einsum(
        score_form, query_rows, key_matrix_rows, preferred_element_type=jnp.float32
    ) * query_rows.shape[-1] ** (-0.5)
    causal = lax.broadcasted_iota(
        jnp.int32, (signal_length, signal_length), 0
    ) >= lax.broadcasted_iota(jnp.int32, (signal_length, signal_length), 1)
    logit_scores = jnp.where(causal[None, None], logit_scores, -1e30)
    highest = jnp.max(logit_scores, axis=-1, keepdims=True)
    attention_weight = jnp.exp(logit_scores - highest)
    attention_weight = (
        attention_weight / jnp.sum(attention_weight, axis=-1, keepdims=True)
    ).astype(jnp.bfloat16)
    return jnp.einsum(
        mix_form, attention_weight, value_rows, preferred_element_type=jnp.float32
    ).astype(jnp.bfloat16)


def normalize(shard, norm_gain):
    width = norm_gain.shape[0]
    local = shard.shape[2]
    value_rows = shard.astype(jnp.float32)
    totals = lax.psum(jnp.sum(value_rows * value_rows, axis=2, keepdims=True), "head")
    gain_part = lax.dynamic_slice_in_dim(norm_gain, lax.axis_index("head") * local, local, 0)
    normed = (value_rows * lax.rsqrt(totals / width + STABILITY_FLOOR) * gain_part).astype(
        jnp.bfloat16
    )
    return lax.all_gather(normed, "head", axis=2, tiled=True)


def project(normed, qkv_weight):
    leading_dims, trailing, width = normed.shape
    flat = normed.reshape(leading_dims * trailing, width)
    local = qkv_weight.shape[2]
    summed = jnp.einsum(
        "td,dkf->tkf",
        flat,
        lax.all_gather(qkv_weight, "seq", axis=0, tiled=True),
        preferred_element_type=jnp.float32,
    )
    return summed.astype(jnp.bfloat16).reshape(leading_dims, trailing, 3, local // HEAD, HEAD)


def on_device(stream_in, row_query, row_key, row_value, out_weight, norm_gain, qkv_weight):
    rows_here, steps, local = row_query.shape
    heads_here = local // HEAD

    def split_heads(array):
        return array.reshape(rows_here, steps, heads_here, HEAD)

    mixed_rows = attend(
        split_heads(row_query), split_heads(row_key), split_heads(row_value), "rows"
    )
    mixed_flat = mixed_rows.reshape(rows_here, steps, local)
    partial_value = jnp.dot(
        mixed_flat.reshape(rows_here * steps, local), out_weight, preferred_element_type=jnp.float32
    )
    summed = lax.psum_scatter(
        partial_value.reshape(rows_here, steps, out_weight.shape[1]),
        "head",
        scatter_dimension=2,
        tiled=True,
    )
    stream_out = (stream_in.astype(jnp.float32) + summed).astype(jnp.bfloat16)
    normed = normalize(stream_out, norm_gain)
    joined = project(normed, qkv_weight)
    mixed = attend(
        lax.all_to_all(joined[:, :, 0], "seq", split_axis=1, concat_axis=0, tiled=True),
        lax.all_to_all(joined[:, :, 1], "seq", split_axis=1, concat_axis=0, tiled=True),
        lax.all_to_all(joined[:, :, 2], "seq", split_axis=1, concat_axis=0, tiled=True),
        "columns",
    )
    column_mixed = lax.all_to_all(mixed, "seq", split_axis=0, concat_axis=1, tiled=True)
    return (stream_out, column_mixed.reshape(rows_here, steps, local))


def solution(mesh):
    in_specs = (
        P("seq", None, "head"),
        P("seq", None, "head"),
        P("seq", None, "head"),
        P("seq", None, "head"),
        P("head", None),
        P(),
        P("seq", None, "head"),
    )
    out_specs = (P("seq", None, "head"), P("seq", None, "head"))
    return jax.shard_map(
        on_device, mesh=mesh, in_specs=in_specs, out_specs=out_specs, check_vma=False
    )
```

profile of v0, /device:TPU:1, one launch (start us, length us, event | category | flops | bytes accessed | tf_op | source)
XLA Modules:
  0.0 404.2 jit_solution(15659920845564141013)
XLA Ops:
  7.2 0.0 copy-start
  7.2 0.0 reduce-scatter.2.cloned.1.call-start
  7.3 1.0 reshape.90
  8.3 0.9 reshape.91
  9.2 0.2 fusion.4
  9.5 0.3 fusion.28
  9.8 1.0 copy.43
  10.8 0.3 convolution_convert_fusion.1
  11.1 0.0 copy-start.2
  11.1 0.0 copy-done
  11.1 1.8 convolution_bitcast_fusion
  12.9 0.0 reduce-scatter.2.cloned.1.call-update
  13.0 0.0 all-gather.3.cloned.1.call-start
  13.0 0.8 dynamic_slice.3
  13.8 64.6 %reduce-scatter.2.cloned.1.call-done = f32[1,256,256]{2,1,0:T(8,128)} async-done(((f32[1,256,2048]{2,1,0:T(8,128)}), f32[1,256,256]{2,1,0:T(8,128)}) %reduce-scatter.2.cloned.1.call-update) | async-done | bytes 262160 | tf_op jit(solution)/shard_map/reduce_scatter | solution.py:77
  78.4 0.0 copy-done.2
  78.4 1.1 fusion.10
  79.5 0.0 copy-start.1
  79.5 13.1 %psum.7 = f32[1,256,1]{1,2,0:T(1,128)S(1)} all-reduce(f32[1,256,1]{1,2,0:T(1,128)S(1)} %bitcast.38), channel_id=1, replica_groups=mesh['seq'=64,'head'=8] {'head'}, use_global_device_ids=true, to_apply=%region_4.5 | all-reduce | flops 256 | bytes 2048 | tf_op jit(solution)/shard_map/psum | solution.py:42
  92.6 0.8 fusion.12
  93.4 0.0 all-gather.3.cloned.1.call-update
  93.4 0.0 all-gather.5.cloned.1.call-start
  93.4 0.7 all-gather.5.cloned.1.call-update
  94.1 45.8 %all-gather.3.cloned.1.call-done = bf16[1,256,2048]{2,1,0:T(8,128)(2,1)} async-done(((bf16[1,256,256]{2,1,0:T(8,128)(2,1)}), bf16[1,256,2048]{2,1,0:T(8,128)(2,1)}) %all-gather.3.cloned.1.call-update) | async-done | bytes 1048592 | tf_op jit(solution)/shard_map/all_gather | solution.py:47
  139.9 157.1 %all-gather.5.cloned.1.call-done = bf16[2048,3,256]{2,0,1:T(8,128)(2,1)} async-done(((bf16[32,3,256]{2,0,1:T(8,128)(2,1)}), bf16[2048,3,256]{2,0,1:T(8,128)(2,1)}) %all-gather.5.cloned.1.call-update) | async-done | bytes 3145744 | tf_op jit(solution)/shard_map/all_gather | solution.py:57
  297.0 3.5 convolution_convert_fusion
  300.6 0.0 copy-done.1
  300.6 0.8 copy.51
  301.4 7.9 %all-to-all-start.1 = ((bf16[1,256,2,128]{3,2,0,1:T(2,128)(2,1)}), bf16[1,256,2,128]{3,2,0,1:T(2,128)(2,1)S(1)}, u32[]{:S(2)}, u32[]{:S(2)}) async-start(bf16[1,256,2,128]{3,2,0,1:T(2,128)(2,1)} %bitcast.13), calls=%async_computation.2 | async-start | bytes 262144 | tf_op jit(solution)/shard_map/all_to_all | solution.py:87
  309.3 0.8 copy.52
  310.0 17.8 %all-to-all-done.1 = bf16[1,256,2,128]{3,2,0,1:T(2,128)(2,1)S(1)} async-done(((bf16[1,256,2,128]{3,2,0,1:T(2,128)(2,1)}), bf16[1,256,2,128]{3,2,0,1:T(2,128)(2,1)S(1)}, u32[]{:S(2)}, u32[]{:S(2)}) %all-to-all-start.1) | async-done | bytes 131104 | tf_op jit(solution)/shard_map/all_to_all | solution.py:87
  327.9 4.4 %all-to-all-start.2 = ((bf16[1,256,2,128]{3,2,0,1:T(2,128)(2,1)}), bf16[1,256,2,128]{3,2,0,1:T(2,128)(2,1)S(1)}, u32[]{:S(2)}, u32[]{:S(2)}) async-start(bf16[1,256,2,128]{3,2,0,1:T(2,128)(2,1)} %bitcast.15), calls=%async_computation.3 | async-start | bytes 262144 | tf_op jit(solution)/shard_map/all_to_all | solution.py:88
  332.3 0.8 copy.50
  333.1 17.9 %all-to-all-done.2 = bf16[1,256,2,128]{3,2,0,1:T(2,128)(2,1)S(1)} async-done(((bf16[1,256,2,128]{3,2,0,1:T(2,128)(2,1)}), bf16[1,256,2,128]{3,2,0,1:T(2,128)(2,1)S(1)}, u32[]{:S(2)}, u32[]{:S(2)}) %all-to-all-start.2) | async-done | bytes 131104 | tf_op jit(solution)/shard_map/all_to_all | solution.py:88
  351.0 4.4 %all-to-all-start = ((bf16[1,256,2,128]{3,2,0,1:T(2,128)(2,1)}), bf16[1,256,2,128]{3,2,0,1:T(2,128)(2,1)S(1)}, u32[]{:S(2)}, u32[]{:S(2)}) async-start(bf16[1,256,2,128]{3,2,0,1:T(2,128)(2,1)} %bitcast.11), calls=%async_computation.1 | async-start | bytes 262144 | tf_op jit(solution)/shard_map/all_to_all | solution.py:89
  355.5 0.2 fusion.6
  355.7 0.1 fusion.33
  355.8 18.4 %all-to-all-done = bf16[1,256,2,128]{3,2,0,1:T(2,128)(2,1)S(1)} async-done(((bf16[1,256,2,128]{3,2,0,1:T(2,128)(2,1)}), bf16[1,256,2,128]{3,2,0,1:T(2,128)(2,1)S(1)}, u32[]{:S(2)}, u32[]{:S(2)}) %all-to-all-start) | async-done | bytes 131104 | tf_op jit(solution)/shard_map/all_to_all | solution.py:89
  374.2 0.3 fusion.8
  374.4 0.1 copy.40
  374.6 22.3 %all_to_all.45 = bf16[64,4,2,128]{3,2,1,0:T(2,128)(2,1)S(1)} all-to-all(bf16[64,4,2,128]{3,2,1,0:T(2,128)(2,1)S(1)} %copy.40), channel_id=1, replica_groups=mesh['seq'=64,'head'=8] {'seq'}, dimensions={0} | all-to-all | bytes 262144 | tf_op jit(solution)/shard_map/all_to_all | solution.py:92
  396.9 0.7 reshape.96
  (4 shorter events, 0.1 us)
Async XLA Ops:
  7.2 4.0 copy-start
  7.2 71.2 %reduce-scatter.2.cloned.1.call-start = ((), (), s32[]{:S(2)}) async-start(), calls=%async_computation.5 | async-start | bytes 2359296 | tf_op jit(solution)/shard_map/reduce_scatter | solution.py:77
  11.1 67.3 %copy-start.2 = (bf16[1,256,256]{2,1,0:T(8,128)(2,1)S(1)}, bf16[1,256,256]{2,1,0:T(8,128)(2,1)}, u32[]{:S(2)}) copy-start(bf16[1,256,256]{2,1,0:T(8,128)(2,1)} %param.7) | copy-start | bytes 393220
  13.0 126.9 %all-gather.3.cloned.1.call-start = ((), (), s32[]{:S(2)}) async-start(), calls=%async_computation.6 | async-start | bytes 1179648 | tf_op jit(solution)/shard_map/all_gather | solution.py:47
  79.5 221.1 %copy-start.1 = (bf16[1,256,256]{2,1,0:T(8,128)(2,1)}, bf16[1,256,256]{2,1,0:T(8,128)(2,1)S(1)}, u32[]{:S(2)}) copy-start(bf16[1,256,256]{2,1,0:T(8,128)(2,1)S(1)} %get-tuple-element.3) | copy-start | bytes 393220
  93.4 203.6 %all-gather.5.cloned.1.call-start = ((), (), s32[]{:S(2)}) async-start(), calls=%async_computation.7 | async-start | bytes 3194880 | tf_op jit(solution)/shard_map/all_gather | solution.py:57
  301.4 26.5 %all-to-all-start.1 = ((bf16[1,256,2,128]{3,2,0,1:T(2,128)(2,1)}), bf16[1,256,2,128]{3,2,0,1:T(2,128)(2,1)S(1)}, u32[]{:S(2)}, u32[]{:S(2)}) async-start(bf16[1,256,2,128]{3,2,0,1:T(2,128)(2,1)} %bitcast.13), calls=%async_computation.2 | async-start | bytes 262144 | tf_op jit(solution)/shard_map/all_to_all | solution.py:87
  327.9 23.1 %all-to-all-start.2 = ((bf16[1,256,2,128]{3,2,0,1:T(2,128)(2,1)}), bf16[1,256,2,128]{3,2,0,1:T(2,128)(2,1)S(1)}, u32[]{:S(2)}, u32[]{:S(2)}) async-start(bf16[1,256,2,128]{3,2,0,1:T(2,128)(2,1)} %bitcast.15), calls=%async_computation.3 | async-start | bytes 262144 | tf_op jit(solution)/shard_map/all_to_all | solution.py:88
  351.0 23.1 %all-to-all-start = ((bf16[1,256,2,128]{3,2,0,1:T(2,128)(2,1)}), bf16[1,256,2,128]{3,2,0,1:T(2,128)(2,1)S(1)}, u32[]{:S(2)}, u32[]{:S(2)}) async-start(bf16[1,256,2,128]{3,2,0,1:T(2,128)(2,1)} %bitcast.11), calls=%async_computation.1 | async-start | bytes 262144 | tf_op jit(solution)/shard_map/all_to_all | solution.py:89
Sparse Core Ops, SparseCore 0:
  13.1 65.2 reduce-scatter.1
  93.5 46.3 all-gather.2
  143.2 153.7 all-gather.4
where the time goes:
time: 405 us; the launch traced here: 404 us
  waiting for transfers between devices  322 us (80%)
  blocking collectives  35.4 us (9%)
  starting transfers between devices  16.9 us (4%)
  between operations  13.9 us (3%)
  local copies, waits for them, and re-layouts  6.97 us (2%)
  matrix products  6.68 us (2%)
    all_gather x1, waiting for transfers between devices, project(): lax.all_gather(qkv_weight, 'seq', axis=0, tiled=True)  157 us
    reduce_scatter x1, waiting for transfers between devices, on_device(): lax.psum_scatter(partial_value.reshape(rows_here, steps, out_weight.shape...  64.6 us
    all_gather x1, waiting for transfers between devices, normalize(): return lax.all_gather(normed, 'head', axis=2, tiled=True)  45.8 us
    all_to_all x1, blocking collectives, on_device(): lax.all_to_all(mixed, 'seq', split_axis=0, concat_axis=1, tiled=True)  22.3 us
    all_to_all x1, waiting for transfers between devices, on_device(): lax.all_to_all(joined[:, :, 2], 'seq', split_axis=1, concat_axis=0, tiled...  18.4 us
    all_to_all x1, waiting for transfers between devices, on_device(): lax.all_to_all(joined[:, :, 1], 'seq', split_axis=1, concat_axis=0, tiled...  17.9 us
    all_to_all x1, waiting for transfers between devices, on_device(): lax.all_to_all(joined[:, :, 0], 'seq', split_axis=1, concat_axis=0, tiled...  17.8 us
    psum x1, blocking collectives, normalize(): lax.psum(jnp.sum(value_rows * value_rows, axis=2, keepdims=True), 'head')  13.1 us
  transfers between devices with their start and end apart: 6, of which 6 were waited for; matrix products, arithmetic and copies ran while one was open for 1% of the time, Pallas kernels for 0%

commit v1 on v0

v1 whole, which is shorter than its diff:
```python
import functools

import jax
import jax.numpy as jnp
from jax import lax
from jax.experimental import pallas as pl
from jax.experimental.pallas import tpu as pltpu
from jax.sharding import Mesh, PartitionSpec as P

HEAD = 128
EPS = 1e-05
NEG = -1e30
SEQ = ("z", "xh", "c")
HD = ("y", "xl")


def softmax_mix(q, k, v, mask):
    s = lax.dot_general(q, k, (((1,), (1,)), ((), ())), preferred_element_type=jnp.float32)
    s = jnp.where(mask, s * (HEAD ** -0.5), NEG)
    p = jnp.exp(s - jnp.max(s, axis=-1, keepdims=True))
    w = (p / jnp.sum(p, axis=-1, keepdims=True)).astype(jnp.bfloat16)
    return jnp.dot(w, v, preferred_element_type=jnp.float32).astype(jnp.bfloat16)


def row_kernel(q_ref, k_ref, v_ref, w_ref, out_ref):
    n = q_ref.shape[0]
    mask = lax.broadcasted_iota(jnp.int32, (n, n), 0) >= lax.broadcasted_iota(jnp.int32, (n, n), 1)
    mixed = []
    for h in range(q_ref.shape[1] // HEAD):
        cols = slice(h * HEAD, (h + 1) * HEAD)
        mixed.append(softmax_mix(q_ref[:, cols], k_ref[:, cols], v_ref[:, cols], mask))
    mixed = jnp.concatenate(mixed, axis=1)
    width = out_ref.shape[2]
    for part in range(out_ref.shape[0]):
        out_ref[part] = jnp.dot(
            mixed, w_ref[:, part * width : (part + 1) * width], preferred_element_type=jnp.float32
        ).astype(jnp.bfloat16)


def row_part(q, k, v, w, heads):
    n, local = q.shape
    width = w.shape[1] // heads
    return pl.pallas_call(
        row_kernel,
        out_shape=jax.ShapeDtypeStruct((heads, n, width), jnp.bfloat16),
        in_specs=[pl.BlockSpec(memory_space=pltpu.VMEM)] * 4,
        out_specs=pl.BlockSpec(memory_space=pltpu.VMEM),
        compiler_params=pltpu.CompilerParams(vmem_limit_bytes=32 * 1024 * 1024),
        cost_estimate=pl.CostEstimate(
            flops=2 * n * local * (n * 2 + w.shape[1]), bytes_accessed=3 * 2**20, transcendentals=2 * n * n
        ),
        name="row_attention",
    )(q, k, v, w)


def column_kernel(where_ref, x_ref, gain_ref, own_ref, other_ref, out_ref, w_ref, normed_ref, sems):
    xh = where_ref[0]
    core = where_ref[1]
    copies = []
    for side, ref in enumerate((own_ref, other_ref)):
        c = core if side == 0 else 1 - core
        for g in range(2):
            x = xh if g == 0 else 1 - xh
            for j in range(3):
                copies.append(
                    pltpu.make_async_copy(ref.at[:, g, j], w_ref.at[j, :, x, c], sems.at[side, g, j])
                )
    for copy in copies:
        copy.start()
    heads, n, local = x_ref.shape
    total = jnp.zeros((n, 1), jnp.float32)
    for h in range(heads):
        x = x_ref[h].astype(jnp.float32)
        total = total + jnp.sum(x * x, axis=1, keepdims=True)
    scale = lax.rsqrt(total / (heads * local) + EPS)
    for h in range(heads):
        cols = slice(h * local, (h + 1) * local)
        normed_ref[:, cols] = (x_ref[h].astype(jnp.float32) * scale * gain_ref[:, cols]).astype(jnp.bfloat16)
    for copy in copies:
        copy.wait()
    parts = []
    for j in range(3):
        w = w_ref[j].reshape(heads * local, local)
        parts.append(
            jnp.dot(normed_ref[...], w, preferred_element_type=jnp.float32).astype(jnp.bfloat16)
        )
    q, k, v = parts
    t0 = lax.broadcasted_iota(jnp.int32, (n, n), 0)
    t1 = lax.broadcasted_iota(jnp.int32, (n, n), 1)
    cols_here = 4
    mask = (t0 >= t1) & ((t0 & (cols_here - 1)) == (t1 & (cols_here - 1)))
    for h in range(local // HEAD):
        cols = slice(h * HEAD, (h + 1) * HEAD)
        out_ref[:, cols] = softmax_mix(q[:, cols], k[:, cols], v[:, cols], mask)


def column_part(where, x, gain, own, other):
    heads, n, local = x.shape
    nz, nx, _, rows, _ = own.shape
    vm = pl.BlockSpec(memory_space=pltpu.VMEM)
    anyspace = pl.BlockSpec(memory_space=pl.ANY)
    return pl.pallas_call(
        column_kernel,
        out_shape=jax.ShapeDtypeStruct((n, local), jnp.bfloat16),
        in_specs=[pl.BlockSpec(memory_space=pltpu.SMEM), vm, vm, anyspace, anyspace],
        out_specs=vm,
        scratch_shapes=[
            pltpu.VMEM((3, nz, nx, 2, rows, local), jnp.bfloat16),
            pltpu.VMEM((n, heads * local), jnp.bfloat16),
            pltpu.SemaphoreType.DMA((2, 2, 3)),
        ],
        compiler_params=pltpu.CompilerParams(vmem_limit_bytes=40 * 1024 * 1024),
        cost_estimate=pl.CostEstimate(
            flops=2 * n * heads * local * 3 * local, bytes_accessed=5 * 2**20, transcendentals=2 * n * n
        ),
        name="column_attention",
    )(where, x, gain, own, other)


def on_device(stream_in, row_query, row_key, row_value, out_weight, norm_gain, qkv_weight):
    _, steps, local = row_query.shape
    heads = norm_gain.shape[0] // local
    seq = 64
    here = steps // seq

    w = jnp.transpose(qkv_weight, (1, 0, 2))
    w2 = lax.ppermute(w, "xh", [(0, 1), (1, 0)])

    partial = row_part(row_query[0], row_key[0], row_value[0], out_weight, heads)

    pair = jnp.stack([w, w2])
    own = lax.all_gather(pair, "z", axis=0)

    parts = lax.all_to_all(partial, HD, 0, 0, tiled=True)
    stream = stream_in[0].astype(jnp.float32) + jnp.sum(parts.astype(jnp.float32), axis=0)
    stream_out = stream.astype(jnp.bfloat16)
    columns = lax.all_to_all(stream_out.reshape(seq, here, local), SEQ, 0, 0, tiled=True)
    columns = columns.reshape(seq * here, local)
    x = lax.all_to_all(jnp.broadcast_to(columns[None], (heads,) + columns.shape), HD, 0, 0, tiled=True)
    own, x = lax.optimization_barrier((own, x))
    other = lax.ppermute(own, "c", [(0, 1), (1, 0)])
    where = jnp.stack([lax.axis_index("xh"), lax.axis_index("c")]).astype(jnp.int32)
    mixed = column_part(where, x, norm_gain.reshape(1, -1), own, other)
    back = lax.all_to_all(mixed.reshape(seq, here, local), SEQ, 0, 0, tiled=True)
    return (stream_out[None], back.reshape(1, steps, local))


def solution(mesh):
    fine = Mesh(mesh.devices.reshape(16, 2, 2, 4, 2), SEQ + HD)
    rows = P(SEQ, None, HD)
    return jax.shard_map(
        on_device,
        mesh=fine,
        in_specs=(rows, rows, rows, rows, P(HD, None), P(), rows),
        out_specs=(rows, rows),
        check_vma=False,
    )
```

time: 405 us -> 145 us (0.36)
  waiting for transfers between devices: 322 us -> 33.1 us
  blocking collectives: 35.4 us -> 62 us
  matrix products: 6.68 us -> 0 us
  Pallas kernels: 0 us -> 5.49 us
    all_gather x2 -> x1, waiting for transfers between devices: 203 us -> 0.01 us  [on_device(): own = lax.all_gather(pair, 'z', axis=0)]
    reduce_scatter x1 -> x0, waiting for transfers between devices: 64.6 us -> none  [on_device(): lax.psum_scatter(partial_value.reshape(rows_here, steps, out_weight.shape...]
    all_to_all x1 -> x2, blocking collectives: 22.3 us -> 62 us  [the longest x1 44 us: on_device(): lax.all_to_all(stream_out.reshape(seq, here, local), SEQ, 0, 0, tiled=True)]
    all_to_all x3 -> x2, waiting for transfers between devices: 54.1 us -> 28.3 us  [the longest x1 17.9 us: on_device(): lax.all_to_all(mixed.reshape(seq, here, local), SEQ, 0, 0, tiled=True)]
    psum x1 -> x0, blocking collectives: 13.1 us -> none  [normalize(): lax.psum(jnp.sum(value_rows * value_rows, axis=2, keepdims=True), 'head')]
    ppermute x0 -> x2, starting transfers between devices: none -> 8.45 us  [the longest x1 5.48 us: on_device(): w2 = lax.ppermute(w, 'xh', [(0, 1), (1, 0)])]
    dot_general x6 -> x0, matrix products: 6.33 us -> none  [the longest x1 3.55 us: project(): jnp.einsum('td,dkf->tkf', flat, lax.all_gather(qkv_weight, 'seq', axis=0,...]
    pallas_call x0 -> x2, Pallas kernels: none -> 5.49 us  [the longest x1 3.22 us: column_part(): pl.pallas_call(column_kernel, out_shape=jax.ShapeDtypeStruct((n, local),...]
  transfers between devices with their start and end apart: 6 -> 5, of which waited for: 6 -> 4; matrix products, arithmetic and copies ran while one was open for 1% -> 1% of each run, Pallas kernels for 0% -> 2%
where the time goes in v1:
time: 145 us; the launch traced here: 144 us
  blocking collectives  62 us (43%)
  waiting for transfers between devices  33.1 us (23%)
  starting transfers between devices  19.9 us (14%)
  between operations  14.1 us (10%)
  local copies, waits for them, and re-layouts  6.97 us (5%)
  Pallas kernels  5.49 us (4%)
  other arithmetic  2.42 us (2%)
    all_to_all x1, blocking collectives, on_device(): lax.all_to_all(stream_out.reshape(seq, here, local), SEQ, 0, 0, tiled=True)  44 us
    all_to_all x1, blocking collectives, on_device(): lax.all_to_all(jnp.broadcast_to(columns[None], (heads,) + columns.shape),...  18 us
    all_to_all x1, waiting for transfers between devices, on_device(): lax.all_to_all(mixed.reshape(seq, here, local), SEQ, 0, 0, tiled=True)  17.9 us
    all_to_all x1, waiting for transfers between devices, on_device(): parts = lax.all_to_all(partial, HD, 0, 0, tiled=True)  10.4 us
    all_to_all x1, starting transfers between devices, on_device(): lax.all_to_all(mixed.reshape(seq, here, local), SEQ, 0, 0, tiled=True)  5.99 us
    ppermute x1, starting transfers between devices, on_device(): w2 = lax.ppermute(w, 'xh', [(0, 1), (1, 0)])  5.48 us
    all_to_all x1, starting transfers between devices, on_device(): parts = lax.all_to_all(partial, HD, 0, 0, tiled=True)  5.46 us
    unnamed x14, local copies, waits for them, and re-layouts  5.35 us
  transfers between devices with their start and end apart: 5, of which 4 were waited for; matrix products, arithmetic and copies ran while one was open for 1% of the time, Pallas kernels for 2%

profile of v1, /device:TPU:1, one launch (start us, length us, event | category | flops | bytes accessed | tf_op | source)
XLA Modules:
  0.0 144.1 jit_solution(1235095332163348727)
XLA Ops:
  7.2 0.0 all-gather.3.cloned.1.call-start
  7.2 5.5 %collective-permute-start = (bf16[3,32,256]{2,1,0:T(8,128)(2,1)}, bf16[3,32,256]{2,1,0:T(8,128)(2,1)S(1)}, u32[]{:S(2)}, u32[]{:S(2)}) collective-permute-start(bf16[3,32,256]{2,1,0:T(8,128)(2,1)} %bitcast.21), channel_id=1, source_target_pairs={{0,16},{16,0},{1,17},{17,1},{2,18},{18,2},{3,19},{19,3},{4,20},{20... | collective-permute-start | bytes 147464 | tf_op jit(solution)/shard_map/ppermute | solution.py:127
  12.7 1.7 %collective-permute-done = bf16[3,32,256]{2,1,0:T(8,128)(2,1)S(1)} collective-permute-done((bf16[3,32,256]{2,1,0:T(8,128)(2,1)}, bf16[3,32,256]{2,1,0:T(8,128)(2,1)S(1)}, u32[]{:S(2)}, u32[]{:S(2)}) %collective-permute-start) | collective-permute-done | bytes 49184 | tf_op jit(solution)/shard_map/ppermute | solution.py:127
  14.4 1.4 %pad_maximum_fusion = bf16[2,3,32,256]{3,2,1,0:T(8,128)(2,1)} fusion(bf16[1,3,32,256]{3,2,1,0:T(8,128)(2,1)S(1)} %bitcast.23, bf16[1,3,32,256]{3,2,1,0:T(8,128)(2,1)} %bitcast.22), kind=kLoop, calls=%fused_computation.4 | loop fusion | flops 49152 | bytes 196608 | tf_op jit(solution)/shard_map/stack | solution.py:131
  15.8 0.0 all-gather.3.cloned.1.call-update
  15.8 0.0 copy-start.1
  15.9 1.2 copy-done.1
  17.1 0.0 copy-start.2
  17.1 0.9 copy-done.2
  18.0 0.0 copy-start.3
  18.0 0.9 copy-done.3
  18.9 0.0 copy-start.4
  18.9 0.9 copy-done.4
  19.8 2.3 %row_attention.1 = bf16[8,256,256]{2,1,0:T(8,128)(2,1)} custom-call(bf16[256,256]{1,0:T(8,128)(2,1)S(1)} %bitcast.17, bf16[256,256]{1,0:T(8,128)(2,1)S(1)} %bitcast.18, bf16[256,256]{1,0:T(8,128)(2,1)S(1)} %bitcast.19, bf16[256,2048]{1,0:T(8,128)(2,1)S(1)} %copy-done.1), custom_call_target="tpu_custom_call" | custom-call | flops 335544320 | bytes 3145728 | tf_op jit(solution)/shard_map/row_attention/pallas_call | solution.py:43
  22.1 0.0 copy-start.6
  22.1 5.5 %all-to-all-start = ((bf16[8,256,256]{2,1,0:T(8,128)(2,1)}), bf16[8,256,256]{2,1,0:T(8,128)(2,1)S(1)}, u32[]{:S(2)}, u32[]{:S(2)}) async-start(bf16[8,256,256]{2,1,0:T(8,128)(2,1)} %row_attention.1), calls=%async_computation | async-start | bytes 2097152 | tf_op jit(solution)/shard_map/all_to_all | solution.py:134
  27.5 0.0 copy-done.6
  27.5 0.1 reshape.23
  27.6 10.4 %all-to-all-done = bf16[8,256,256]{2,1,0:T(8,128)(2,1)S(1)} async-done(((bf16[8,256,256]{2,1,0:T(8,128)(2,1)}), bf16[8,256,256]{2,1,0:T(8,128)(2,1)S(1)}, u32[]{:S(2)}, u32[]{:S(2)}) %all-to-all-start) | async-done | bytes 1048608 | tf_op jit(solution)/shard_map/all_to_all | solution.py:134
  38.0 0.1 convert_reduce_fusion
  38.1 0.1 reduce_sum.15
  38.2 0.1 add_convert_fusion
  38.3 44.0 %all_to_all.20 = bf16[64,4,256]{2,1,0:T(4,128)(2,1)S(1)} all-to-all(bf16[64,4,256]{2,1,0:T(4,128)(2,1)S(1)} %add_convert_fusion), channel_id=1, replica_groups=mesh['z'=16,'xh'=2,'c'=2,'y'=4,'xl'=2] {'z','xh','c'}, dimensions={0} | all-to-all | bytes 262144 | tf_op jit(solution)/shard_map/all_to_all | solution.py:137
  82.3 0.0 copy-start.5
  82.3 0.1 broadcast_in_dim.9
  82.4 18.0 %all_to_all.21.x_ref = bf16[8,256,256]{2,1,0:T(8,128)(2,1)S(1)} all-to-all(bf16[8,256,256]{2,1,0:T(8,128)(2,1)S(1)} %broadcast_in_dim.9), channel_id=1, replica_groups=mesh['z'=16,'xh'=2,'c'=2,'y'=4,'xl'=2] {'y','xl'}, dimensions={0} | all-to-all | bytes 2097152 | tf_op jit(solution)/shard_map/all_to_all | solution.py:139
  100.4 0.0 all-gather.3.cloned.1.call-done
  100.4 3.0 %collective-permute-start.1 = (bf16[16,2,3,32,256]{4,3,2,1,0:T(8,128)(2,1)}, bf16[16,2,3,32,256]{4,3,2,1,0:T(8,128)(2,1)S(1)}, u32[]{:S(2)}, u32[]{:S(2)}) collective-permute-start(bf16[16,2,3,32,256]{4,3,2,1,0:T(8,128)(2,1)} %bitcast.15), channel_id=1, source_target_pairs={{0,8},{8,0},{1,9},{9,1},{2,10},{10,2},{3,11},{11,3},{4,12},{12,4},... | collective-permute-start | bytes 4718600 | tf_op jit(solution)/shard_map/ppermute | solution.py:141
  103.4 0.1 pad_add_fusion.where_ref
  103.4 3.1 %collective-permute-done.1.other_ref = bf16[16,2,3,32,256]{4,3,2,1,0:T(8,128)(2,1)S(1)} collective-permute-done((bf16[16,2,3,32,256]{4,3,2,1,0:T(8,128)(2,1)}, bf16[16,2,3,32,256]{4,3,2,1,0:T(8,128)(2,1)S(1)}, u32[]{:S(2)}, u32[]{:S(2)}) %collective-permute-start.1) | collective-permute-done | bytes 1572896 | tf_op jit(solution)/shard_map/ppermute | solution.py:141
  106.6 0.0 copy-done.5
  106.6 0.0 copy-start
  106.6 1.4 copy-done
  108.0 3.2 %column_attention.1 = bf16[256,256]{1,0:T(8,128)(2,1)S(1)} custom-call(s32[2]{0:T(128)S(1)} %pad_add_fusion.where_ref, bf16[8,256,256]{2,1,0:T(8,128)(2,1)S(1)} %all_to_all.21.x_ref, f32[1,2048]{1,0:T(1,128)S(1)} %bitcast.20, bf16[16,2,3,32,256]{4,3,2,1,0:T(8,128)(2,1)S(1)} %bitcast.16, bf16[16,2,3,32,256]{4,3,2,1,0:T(8,128)(2,1)S(1)} %collective-permute-done.1.other_ref), custom_call_target="tpu_custom_call" | custom-call | flops 805306368 | bytes 5242880 | tf_op jit(solution)/shard_map/column_attention/pallas_call | solution.py:102
  111.2 0.7 reshape.21
  111.9 6.0 %all-to-all-start.3 = ((bf16[64,4,256]{2,1,0:T(4,128)(2,1)}), bf16[64,4,256]{2,1,0:T(4,128)(2,1)S(1)}, u32[]{:S(2)}, u32[]{:S(2)}) async-start(bf16[64,4,256]{2,1,0:T(4,128)(2,1)} %reshape.21), calls=%async_computation.3 | async-start | bytes 262144 | tf_op jit(solution)/shard_map/all_to_all | solution.py:144
  117.9 0.7 fusion
  118.6 17.9 %all-to-all-done.3 = bf16[64,4,256]{2,1,0:T(4,128)(2,1)S(1)} async-done(((bf16[64,4,256]{2,1,0:T(4,128)(2,1)}), bf16[64,4,256]{2,1,0:T(4,128)(2,1)S(1)}, u32[]{:S(2)}, u32[]{:S(2)}) %all-to-all-start.3) | async-done | bytes 131104 | tf_op jit(solution)/shard_map/all_to_all | solution.py:144
  136.5 0.7 reshape.22
  (1 shorter events, 0.0 us)
Async XLA Ops:
  7.2 93.2 %all-gather.3.cloned.1.call-start = ((), (), s32[]{:S(2)}) async-start(), calls=%async_computation.4 | async-start | bytes 1671168 | tf_op jit(solution)/shard_map/all_gather | solution.py:132
  7.2 7.2 %collective-permute-start = (bf16[3,32,256]{2,1,0:T(8,128)(2,1)}, bf16[3,32,256]{2,1,0:T(8,128)(2,1)S(1)}, u32[]{:S(2)}, u32[]{:S(2)}) collective-permute-start(bf16[3,32,256]{2,1,0:T(8,128)(2,1)} %bitcast.21), channel_id=1, source_target_pairs={{0,16},{16,0},{1,17},{17,1},{2,18},{18,2},{3,19},{19,3},{4,20},{20... | collective-permute-start | bytes 147464 | tf_op jit(solution)/shard_map/ppermute | solution.py:127
  15.8 1.2 copy-start.1
  17.1 0.9 copy-start.2
  18.0 0.9 copy-start.3
  18.9 0.9 copy-start.4
  22.1 5.5 %copy-start.6 = (bf16[1,256,256]{2,1,0:T(8,128)(2,1)S(1)}, bf16[1,256,256]{2,1,0:T(8,128)(2,1)}, u32[]{:S(2)}) copy-start(bf16[1,256,256]{2,1,0:T(8,128)(2,1)} %param.7) | copy-start | bytes 393220
  22.1 15.9 %all-to-all-start = ((bf16[8,256,256]{2,1,0:T(8,128)(2,1)}), bf16[8,256,256]{2,1,0:T(8,128)(2,1)S(1)}, u32[]{:S(2)}, u32[]{:S(2)}) async-start(bf16[8,256,256]{2,1,0:T(8,128)(2,1)} %row_attention.1), calls=%async_computation | async-start | bytes 2097152 | tf_op jit(solution)/shard_map/all_to_all | solution.py:134
  82.3 24.3 %copy-start.5 = (f32[2048]{0:T(1024)S(1)}, f32[2048]{0:T(1024)}, u32[]{:S(2)}) copy-start(f32[2048]{0:T(1024)} %param.12) | copy-start | bytes 24580
  100.4 6.2 %collective-permute-start.1 = (bf16[16,2,3,32,256]{4,3,2,1,0:T(8,128)(2,1)}, bf16[16,2,3,32,256]{4,3,2,1,0:T(8,128)(2,1)S(1)}, u32[]{:S(2)}, u32[]{:S(2)}) collective-permute-start(bf16[16,2,3,32,256]{4,3,2,1,0:T(8,128)(2,1)} %bitcast.15), channel_id=1, source_target_pairs={{0,8},{8,0},{1,9},{9,1},{2,10},{10,2},{3,11},{11,3},{4,12},{12,4},... | collective-permute-start | bytes 4718600 | tf_op jit(solution)/shard_map/ppermute | solution.py:141
  106.6 1.4 copy-start
  111.9 24.6 %all-to-all-start.3 = ((bf16[64,4,256]{2,1,0:T(4,128)(2,1)}), bf16[64,4,256]{2,1,0:T(4,128)(2,1)S(1)}, u32[]{:S(2)}, u32[]{:S(2)}) async-start(bf16[64,4,256]{2,1,0:T(4,128)(2,1)} %reshape.21), calls=%async_computation.3 | async-start | bytes 262144 | tf_op jit(solution)/shard_map/all_to_all | solution.py:144
Sparse Core Ops, SparseCore 0:
  16.0 73.0 all-gather.2

commit v2 on v1

--- a/solution.py
+++ b/solution.py
@@ -10,6 +10,7 @@
 HEAD = 128
 EPS = 1e-05
 NEG = -1e30
+VMEM_BYTES = 60 * 1024 * 1024
 SEQ = ("z", "xh", "c")
 HD = ("y", "xl")
 
@@ -22,7 +23,15 @@
     return jnp.dot(w, v, preferred_element_type=jnp.float32).astype(jnp.bfloat16)
 
 
-def row_kernel(q_ref, k_ref, v_ref, w_ref, out_ref):
+def row_kernel(q_hbm, k_hbm, v_hbm, w_hbm, out_ref, q_ref, k_ref, v_ref, w_ref, sems):
+    copies = [
+        pltpu.make_async_copy(src, dst, sems.at[i])
+        for i, (src, dst) in enumerate(((q_hbm, q_ref), (k_hbm, k_ref), (v_hbm, v_ref), (w_hbm, w_ref)))
+    ]
+    for copy in copies:
+        copy.start()
+    for copy in copies[:3]:
+        copy.wait()
     n = q_ref.shape[0]
     mask = lax.broadcasted_iota(jnp.int32, (n, n), 0) >= lax.broadcasted_iota(jnp.int32, (n, n), 1)
     mixed = []
@@ -30,6 +39,7 @@
         cols = slice(h * HEAD, (h + 1) * HEAD)
         mixed.append(softmax_mix(q_ref[:, cols], k_ref[:, cols], v_ref[:, cols], mask))
     mixed = jnp.concatenate(mixed, axis=1)
+    copies[3].wait()
     width = out_ref.shape[2]
     for part in range(out_ref.shape[0]):
         out_ref[part] = jnp.dot(
@@ -40,12 +50,14 @@
 def row_part(q, k, v, w, heads):
     n, local = q.shape
     width = w.shape[1] // heads
+    tile = pltpu.VMEM((n, local), jnp.bfloat16)
     return pl.pallas_call(
         row_kernel,
         out_shape=jax.ShapeDtypeStruct((heads, n, width), jnp.bfloat16),
-        in_specs=[pl.BlockSpec(memory_space=pltpu.VMEM)] * 4,
+        in_specs=[pl.BlockSpec(memory_space=pltpu.HBM)] * 4,
         out_specs=pl.BlockSpec(memory_space=pltpu.VMEM),
-        compiler_params=pltpu.CompilerParams(vmem_limit_bytes=32 * 1024 * 1024),
+        scratch_shapes=[tile, tile, tile, pltpu.VMEM(w.shape, jnp.bfloat16), pltpu.SemaphoreType.DMA((4,))],
+        compiler_params=pltpu.CompilerParams(vmem_limit_bytes=VMEM_BYTES),
         cost_estimate=pl.CostEstimate(
             flops=2 * n * local * (n * 2 + w.shape[1]), bytes_accessed=3 * 2**20, transcendentals=2 * n * n
         ),
@@ -53,20 +65,52 @@
     )(q, k, v, w)
 
 
-def column_kernel(where_ref, x_ref, gain_ref, own_ref, other_ref, out_ref, w_ref, normed_ref, sems):
-    xh = where_ref[0]
-    core = where_ref[1]
-    copies = []
+def pack_kernel(count, *refs):
+    pieces, out_ref = refs[:count], refs[-1]
+    at = 0
+    for ref in pieces:
+        for i in range(ref.shape[0]):
+            out_ref[at + i] = ref[i]
+        at += ref.shape[0]
+
+
+def pack(*pieces, event=()):
+    total = sum(p.shape[0] for p in pieces)
+    shape = (total,) + pieces[0].shape[1:]
+    size = 4
+    for d in shape:
+        size *= d
+    vm = pl.BlockSpec(memory_space=pltpu.VMEM)
+    return pl.pallas_call(
+        functools.partial(pack_kernel, len(pieces)),
+        out_shape=jax.ShapeDtypeStruct(shape, pieces[0].dtype),
+        in_specs=[vm] * len(pieces) + [pl.BlockSpec(memory_space=pl.ANY)] * len(event),
+        out_specs=vm,
+        compiler_params=pltpu.CompilerParams(vmem_limit_bytes=16 * 1024 * 1024),
+        cost_estimate=pl.CostEstimate(flops=0, bytes_accessed=size, transcendentals=0),
+        name="pack",
+    )(*pieces, *event)
+
+
+FOUR = (0, 4, -4, 8)
+SLOTS = (
+    [(f, o) for o in (0, 1) for f in FOUR]
+    + [(1 + f, o) for o in (0, 1) for f in FOUR]
+    + [(-1 + f, o) for o in (0, 1) for f in FOUR]
+    + [(2 + f, 0) for f in FOUR]
+    + [(-2 + f, 1) for f in FOUR]
+)
+
+
+def column_kernel(where_ref, x_ref, gain_ref, own_ref, other_ref, out_ref, w_ref, normed_ref):
+    z, xh, core = where_ref[0], where_ref[1], where_ref[2]
     for side, ref in enumerate((own_ref, other_ref)):
         c = core if side == 0 else 1 - core
-        for g in range(2):
-            x = xh if g == 0 else 1 - xh
+        for i, (off, flip) in enumerate(SLOTS):
+            zi = lax.rem(z + (off + 16), 16)
+            xi = 1 - xh if flip else xh
             for j in range(3):
-                copies.append(
-                    pltpu.make_async_copy(ref.at[:, g, j], w_ref.at[j, :, x, c], sems.at[side, g, j])
-                )
-    for copy in copies:
-        copy.start()
+                w_ref[j, zi, xi, c] = ref[i, j]
     heads, n, local = x_ref.shape
     total = jnp.zeros((n, 1), jnp.float32)
     for h in range(heads):
@@ -76,8 +120,6 @@
     for h in range(heads):
         cols = slice(h * local, (h + 1) * local)
         normed_ref[:, cols] = (x_ref[h].astype(jnp.float32) * scale * gain_ref[:, cols]).astype(jnp.bfloat16)
-    for copy in copies:
-        copy.wait()
     parts = []
     for j in range(3):
         w = w_ref[j].reshape(heads * local, local)
@@ -96,18 +138,16 @@
 
 def column_part(where, x, gain, own, other):
     heads, n, local = x.shape
-    nz, nx, _, rows, _ = own.shape
+    rows = own.shape[2]
     vm = pl.BlockSpec(memory_space=pltpu.VMEM)
-    anyspace = pl.BlockSpec(memory_space=pl.ANY)
     return pl.pallas_call(
         column_kernel,
         out_shape=jax.ShapeDtypeStruct((n, local), jnp.bfloat16),
-        in_specs=[pl.BlockSpec(memory_space=pltpu.SMEM), vm, vm, anyspace, anyspace],
+        in_specs=[pl.BlockSpec(memory_space=pltpu.SMEM), vm, vm, vm, vm],
         out_specs=vm,
         scratch_shapes=[
-            pltpu.VMEM((3, nz, nx, 2, rows, local), jnp.bfloat16),
+            pltpu.VMEM((3, 16, 2, 2, rows, local), jnp.bfloat16),
             pltpu.VMEM((n, heads * local), jnp.bfloat16),
-            pltpu.SemaphoreType.DMA((2, 2, 3)),
         ],
         compiler_params=pltpu.CompilerParams(vmem_limit_bytes=40 * 1024 * 1024),
         cost_estimate=pl.CostEstimate(
@@ -117,29 +157,32 @@
     )(where, x, gain, own, other)
 
 
+def shift(x, d):
+    return lax.ppermute(x, "z", [((i + d) % 16, i) for i in range(16)])
+
+
 def on_device(stream_in, row_query, row_key, row_value, out_weight, norm_gain, qkv_weight):
     _, steps, local = row_query.shape
     heads = norm_gain.shape[0] // local
     seq = 64
     here = steps // seq
 
-    w = jnp.transpose(qkv_weight, (1, 0, 2))
-    w2 = lax.ppermute(w, "xh", [(0, 1), (1, 0)])
-
+    w = jnp.transpose(qkv_weight, (1, 0, 2))[None]
+    fours = [shift(w, d) for d in FOUR[1:]]
     partial = row_part(row_query[0], row_key[0], row_value[0], out_weight, heads)
-
-    pair = jnp.stack([w, w2])
-    own = lax.all_gather(pair, "z", axis=0)
-
     parts = lax.all_to_all(partial, HD, 0, 0, tiled=True)
+    mine = pack(w, *fours)
+    theirs = lax.ppermute(mine, "xh", [(0, 1), (1, 0)])
     stream = stream_in[0].astype(jnp.float32) + jnp.sum(parts.astype(jnp.float32), axis=0)
     stream_out = stream.astype(jnp.bfloat16)
     columns = lax.all_to_all(stream_out.reshape(seq, here, local), SEQ, 0, 0, tiled=True)
+    both = pack(mine, theirs, event=(stream_out,))
+    up1, down1, up2, down2 = shift(both, 1), shift(both, -1), shift(mine, 2), shift(theirs, -2)
     columns = columns.reshape(seq * here, local)
     x = lax.all_to_all(jnp.broadcast_to(columns[None], (heads,) + columns.shape), HD, 0, 0, tiled=True)
-    own, x = lax.optimization_barrier((own, x))
+    own = pack(both, up1, down1, up2, down2, event=(columns,))
     other = lax.ppermute(own, "c", [(0, 1), (1, 0)])
-    where = jnp.stack([lax.axis_index("xh"), lax.axis_index("c")]).astype(jnp.int32)
+    where = jnp.stack([lax.axis_index("z"), lax.axis_index("xh"), lax.axis_index("c")]).astype(jnp.int32)
     mixed = column_part(where, x, norm_gain.reshape(1, -1), own, other)
     back = lax.all_to_all(mixed.reshape(seq, here, local), SEQ, 0, 0, tiled=True)
     return (stream_out[None], back.reshape(1, steps, local))

time: 145 us -> 144 us (level)
  blocking collectives: 62 us -> 0 us
  starting transfers between devices: 19.9 us -> 80.2 us
  waiting for transfers between devices: 33.1 us -> 50.9 us
  between operations: 14.1 us -> 0.86 us
  local copies, waits for them, and re-layouts: 6.97 us -> 2.64 us
  Pallas kernels: 5.49 us -> 7.24 us
    all_to_all x2 -> x0, blocking collectives: 62 us -> none  [the longest x1 44 us: on_device(): lax.all_to_all(stream_out.reshape(seq, here, local), SEQ, 0, 0, tiled=True)]
    ppermute x1 -> x8, starting transfers between devices: 5.48 us -> 41.9 us  [the longest x7 37.5 us: shift(): return lax.ppermute(x, 'z', [((i + d) % 16, i) for i in range(16)])]
    all_to_all x0 -> x2, waiting for transfers between devices: none -> 21.1 us  [the longest x1 15.5 us: on_device(): lax.all_to_all(jnp.broadcast_to(columns[None], (heads,) + columns.shape),...]
    all_to_all x0 -> x2, starting transfers between devices: none -> 15.3 us  [the longest x1 9.73 us: on_device(): lax.all_to_all(stream_out.reshape(seq, here, local), SEQ, 0, 0, tiled=True)]
    all_to_all x1, waiting for transfers between devices: 10.4 us -> 0.01 us  [on_device(): parts = lax.all_to_all(partial, HD, 0, 0, tiled=True)]
    ppermute x1 -> x8, waiting for transfers between devices: 1.67 us -> 11.9 us  [the longest x7 11.9 us: shift(): return lax.ppermute(x, 'z', [((i + d) % 16, i) for i in range(16)])]
    all_to_all x1, starting transfers between devices: 5.99 us -> 14.1 us  [on_device(): lax.all_to_all(mixed.reshape(seq, here, local), SEQ, 0, 0, tiled=True)]
    unnamed x14 -> x8, local copies, waits for them, and re-layouts: 5.35 us -> 0.02 us
  transfers between devices with their start and end apart: 5 -> 13, of which waited for: 4 -> 7; matrix products, arithmetic and copies ran while one was open for 1% -> 2% of each run, Pallas kernels for 2% -> 0%
where the time goes in v2:
time: 144 us; the launch traced here: 143 us
  starting transfers between devices  80.2 us (56%)
  waiting for transfers between devices  50.9 us (35%)
  Pallas kernels  7.24 us (5%)
  local copies, waits for them, and re-layouts  2.64 us (2%)
  other arithmetic  1.66 us (1%)
    ppermute x7, starting transfers between devices, shift(): return lax.ppermute(x, 'z', [((i + d) % 16, i) for i in range(16)])  37.5 us
    all_to_all x1, waiting for transfers between devices, on_device(): lax.all_to_all(mixed.reshape(seq, here, local), SEQ, 0, 0, tiled=True)  17.9 us
    all_to_all x1, waiting for transfers between devices, on_device(): lax.all_to_all(jnp.broadcast_to(columns[None], (heads,) + columns.shape),...  15.5 us
    all_to_all x1, starting transfers between devices, on_device(): lax.all_to_all(mixed.reshape(seq, here, local), SEQ, 0, 0, tiled=True)  14.1 us
    ppermute x7, waiting for transfers between devices, shift(): return lax.ppermute(x, 'z', [((i + d) % 16, i) for i in range(16)])  11.9 us
    all_to_all x1, starting transfers between devices, on_device(): lax.all_to_all(stream_out.reshape(seq, here, local), SEQ, 0, 0, tiled=True)  9.73 us
    all_to_all x1, starting transfers between devices, on_device(): parts = lax.all_to_all(partial, HD, 0, 0, tiled=True)  6.09 us
    all_to_all x1, waiting for transfers between devices, on_device(): lax.all_to_all(stream_out.reshape(seq, here, local), SEQ, 0, 0, tiled=True)  5.61 us
  transfers between devices with their start and end apart: 13, of which 7 were waited for; matrix products, arithmetic and copies ran while one was open for 2% of the time, Pallas kernels for 0%

profile of v2, /device:TPU:1, one launch (start us, length us, event | category | flops | bytes accessed | tf_op | source)
XLA Modules:
  0.0 143.5 jit_solution(857984777929353654)
XLA Ops:
  0.6 3.4 %row_attention.1 = bf16[8,256,256]{2,1,0:T(8,128)(2,1)} custom-call(bf16[256,256]{1,0:T(8,128)(2,1)} %bitcast.23, bf16[256,256]{1,0:T(8,128)(2,1)} %bitcast.24, bf16[256,256]{1,0:T(8,128)(2,1)} %bitcast.25, bf16[256,2048]{1,0:T(8,128)(2,1)} %w_hbm.1), custom_call_target="tpu_custom_call" | custom-call | flops 335544320 | bytes 3145728 | tf_op jit(solution)/shard_map/row_attention/pallas_call | solution.py:54
  4.1 0.0 copy-start
  4.1 0.0 copy-start.2
  4.1 6.1 %all-to-all-start = ((bf16[8,256,256]{2,1,0:T(8,128)(2,1)}), bf16[8,256,256]{2,1,0:T(8,128)(2,1)S(1)}, u32[]{:S(2)}, u32[]{:S(2)}) async-start(bf16[8,256,256]{2,1,0:T(8,128)(2,1)} %row_attention.1), calls=%async_computation | async-start | bytes 2097152 | tf_op jit(solution)/shard_map/all_to_all | solution.py:173
  10.2 0.0 copy-done
  10.2 15.4 %collective-permute-start.2 = (bf16[1,3,32,256]{3,2,1,0:T(8,128)(2,1)S(1)}, bf16[1,3,32,256]{3,2,1,0:T(8,128)(2,1)S(1)}, u32[]{:S(2)}, u32[]{:S(2)}) collective-permute-start(bf16[1,3,32,256]{3,2,1,0:T(8,128)(2,1)S(1)} %bitcast.18), channel_id=1, source_target_pairs={{256,0},{288,32},{320,64},{352,96},{384,128},{416,160},{448,192},{... | collective-permute-start | bytes 147464 | tf_op jit(solution)/shard_map/ppermute | solution.py:161
  25.6 4.0 %collective-permute-start.1 = (bf16[1,3,32,256]{3,2,1,0:T(8,128)(2,1)S(1)}, bf16[1,3,32,256]{3,2,1,0:T(8,128)(2,1)S(1)}, u32[]{:S(2)}, u32[]{:S(2)}) collective-permute-start(bf16[1,3,32,256]{3,2,1,0:T(8,128)(2,1)S(1)} %bitcast.19), channel_id=1, source_target_pairs={{384,0},{416,32},{448,64},{480,96},{0,128},{32,160},{64,192},{96,2... | collective-permute-start | bytes 147464 | tf_op jit(solution)/shard_map/ppermute | solution.py:161
  29.7 5.2 %collective-permute-start = (bf16[1,3,32,256]{3,2,1,0:T(8,128)(2,1)S(1)}, bf16[1,3,32,256]{3,2,1,0:T(8,128)(2,1)S(1)}, u32[]{:S(2)}, u32[]{:S(2)}) collective-permute-start(bf16[1,3,32,256]{3,2,1,0:T(8,128)(2,1)S(1)} %bitcast.20), channel_id=1, source_target_pairs={{128,0},{160,32},{192,64},{224,96},{256,128},{288,160},{320,192},{... | collective-permute-start | bytes 147464 | tf_op jit(solution)/shard_map/ppermute | solution.py:161
  34.8 0.0 copy-done.2
  34.9 0.1 reshape.26
  34.9 0.0 collective-permute-done.2.refs_3_
  34.9 0.5 collective-permute-done.1.refs_2_
  35.5 3.2 %collective-permute-done.refs_1_ = bf16[1,3,32,256]{3,2,1,0:T(8,128)(2,1)S(1)} collective-permute-done((bf16[1,3,32,256]{3,2,1,0:T(8,128)(2,1)S(1)}, bf16[1,3,32,256]{3,2,1,0:T(8,128)(2,1)S(1)}, u32[]{:S(2)}, u32[]{:S(2)}) %collective-permute-start) | collective-permute-done | bytes 49184 | tf_op jit(solution)/shard_map/ppermute | solution.py:161
  38.7 4.4 %collective-permute-start.3 = (bf16[4,3,32,256]{3,2,1,0:T(8,128)(2,1)S(1)}, bf16[4,3,32,256]{3,2,1,0:T(8,128)(2,1)S(1)}, u32[]{:S(2)}, u32[]{:S(2)}) collective-permute-start(bf16[4,3,32,256]{3,2,1,0:T(8,128)(2,1)S(1)} %pack.3.refs_0_), channel_id=1, source_target_pairs={{0,16},{16,0},{1,17},{17,1},{2,18},{18,2},{3,19},{19,3},{4,20},{20... | collective-permute-start | bytes 589832 | tf_op jit(solution)/shard_map/ppermute | solution.py:175
  43.0 0.0 all-to-all-done
  43.0 0.1 convert_reduce_fusion
  43.2 0.1 reduce_sum.15
  43.3 0.7 add_convert_fusion
  44.0 9.7 %all-to-all-start.1 = ((bf16[64,4,256]{2,1,0:T(4,128)(2,1)}), bf16[64,4,256]{2,1,0:T(4,128)(2,1)S(1)}, u32[]{:S(2)}, u32[]{:S(2)}) async-start(bf16[64,4,256]{2,1,0:T(4,128)(2,1)} %add_convert_fusion), calls=%async_computation.1 | async-start | bytes 262144 | tf_op jit(solution)/shard_map/all_to_all | solution.py:178
  53.8 0.0 collective-permute-done.3.refs_1_
  53.8 3.3 %collective-permute-start.5 = (bf16[8,3,32,256]{3,2,1,0:T(8,128)(2,1)S(1)}, bf16[8,3,32,256]{3,2,1,0:T(8,128)(2,1)S(1)}, u32[]{:S(2)}, u32[]{:S(2)}) collective-permute-start(bf16[8,3,32,256]{3,2,1,0:T(8,128)(2,1)S(1)} %pack.4.refs_0_), channel_id=1, source_target_pairs={{480,0},{0,32},{32,64},{64,96},{96,128},{128,160},{160,192},{192,2... | collective-permute-start | bytes 1179656 | tf_op jit(solution)/shard_map/ppermute | solution.py:161
  57.1 3.4 %collective-permute-start.4 = (bf16[8,3,32,256]{3,2,1,0:T(8,128)(2,1)S(1)}, bf16[8,3,32,256]{3,2,1,0:T(8,128)(2,1)S(1)}, u32[]{:S(2)}, u32[]{:S(2)}) collective-permute-start(bf16[8,3,32,256]{3,2,1,0:T(8,128)(2,1)S(1)} %pack.4.refs_0_), channel_id=1, source_target_pairs={{32,0},{64,32},{96,64},{128,96},{160,128},{192,160},{224,192},{256... | collective-permute-start | bytes 1179656 | tf_op jit(solution)/shard_map/ppermute | solution.py:161
  60.5 4.2 %collective-permute-start.6 = (bf16[4,3,32,256]{3,2,1,0:T(8,128)(2,1)S(1)}, bf16[4,3,32,256]{3,2,1,0:T(8,128)(2,1)S(1)}, u32[]{:S(2)}, u32[]{:S(2)}) collective-permute-start(bf16[4,3,32,256]{3,2,1,0:T(8,128)(2,1)S(1)} %pack.3.refs_0_), channel_id=1, source_target_pairs={{64,0},{96,32},{128,64},{160,96},{192,128},{224,160},{256,192},{28... | collective-permute-start | bytes 589832 | tf_op jit(solution)/shard_map/ppermute | solution.py:161
  64.8 1.9 %collective-permute-start.7 = (bf16[4,3,32,256]{3,2,1,0:T(8,128)(2,1)S(1)}, bf16[4,3,32,256]{3,2,1,0:T(8,128)(2,1)S(1)}, u32[]{:S(2)}, u32[]{:S(2)}) collective-permute-start(bf16[4,3,32,256]{3,2,1,0:T(8,128)(2,1)S(1)} %collective-permute-done.3.refs_1_), channel_id=1, source_target_pairs={{448,0},{480,32},{0,64},{32,96},{64,128},{96,160},{128,192},{160,2... | collective-permute-start | bytes 589832 | tf_op jit(solution)/shard_map/ppermute | solution.py:161
  66.7 5.6 %all-to-all-done.1 = bf16[64,4,256]{2,1,0:T(4,128)(2,1)S(1)} async-done(((bf16[64,4,256]{2,1,0:T(4,128)(2,1)}), bf16[64,4,256]{2,1,0:T(4,128)(2,1)S(1)}, u32[]{:S(2)}, u32[]{:S(2)}) %all-to-all-start.1) | async-done | bytes 131104 | tf_op jit(solution)/shard_map/all_to_all | solution.py:178
  72.4 7.9 %collective-permute-done.6.refs_3_ = bf16[4,3,32,256]{3,2,1,0:T(8,128)(2,1)S(1)} collective-permute-done((bf16[4,3,32,256]{3,2,1,0:T(8,128)(2,1)S(1)}, bf16[4,3,32,256]{3,2,1,0:T(8,128)(2,1)S(1)}, u32[]{:S(2)}, u32[]{:S(2)}) %collective-permute-start.6) | collective-permute-done | bytes 196640 | tf_op jit(solution)/shard_map/ppermute | solution.py:161
  80.3 0.2 collective-permute-done.7.refs_4_
  80.6 0.0 collective-permute-done.5.refs_2_
  80.6 0.0 collective-permute-done.4.refs_1_
  80.6 0.1 pack.5.own_ref
  80.7 0.0 copy-start.1
  80.7 2.8 %collective-permute-start.8 = (bf16[32,3,32,256]{3,2,1,0:T(8,128)(2,1)S(1)}, bf16[32,3,32,256]{3,2,1,0:T(8,128)(2,1)}, u32[]{:S(2)}, u32[]{:S(2)}) collective-permute-start(bf16[32,3,32,256]{3,2,1,0:T(8,128)(2,1)S(1)} %pack.5.own_ref), channel_id=1, source_target_pairs={{0,8},{8,0},{1,9},{9,1},{2,10},{10,2},{3,11},{11,3},{4,12},{12,4},... | collective-permute-start | bytes 4718600 | tf_op jit(solution)/shard_map/ppermute | solution.py:184
  83.5 1.1 broadcast_in_dim.12
  84.5 5.6 %all-to-all-start.2 = ((bf16[8,256,256]{2,1,0:T(8,128)(2,1)}), bf16[8,256,256]{2,1,0:T(8,128)(2,1)S(1)}, u32[]{:S(2)}, u32[]{:S(2)}) async-start(bf16[8,256,256]{2,1,0:T(8,128)(2,1)} %broadcast_in_dim.12), calls=%async_computation.2 | async-start | bytes 2097152 | tf_op jit(solution)/shard_map/all_to_all | solution.py:182
  90.1 0.1 pad_add_fusion.where_ref
  90.2 15.5 %all-to-all-done.2.x_ref = bf16[8,256,256]{2,1,0:T(8,128)(2,1)S(1)} async-done(((bf16[8,256,256]{2,1,0:T(8,128)(2,1)}), bf16[8,256,256]{2,1,0:T(8,128)(2,1)S(1)}, u32[]{:S(2)}, u32[]{:S(2)}) %all-to-all-start.2) | async-done | bytes 1048608 | tf_op jit(solution)/shard_map/all_to_all | solution.py:182
  105.7 0.0 collective-permute-done.8.other_ref
  105.7 0.0 copy-done.1
  105.7 0.0 copy-start.3
  105.7 3.7 %column_attention.1 = bf16[256,256]{1,0:T(8,128)(2,1)S(1)} custom-call(s32[3]{0:T(128)S(1)} %pad_add_fusion.where_ref, bf16[8,256,256]{2,1,0:T(8,128)(2,1)S(1)} %all-to-all-done.2.x_ref, f32[1,2048]{1,0:T(1,128)S(1)} %bitcast.22, bf16[32,3,32,256]{3,2,1,0:T(8,128)(2,1)S(1)} %pack.5.own_ref, bf16[32,3,32,256]{3,2,1,0:T(8,128)(2,1)} %collective-permute-done.8.other_ref), custom_call_target="tpu_custom_call" | custom-call | flops 805306368 | bytes 5242880 | tf_op jit(solution)/shard_map/column_attention/pallas_call | solution.py:143
  109.4 0.7 reshape.24
  110.1 14.1 %all-to-all-start.3 = ((bf16[64,4,256]{2,1,0:T(4,128)(2,1)}), bf16[64,4,256]{2,1,0:T(4,128)(2,1)S(1)}, u32[]{:S(2)}, u32[]{:S(2)}) async-start(bf16[64,4,256]{2,1,0:T(4,128)(2,1)} %reshape.24), calls=%async_computation.3 | async-start | bytes 262144 | tf_op jit(solution)/shard_map/all_to_all | solution.py:187
  124.2 0.0 copy-done.3
  124.2 0.7 fusion.1
  124.9 17.9 %all-to-all-done.3 = bf16[64,4,256]{2,1,0:T(4,128)(2,1)S(1)} async-done(((bf16[64,4,256]{2,1,0:T(4,128)(2,1)}), bf16[64,4,256]{2,1,0:T(4,128)(2,1)S(1)}, u32[]{:S(2)}, u32[]{:S(2)}) %all-to-all-start.3) | async-done | bytes 131104 | tf_op jit(solution)/shard_map/all_to_all | solution.py:187
  142.8 0.7 reshape.25
  (4 shorter events, 0.1 us)
Async XLA Ops:
  4.1 6.1 %copy-start = (bf16[32,3,256]{2,0,1:T(8,128)(2,1)S(1)}, bf16[32,3,256]{2,0,1:T(8,128)(2,1)}, u32[]{:S(2)}) copy-start(bf16[32,3,256]{2,0,1:T(8,128)(2,1)} %param.13) | copy-start | bytes 147460
  4.1 30.8 %copy-start.2 = (bf16[1,256,256]{2,1,0:T(8,128)(2,1)S(1)}, bf16[1,256,256]{2,1,0:T(8,128)(2,1)}, u32[]{:S(2)}) copy-start(bf16[1,256,256]{2,1,0:T(8,128)(2,1)} %param.7) | copy-start | bytes 393220
  4.1 38.9 %all-to-all-start = ((bf16[8,256,256]{2,1,0:T(8,128)(2,1)}), bf16[8,256,256]{2,1,0:T(8,128)(2,1)S(1)}, u32[]{:S(2)}, u32[]{:S(2)}) async-start(bf16[8,256,256]{2,1,0:T(8,128)(2,1)} %row_attention.1), calls=%async_computation | async-start | bytes 2097152 | tf_op jit(solution)/shard_map/all_to_all | solution.py:173
  10.2 24.7 %collective-permute-start.2 = (bf16[1,3,32,256]{3,2,1,0:T(8,128)(2,1)S(1)}, bf16[1,3,32,256]{3,2,1,0:T(8,128)(2,1)S(1)}, u32[]{:S(2)}, u32[]{:S(2)}) collective-permute-start(bf16[1,3,32,256]{3,2,1,0:T(8,128)(2,1)S(1)} %bitcast.18), channel_id=1, source_target_pairs={{256,0},{288,32},{320,64},{352,96},{384,128},{416,160},{448,192},{... | collective-permute-start | bytes 147464 | tf_op jit(solution)/shard_map/ppermute | solution.py:161
  25.6 9.8 %collective-permute-start.1 = (bf16[1,3,32,256]{3,2,1,0:T(8,128)(2,1)S(1)}, bf16[1,3,32,256]{3,2,1,0:T(8,128)(2,1)S(1)}, u32[]{:S(2)}, u32[]{:S(2)}) collective-permute-start(bf16[1,3,32,256]{3,2,1,0:T(8,128)(2,1)S(1)} %bitcast.19), channel_id=1, source_target_pairs={{384,0},{416,32},{448,64},{480,96},{0,128},{32,160},{64,192},{96,2... | collective-permute-start | bytes 147464 | tf_op jit(solution)/shard_map/ppermute | solution.py:161
  29.7 9.0 %collective-permute-start = (bf16[1,3,32,256]{3,2,1,0:T(8,128)(2,1)S(1)}, bf16[1,3,32,256]{3,2,1,0:T(8,128)(2,1)S(1)}, u32[]{:S(2)}, u32[]{:S(2)}) collective-permute-start(bf16[1,3,32,256]{3,2,1,0:T(8,128)(2,1)S(1)} %bitcast.20), channel_id=1, source_target_pairs={{128,0},{160,32},{192,64},{224,96},{256,128},{288,160},{320,192},{... | collective-permute-start | bytes 147464 | tf_op jit(solution)/shard_map/ppermute | solution.py:161
  38.7 15.1 %collective-permute-start.3 = (bf16[4,3,32,256]{3,2,1,0:T(8,128)(2,1)S(1)}, bf16[4,3,32,256]{3,2,1,0:T(8,128)(2,1)S(1)}, u32[]{:S(2)}, u32[]{:S(2)}) collective-permute-start(bf16[4,3,32,256]{3,2,1,0:T(8,128)(2,1)S(1)} %pack.3.refs_0_), channel_id=1, source_target_pairs={{0,16},{16,0},{1,17},{17,1},{2,18},{18,2},{3,19},{19,3},{4,20},{20... | collective-permute-start | bytes 589832 | tf_op jit(solution)/shard_map/ppermute | solution.py:175
  44.0 28.4 %all-to-all-start.1 = ((bf16[64,4,256]{2,1,0:T(4,128)(2,1)}), bf16[64,4,256]{2,1,0:T(4,128)(2,1)S(1)}, u32[]{:S(2)}, u32[]{:S(2)}) async-start(bf16[64,4,256]{2,1,0:T(4,128)(2,1)} %add_convert_fusion), calls=%async_computation.1 | async-start | bytes 262144 | tf_op jit(solution)/shard_map/all_to_all | solution.py:178
  53.8 26.7 %collective-permute-start.5 = (bf16[8,3,32,256]{3,2,1,0:T(8,128)(2,1)S(1)}, bf16[8,3,32,256]{3,2,1,0:T(8,128)(2,1)S(1)}, u32[]{:S(2)}, u32[]{:S(2)}) collective-permute-start(bf16[8,3,32,256]{3,2,1,0:T(8,128)(2,1)S(1)} %pack.4.refs_0_), channel_id=1, source_target_pairs={{480,0},{0,32},{32,64},{64,96},{96,128},{128,160},{160,192},{192,2... | collective-permute-start | bytes 1179656 | tf_op jit(solution)/shard_map/ppermute | solution.py:161
  57.1 23.4 %collective-permute-start.4 = (bf16[8,3,32,256]{3,2,1,0:T(8,128)(2,1)S(1)}, bf16[8,3,32,256]{3,2,1,0:T(8,128)(2,1)S(1)}, u32[]{:S(2)}, u32[]{:S(2)}) collective-permute-start(bf16[8,3,32,256]{3,2,1,0:T(8,128)(2,1)S(1)} %pack.4.refs_0_), channel_id=1, source_target_pairs={{32,0},{64,32},{96,64},{128,96},{160,128},{192,160},{224,192},{256... | collective-permute-start | bytes 1179656 | tf_op jit(solution)/shard_map/ppermute | solution.py:161
  60.5 19.8 %collective-permute-start.6 = (bf16[4,3,32,256]{3,2,1,0:T(8,128)(2,1)S(1)}, bf16[4,3,32,256]{3,2,1,0:T(8,128)(2,1)S(1)}, u32[]{:S(2)}, u32[]{:S(2)}) collective-permute-start(bf16[4,3,32,256]{3,2,1,0:T(8,128)(2,1)S(1)} %pack.3.refs_0_), channel_id=1, source_target_pairs={{64,0},{96,32},{128,64},{160,96},{192,128},{224,160},{256,192},{28... | collective-permute-start | bytes 589832 | tf_op jit(solution)/shard_map/ppermute | solution.py:161
  64.8 15.8 %collective-permute-start.7 = (bf16[4,3,32,256]{3,2,1,0:T(8,128)(2,1)S(1)}, bf16[4,3,32,256]{3,2,1,0:T(8,128)(2,1)S(1)}, u32[]{:S(2)}, u32[]{:S(2)}) collective-permute-start(bf16[4,3,32,256]{3,2,1,0:T(8,128)(2,1)S(1)} %collective-permute-done.3.refs_1_), channel_id=1, source_target_pairs={{448,0},{480,32},{0,64},{32,96},{64,128},{96,160},{128,192},{160,2... | collective-permute-start | bytes 589832 | tf_op jit(solution)/shard_map/ppermute | solution.py:161
  80.7 25.0 %copy-start.1 = (f32[2048]{0:T(1024)S(1)}, f32[2048]{0:T(1024)}, u32[]{:S(2)}) copy-start(f32[2048]{0:T(1024)} %param.12) | copy-start | bytes 24580
  80.7 25.0 %collective-permute-start.8 = (bf16[32,3,32,256]{3,2,1,0:T(8,128)(2,1)S(1)}, bf16[32,3,32,256]{3,2,1,0:T(8,128)(2,1)}, u32[]{:S(2)}, u32[]{:S(2)}) collective-permute-start(bf16[32,3,32,256]{3,2,1,0:T(8,128)(2,1)S(1)} %pack.5.own_ref), channel_id=1, source_target_pairs={{0,8},{8,0},{1,9},{9,1},{2,10},{10,2},{3,11},{11,3},{4,12},{12,4},... | collective-permute-start | bytes 4718600 | tf_op jit(solution)/shard_map/ppermute | solution.py:184
  84.5 21.2 %all-to-all-start.2 = ((bf16[8,256,256]{2,1,0:T(8,128)(2,1)}), bf16[8,256,256]{2,1,0:T(8,128)(2,1)S(1)}, u32[]{:S(2)}, u32[]{:S(2)}) async-start(bf16[8,256,256]{2,1,0:T(8,128)(2,1)} %broadcast_in_dim.12), calls=%async_computation.2 | async-start | bytes 2097152 | tf_op jit(solution)/shard_map/all_to_all | solution.py:182
  105.7 18.5 %copy-start.3 = (bf16[1,256,256]{2,1,0:T(8,128)(2,1)S(1)}, bf16[1,256,256]{2,1,0:T(8,128)(2,1)}, u32[]{:S(2)}) copy-start(bf16[1,256,256]{2,1,0:T(8,128)(2,1)} %param.7) | copy-start | bytes 393220
  110.1 32.7 %all-to-all-start.3 = ((bf16[64,4,256]{2,1,0:T(4,128)(2,1)}), bf16[64,4,256]{2,1,0:T(4,128)(2,1)S(1)}, u32[]{:S(2)}, u32[]{:S(2)}) async-start(bf16[64,4,256]{2,1,0:T(4,128)(2,1)} %reshape.24), calls=%async_computation.3 | async-start | bytes 262144 | tf_op jit(solution)/shard_map/all_to_all | solution.py:187

commit v3 on v2

--- a/solution.py
+++ b/solution.py
@@ -84,7 +84,7 @@
     return pl.pallas_call(
         functools.partial(pack_kernel, len(pieces)),
         out_shape=jax.ShapeDtypeStruct(shape, pieces[0].dtype),
-        in_specs=[vm] * len(pieces) + [pl.BlockSpec(memory_space=pl.ANY)] * len(event),
+        in_specs=[vm] * (len(pieces) + len(event)),
         out_specs=vm,
         compiler_params=pltpu.CompilerParams(vmem_limit_bytes=16 * 1024 * 1024),
         cost_estimate=pl.CostEstimate(flops=0, bytes_accessed=size, transcendentals=0),
@@ -93,13 +93,31 @@
 
 
 FOUR = (0, 4, -4, 8)
+EIGHT = [(f, o) for f in FOUR for o in (0, 1)]
 SLOTS = (
-    [(f, o) for o in (0, 1) for f in FOUR]
-    + [(1 + f, o) for o in (0, 1) for f in FOUR]
-    + [(-1 + f, o) for o in (0, 1) for f in FOUR]
-    + [(2 + f, 0) for f in FOUR]
-    + [(-2 + f, 1) for f in FOUR]
+    EIGHT
+    + [(1 + f, o) for f, o in EIGHT]
+    + [(-1 + f, o) for f, o in EIGHT]
+    + [(2 + f, o) for f, o in EIGHT[:4]]
+    + [(-2 + f, o) for f, o in EIGHT[:2] + EIGHT[4:6]]
 )
+
+
+def touch_kernel(x_ref, event_ref, out_ref):
+    pass
+
+
+def touch(x, event):
+    anyspace = pl.BlockSpec(memory_space=pl.ANY)
+    return pl.pallas_call(
+        touch_kernel,
+        out_shape=jax.ShapeDtypeStruct(x.shape, x.dtype),
+        in_specs=[anyspace, anyspace],
+        out_specs=anyspace,
+        input_output_aliases={0: 0},
+        compiler_params=pltpu.CompilerParams(vmem_limit_bytes=VMEM_BYTES),
+        name="touch",
+    )(x, event)
 
 
 def column_kernel(where_ref, x_ref, gain_ref, own_ref, other_ref, out_ref, w_ref, normed_ref):
@@ -168,19 +186,20 @@
     here = steps // seq
 
     w = jnp.transpose(qkv_weight, (1, 0, 2))[None]
-    fours = [shift(w, d) for d in FOUR[1:]]
+    theirs = lax.ppermute(w, "xh", [(0, 1), (1, 0)])
     partial = row_part(row_query[0], row_key[0], row_value[0], out_weight, heads)
-    parts = lax.all_to_all(partial, HD, 0, 0, tiled=True)
-    mine = pack(w, *fours)
-    theirs = lax.ppermute(mine, "xh", [(0, 1), (1, 0)])
+    pair = pack(w, theirs)
+    parts = lax.all_to_all(touch(partial, pair[1, 0, :16, :128]), HD, 0, 0, tiled=True)
+    up4, down4, up8 = shift(pair, 4), shift(pair, -4), shift(pair, 8)
     stream = stream_in[0].astype(jnp.float32) + jnp.sum(parts.astype(jnp.float32), axis=0)
     stream_out = stream.astype(jnp.bfloat16)
     columns = lax.all_to_all(stream_out.reshape(seq, here, local), SEQ, 0, 0, tiled=True)
-    both = pack(mine, theirs, event=(stream_out,))
-    up1, down1, up2, down2 = shift(both, 1), shift(both, -1), shift(mine, 2), shift(theirs, -2)
+    eight = pack(pair, up4, down4, up8, event=(stream_out,))
+    first, second = pack(pair, up4, event=(stream_out,)), pack(pair, down4, event=(stream_out,))
+    up1, down1, up2, down2 = shift(eight, 1), shift(eight, -1), shift(first, 2), shift(second, -2)
     columns = columns.reshape(seq * here, local)
     x = lax.all_to_all(jnp.broadcast_to(columns[None], (heads,) + columns.shape), HD, 0, 0, tiled=True)
-    own = pack(both, up1, down1, up2, down2, event=(columns,))
+    own = pack(eight, up1, down1, up2, down2, event=(columns,))
     other = lax.ppermute(own, "c", [(0, 1), (1, 0)])
     where = jnp.stack([lax.axis_index("z"), lax.axis_index("xh"), lax.axis_index("c")]).astype(jnp.int32)
     mixed = column_part(where, x, norm_gain.reshape(1, -1), own, other)

time: 144 us -> 140 us (0.972)
  waiting for transfers between devices: 50.9 us -> 47.1 us
    ppermute x7, waiting for transfers between devices: 11.9 us -> 8.12 us  [shift(): return lax.ppermute(x, 'z', [((i + d) % 16, i) for i in range(16)])]
    all_to_all x1, starting transfers between devices: 6.09 us -> 4.35 us  [on_device(): lax.all_to_all(touch(partial, pair[1, 0, :16, :128]), HD, 0, 0, tiled=True)]
  transfers between devices with their start and end apart: 13 -> 13, of which waited for: 7 -> 5; matrix products, arithmetic and copies ran while one was open for 2% -> 2% of each run, Pallas kernels for 0% -> 3%
where the time goes in v3:
time: 140 us; the launch traced here: 139 us
  starting transfers between devices  79.3 us (57%)
  waiting for transfers between devices  47.1 us (34%)
  Pallas kernels  7.26 us (5%)
  local copies, waits for them, and re-layouts  3.23 us (2%)
  other arithmetic  1.66 us (1%)
    ppermute x7, starting transfers between devices, shift(): return lax.ppermute(x, 'z', [((i + d) % 16, i) for i in range(16)])  37.5 us
    all_to_all x1, waiting for transfers between devices, on_device(): lax.all_to_all(mixed.reshape(seq, here, local), SEQ, 0, 0, tiled=True)  17.9 us
    all_to_all x1, waiting for transfers between devices, on_device(): lax.all_to_all(jnp.broadcast_to(columns[None], (heads,) + columns.shape),...  15.5 us
    all_to_all x1, starting transfers between devices, on_device(): lax.all_to_all(mixed.reshape(seq, here, local), SEQ, 0, 0, tiled=True)  14.1 us
    all_to_all x1, starting transfers between devices, on_device(): lax.all_to_all(stream_out.reshape(seq, here, local), SEQ, 0, 0, tiled=True)  10 us
    ppermute x7, waiting for transfers between devices, shift(): return lax.ppermute(x, 'z', [((i + d) % 16, i) for i in range(16)])  8.12 us
    ppermute x1, starting transfers between devices, on_device(): theirs = lax.ppermute(w, 'xh', [(0, 1), (1, 0)])  5.61 us
    all_to_all x1, waiting for transfers between devices, on_device(): lax.all_to_all(stream_out.reshape(seq, here, local), SEQ, 0, 0, tiled=True)  5.55 us
  transfers between devices with their start and end apart: 13, of which 5 were waited for; matrix products, arithmetic and copies ran while one was open for 2% of the time, Pallas kernels for 3%

profile of v3, /device:TPU:1, one launch (start us, length us, event | category | flops | bytes accessed | tf_op | source)
XLA Modules:
  0.0 139.4 jit_solution(883347204684256277)
XLA Ops:
  0.6 0.0 copy-start
  0.6 5.6 %collective-permute-start = (bf16[1,3,32,256]{3,2,1,0:T(8,128)(2,1)}, bf16[1,3,32,256]{3,2,1,0:T(8,128)(2,1)S(1)}, u32[]{:S(2)}, u32[]{:S(2)}) collective-permute-start(bf16[1,3,32,256]{3,2,1,0:T(8,128)(2,1)} %bitcast.20), channel_id=1, source_target_pairs={{0,16},{16,0},{1,17},{17,1},{2,18},{18,2},{3,19},{19,3},{4,20},{20... | collective-permute-start | bytes 147464 | tf_op jit(solution)/shard_map/ppermute | solution.py:189
  6.3 3.4 %row_attention.1.x_ref = bf16[8,256,256]{2,1,0:T(8,128)(2,1)} custom-call(bf16[256,256]{1,0:T(8,128)(2,1)} %bitcast.23, bf16[256,256]{1,0:T(8,128)(2,1)} %bitcast.24, bf16[256,256]{1,0:T(8,128)(2,1)} %bitcast.25, bf16[256,2048]{1,0:T(8,128)(2,1)} %w_hbm.1), custom_call_target="tpu_custom_call" | custom-call | flops 335544320 | bytes 3145728 | tf_op jit(solution)/shard_map/row_attention/pallas_call | solution.py:54
  9.7 0.0 collective-permute-done.refs_1_
  9.7 0.0 copy-done
  9.7 0.6 slice_bitcast_fusion.event_ref
  10.3 0.0 copy-start.2
  10.3 4.3 %all-to-all-start = ((bf16[8,256,256]{2,1,0:T(8,128)(2,1)}), bf16[8,256,256]{2,1,0:T(8,128)(2,1)S(1)}, u32[]{:S(2)}, u32[]{:S(2)}) async-start(bf16[8,256,256]{2,1,0:T(8,128)(2,1)} %touch.1), calls=%async_computation | async-start | bytes 2097152 | tf_op jit(solution)/shard_map/all_to_all | solution.py:192
  14.7 0.0 copy-done.2
  14.7 0.1 reshape.26
  14.8 15.4 %collective-permute-start.3 = (bf16[2,3,32,256]{3,2,1,0:T(8,128)(2,1)S(1)}, bf16[2,3,32,256]{3,2,1,0:T(8,128)(2,1)S(1)}, u32[]{:S(2)}, u32[]{:S(2)}) collective-permute-start(bf16[2,3,32,256]{3,2,1,0:T(8,128)(2,1)S(1)} %pack.5.refs_0_), channel_id=1, source_target_pairs={{256,0},{288,32},{320,64},{352,96},{384,128},{416,160},{448,192},{... | collective-permute-start | bytes 294920 | tf_op jit(solution)/shard_map/ppermute | solution.py:179
  30.2 4.0 %collective-permute-start.2 = (bf16[2,3,32,256]{3,2,1,0:T(8,128)(2,1)S(1)}, bf16[2,3,32,256]{3,2,1,0:T(8,128)(2,1)S(1)}, u32[]{:S(2)}, u32[]{:S(2)}) collective-permute-start(bf16[2,3,32,256]{3,2,1,0:T(8,128)(2,1)S(1)} %pack.5.refs_0_), channel_id=1, source_target_pairs={{384,0},{416,32},{448,64},{480,96},{0,128},{32,160},{64,192},{96,2... | collective-permute-start | bytes 294920 | tf_op jit(solution)/shard_map/ppermute | solution.py:179
  34.2 5.2 %collective-permute-start.1 = (bf16[2,3,32,256]{3,2,1,0:T(8,128)(2,1)S(1)}, bf16[2,3,32,256]{3,2,1,0:T(8,128)(2,1)S(1)}, u32[]{:S(2)}, u32[]{:S(2)}) collective-permute-start(bf16[2,3,32,256]{3,2,1,0:T(8,128)(2,1)S(1)} %pack.5.refs_0_), channel_id=1, source_target_pairs={{128,0},{160,32},{192,64},{224,96},{256,128},{288,160},{320,192},{... | collective-permute-start | bytes 294920 | tf_op jit(solution)/shard_map/ppermute | solution.py:179
  39.4 0.0 all-to-all-done
  39.4 0.1 convert_reduce_fusion
  39.6 0.1 reduce_sum.15
  39.7 0.7 add_convert_fusion
  40.4 10.0 %all-to-all-start.1 = ((bf16[64,4,256]{2,1,0:T(4,128)(2,1)}), bf16[64,4,256]{2,1,0:T(4,128)(2,1)S(1)}, u32[]{:S(2)}, u32[]{:S(2)}) async-start(bf16[64,4,256]{2,1,0:T(4,128)(2,1)} %add_convert_fusion), calls=%async_computation.1 | async-start | bytes 262144 | tf_op jit(solution)/shard_map/all_to_all | solution.py:196
  50.4 0.0 collective-permute-done.3.refs_3_
  50.5 0.0 collective-permute-done.2.refs_2_.refs_1_
  50.5 0.0 collective-permute-done.1.refs_1_
  50.5 3.3 %collective-permute-start.5 = (bf16[8,3,32,256]{3,2,1,0:T(8,128)(2,1)S(1)}, bf16[8,3,32,256]{3,2,1,0:T(8,128)(2,1)S(1)}, u32[]{:S(2)}, u32[]{:S(2)}) collective-permute-start(bf16[8,3,32,256]{3,2,1,0:T(8,128)(2,1)S(1)} %pack.6.refs_0_), channel_id=1, source_target_pairs={{480,0},{0,32},{32,64},{64,96},{96,128},{128,160},{160,192},{192,2... | collective-permute-start | bytes 1179656 | tf_op jit(solution)/shard_map/ppermute | solution.py:179
  53.8 3.4 %collective-permute-start.4 = (bf16[8,3,32,256]{3,2,1,0:T(8,128)(2,1)S(1)}, bf16[8,3,32,256]{3,2,1,0:T(8,128)(2,1)S(1)}, u32[]{:S(2)}, u32[]{:S(2)}) collective-permute-start(bf16[8,3,32,256]{3,2,1,0:T(8,128)(2,1)S(1)} %pack.6.refs_0_), channel_id=1, source_target_pairs={{32,0},{64,32},{96,64},{128,96},{160,128},{192,160},{224,192},{256... | collective-permute-start | bytes 1179656 | tf_op jit(solution)/shard_map/ppermute | solution.py:179
  57.3 4.2 %collective-permute-start.6 = (bf16[4,3,32,256]{3,2,1,0:T(8,128)(2,1)S(1)}, bf16[4,3,32,256]{3,2,1,0:T(8,128)(2,1)S(1)}, u32[]{:S(2)}, u32[]{:S(2)}) collective-permute-start(bf16[4,3,32,256]{3,2,1,0:T(8,128)(2,1)S(1)} %pack.7), channel_id=1, source_target_pairs={{64,0},{96,32},{128,64},{160,96},{192,128},{224,160},{256,192},{28... | collective-permute-start | bytes 589832 | tf_op jit(solution)/shard_map/ppermute | solution.py:179
  61.5 1.9 %collective-permute-start.7 = (bf16[4,3,32,256]{3,2,1,0:T(8,128)(2,1)S(1)}, bf16[4,3,32,256]{3,2,1,0:T(8,128)(2,1)S(1)}, u32[]{:S(2)}, u32[]{:S(2)}) collective-permute-start(bf16[4,3,32,256]{3,2,1,0:T(8,128)(2,1)S(1)} %pack.8), channel_id=1, source_target_pairs={{448,0},{480,32},{0,64},{32,96},{64,128},{96,160},{128,192},{160,2... | collective-permute-start | bytes 589832 | tf_op jit(solution)/shard_map/ppermute | solution.py:179
  63.5 5.6 %all-to-all-done.1 = bf16[64,4,256]{2,1,0:T(4,128)(2,1)S(1)} async-done(((bf16[64,4,256]{2,1,0:T(4,128)(2,1)}), bf16[64,4,256]{2,1,0:T(4,128)(2,1)S(1)}, u32[]{:S(2)}, u32[]{:S(2)}) %all-to-all-start.1) | async-done | bytes 131104 | tf_op jit(solution)/shard_map/all_to_all | solution.py:196
  69.1 7.9 %collective-permute-done.6.refs_3_ = bf16[4,3,32,256]{3,2,1,0:T(8,128)(2,1)S(1)} collective-permute-done((bf16[4,3,32,256]{3,2,1,0:T(8,128)(2,1)S(1)}, bf16[4,3,32,256]{3,2,1,0:T(8,128)(2,1)S(1)}, u32[]{:S(2)}, u32[]{:S(2)}) %collective-permute-start.6) | collective-permute-done | bytes 196640 | tf_op jit(solution)/shard_map/ppermute | solution.py:179
  77.0 0.2 collective-permute-done.7.refs_4_
  77.2 0.0 collective-permute-done.5.refs_2_
  77.2 0.0 collective-permute-done.4.refs_1_
  77.2 0.1 pack.9.own_ref
  77.3 0.0 copy-start.1
  77.3 2.8 %collective-permute-start.8 = (bf16[32,3,32,256]{3,2,1,0:T(8,128)(2,1)S(1)}, bf16[32,3,32,256]{3,2,1,0:T(8,128)(2,1)}, u32[]{:S(2)}, u32[]{:S(2)}) collective-permute-start(bf16[32,3,32,256]{3,2,1,0:T(8,128)(2,1)S(1)} %pack.9.own_ref), channel_id=1, source_target_pairs={{0,8},{8,0},{1,9},{9,1},{2,10},{10,2},{3,11},{11,3},{4,12},{12,4},... | collective-permute-start | bytes 4718600 | tf_op jit(solution)/shard_map/ppermute | solution.py:203
  80.1 1.1 broadcast_in_dim.13
  81.2 4.8 %all-to-all-start.2 = ((bf16[8,256,256]{2,1,0:T(8,128)(2,1)}), bf16[8,256,256]{2,1,0:T(8,128)(2,1)S(1)}, u32[]{:S(2)}, u32[]{:S(2)}) async-start(bf16[8,256,256]{2,1,0:T(8,128)(2,1)} %broadcast_in_dim.13), calls=%async_computation.2 | async-start | bytes 2097152 | tf_op jit(solution)/shard_map/all_to_all | solution.py:201
  86.0 0.1 pad_add_fusion.where_ref
  86.1 15.5 %all-to-all-done.2.x_ref = bf16[8,256,256]{2,1,0:T(8,128)(2,1)S(1)} async-done(((bf16[8,256,256]{2,1,0:T(8,128)(2,1)}), bf16[8,256,256]{2,1,0:T(8,128)(2,1)S(1)}, u32[]{:S(2)}, u32[]{:S(2)}) %all-to-all-start.2) | async-done | bytes 1048608 | tf_op jit(solution)/shard_map/all_to_all | solution.py:201
  101.6 0.0 collective-permute-done.8.other_ref
  101.6 0.0 copy-done.1
  101.6 0.0 copy-start.3
  101.6 3.7 %column_attention.1 = bf16[256,256]{1,0:T(8,128)(2,1)S(1)} custom-call(s32[3]{0:T(128)S(1)} %pad_add_fusion.where_ref, bf16[8,256,256]{2,1,0:T(8,128)(2,1)S(1)} %all-to-all-done.2.x_ref, f32[1,2048]{1,0:T(1,128)S(1)} %bitcast.22, bf16[32,3,32,256]{3,2,1,0:T(8,128)(2,1)S(1)} %pack.9.own_ref, bf16[32,3,32,256]{3,2,1,0:T(8,128)(2,1)} %collective-permute-done.8.other_ref), custom_call_target="tpu_custom_call" | custom-call | flops 805306368 | bytes 5242880 | tf_op jit(solution)/shard_map/column_attention/pallas_call | solution.py:161
  105.3 0.7 reshape.24
  106.0 14.1 %all-to-all-start.3 = ((bf16[64,4,256]{2,1,0:T(4,128)(2,1)}), bf16[64,4,256]{2,1,0:T(4,128)(2,1)S(1)}, u32[]{:S(2)}, u32[]{:S(2)}) async-start(bf16[64,4,256]{2,1,0:T(4,128)(2,1)} %reshape.24), calls=%async_computation.3 | async-start | bytes 262144 | tf_op jit(solution)/shard_map/all_to_all | solution.py:206
  120.1 0.0 copy-done.3
  120.1 0.7 fusion.1
  120.8 17.9 %all-to-all-done.3 = bf16[64,4,256]{2,1,0:T(4,128)(2,1)S(1)} async-done(((bf16[64,4,256]{2,1,0:T(4,128)(2,1)}), bf16[64,4,256]{2,1,0:T(4,128)(2,1)S(1)}, u32[]{:S(2)}, u32[]{:S(2)}) %all-to-all-start.3) | async-done | bytes 131104 | tf_op jit(solution)/shard_map/all_to_all | solution.py:206
  138.7 0.7 reshape.25
  (7 shorter events, 0.1 us)
Async XLA Ops:
  0.6 9.1 %copy-start = (bf16[32,3,256]{2,0,1:T(8,128)(2,1)S(1)}, bf16[32,3,256]{2,0,1:T(8,128)(2,1)}, u32[]{:S(2)}) copy-start(bf16[32,3,256]{2,0,1:T(8,128)(2,1)} %param.13) | copy-start | bytes 147460
  0.6 9.1 %collective-permute-start = (bf16[1,3,32,256]{3,2,1,0:T(8,128)(2,1)}, bf16[1,3,32,256]{3,2,1,0:T(8,128)(2,1)S(1)}, u32[]{:S(2)}, u32[]{:S(2)}) collective-permute-start(bf16[1,3,32,256]{3,2,1,0:T(8,128)(2,1)} %bitcast.20), channel_id=1, source_target_pairs={{0,16},{16,0},{1,17},{17,1},{2,18},{18,2},{3,19},{19,3},{4,20},{20... | collective-permute-start | bytes 147464 | tf_op jit(solution)/shard_map/ppermute | solution.py:189
  10.3 4.4 %copy-start.2 = (bf16[1,256,256]{2,1,0:T(8,128)(2,1)S(1)}, bf16[1,256,256]{2,1,0:T(8,128)(2,1)}, u32[]{:S(2)}) copy-start(bf16[1,256,256]{2,1,0:T(8,128)(2,1)} %param.7) | copy-start | bytes 393220
  10.3 29.1 %all-to-all-start = ((bf16[8,256,256]{2,1,0:T(8,128)(2,1)}), bf16[8,256,256]{2,1,0:T(8,128)(2,1)S(1)}, u32[]{:S(2)}, u32[]{:S(2)}) async-start(bf16[8,256,256]{2,1,0:T(8,128)(2,1)} %touch.1), calls=%async_computation | async-start | bytes 2097152 | tf_op jit(solution)/shard_map/all_to_all | solution.py:192
  14.8 35.7 %collective-permute-start.3 = (bf16[2,3,32,256]{3,2,1,0:T(8,128)(2,1)S(1)}, bf16[2,3,32,256]{3,2,1,0:T(8,128)(2,1)S(1)}, u32[]{:S(2)}, u32[]{:S(2)}) collective-permute-start(bf16[2,3,32,256]{3,2,1,0:T(8,128)(2,1)S(1)} %pack.5.refs_0_), channel_id=1, source_target_pairs={{256,0},{288,32},{320,64},{352,96},{384,128},{416,160},{448,192},{... | collective-permute-start | bytes 294920 | tf_op jit(solution)/shard_map/ppermute | solution.py:179
  30.2 20.2 %collective-permute-start.2 = (bf16[2,3,32,256]{3,2,1,0:T(8,128)(2,1)S(1)}, bf16[2,3,32,256]{3,2,1,0:T(8,128)(2,1)S(1)}, u32[]{:S(2)}, u32[]{:S(2)}) collective-permute-start(bf16[2,3,32,256]{3,2,1,0:T(8,128)(2,1)S(1)} %pack.5.refs_0_), channel_id=1, source_target_pairs={{384,0},{416,32},{448,64},{480,96},{0,128},{32,160},{64,192},{96,2... | collective-permute-start | bytes 294920 | tf_op jit(solution)/shard_map/ppermute | solution.py:179
  34.2 16.2 %collective-permute-start.1 = (bf16[2,3,32,256]{3,2,1,0:T(8,128)(2,1)S(1)}, bf16[2,3,32,256]{3,2,1,0:T(8,128)(2,1)S(1)}, u32[]{:S(2)}, u32[]{:S(2)}) collective-permute-start(bf16[2,3,32,256]{3,2,1,0:T(8,128)(2,1)S(1)} %pack.5.refs_0_), channel_id=1, source_target_pairs={{128,0},{160,32},{192,64},{224,96},{256,128},{288,160},{320,192},{... | collective-permute-start | bytes 294920 | tf_op jit(solution)/shard_map/ppermute | solution.py:179
  40.4 28.7 %all-to-all-start.1 = ((bf16[64,4,256]{2,1,0:T(4,128)(2,1)}), bf16[64,4,256]{2,1,0:T(4,128)(2,1)S(1)}, u32[]{:S(2)}, u32[]{:S(2)}) async-start(bf16[64,4,256]{2,1,0:T(4,128)(2,1)} %add_convert_fusion), calls=%async_computation.1 | async-start | bytes 262144 | tf_op jit(solution)/shard_map/all_to_all | solution.py:196
  50.5 26.7 %collective-permute-start.5 = (bf16[8,3,32,256]{3,2,1,0:T(8,128)(2,1)S(1)}, bf16[8,3,32,256]{3,2,1,0:T(8,128)(2,1)S(1)}, u32[]{:S(2)}, u32[]{:S(2)}) collective-permute-start(bf16[8,3,32,256]{3,2,1,0:T(8,128)(2,1)S(1)} %pack.6.refs_0_), channel_id=1, source_target_pairs={{480,0},{0,32},{32,64},{64,96},{96,128},{128,160},{160,192},{192,2... | collective-permute-start | bytes 1179656 | tf_op jit(solution)/shard_map/ppermute | solution.py:179
  53.8 23.4 %collective-permute-start.4 = (bf16[8,3,32,256]{3,2,1,0:T(8,128)(2,1)S(1)}, bf16[8,3,32,256]{3,2,1,0:T(8,128)(2,1)S(1)}, u32[]{:S(2)}, u32[]{:S(2)}) collective-permute-start(bf16[8,3,32,256]{3,2,1,0:T(8,128)(2,1)S(1)} %pack.6.refs_0_), channel_id=1, source_target_pairs={{32,0},{64,32},{96,64},{128,96},{160,128},{192,160},{224,192},{256... | collective-permute-start | bytes 1179656 | tf_op jit(solution)/shard_map/ppermute | solution.py:179
  57.3 19.7 %collective-permute-start.6 = (bf16[4,3,32,256]{3,2,1,0:T(8,128)(2,1)S(1)}, bf16[4,3,32,256]{3,2,1,0:T(8,128)(2,1)S(1)}, u32[]{:S(2)}, u32[]{:S(2)}) collective-permute-start(bf16[4,3,32,256]{3,2,1,0:T(8,128)(2,1)S(1)} %pack.7), channel_id=1, source_target_pairs={{64,0},{96,32},{128,64},{160,96},{192,128},{224,160},{256,192},{28... | collective-permute-start | bytes 589832 | tf_op jit(solution)/shard_map/ppermute | solution.py:179
  61.5 15.7 %collective-permute-start.7 = (bf16[4,3,32,256]{3,2,1,0:T(8,128)(2,1)S(1)}, bf16[4,3,32,256]{3,2,1,0:T(8,128)(2,1)S(1)}, u32[]{:S(2)}, u32[]{:S(2)}) collective-permute-start(bf16[4,3,32,256]{3,2,1,0:T(8,128)(2,1)S(1)} %pack.8), channel_id=1, source_target_pairs={{448,0},{480,32},{0,64},{32,96},{64,128},{96,160},{128,192},{160,2... | collective-permute-start | bytes 589832 | tf_op jit(solution)/shard_map/ppermute | solution.py:179
  77.3 24.3 %copy-start.1 = (f32[2048]{0:T(1024)S(1)}, f32[2048]{0:T(1024)}, u32[]{:S(2)}) copy-start(f32[2048]{0:T(1024)} %param.12) | copy-start | bytes 24580
  77.3 24.3 %collective-permute-start.8 = (bf16[32,3,32,256]{3,2,1,0:T(8,128)(2,1)S(1)}, bf16[32,3,32,256]{3,2,1,0:T(8,128)(2,1)}, u32[]{:S(2)}, u32[]{:S(2)}) collective-permute-start(bf16[32,3,32,256]{3,2,1,0:T(8,128)(2,1)S(1)} %pack.9.own_ref), channel_id=1, source_target_pairs={{0,8},{8,0},{1,9},{9,1},{2,10},{10,2},{3,11},{11,3},{4,12},{12,4},... | collective-permute-start | bytes 4718600 | tf_op jit(solution)/shard_map/ppermute | solution.py:203
  81.2 20.4 %all-to-all-start.2 = ((bf16[8,256,256]{2,1,0:T(8,128)(2,1)}), bf16[8,256,256]{2,1,0:T(8,128)(2,1)S(1)}, u32[]{:S(2)}, u32[]{:S(2)}) async-start(bf16[8,256,256]{2,1,0:T(8,128)(2,1)} %broadcast_in_dim.13), calls=%async_computation.2 | async-start | bytes 2097152 | tf_op jit(solution)/shard_map/all_to_all | solution.py:201
  101.6 18.5 %copy-start.3 = (bf16[1,256,256]{2,1,0:T(8,128)(2,1)S(1)}, bf16[1,256,256]{2,1,0:T(8,128)(2,1)}, u32[]{:S(2)}) copy-start(bf16[1,256,256]{2,1,0:T(8,128)(2,1)} %param.7) | copy-start | bytes 393220
  106.0 32.7 %all-to-all-start.3 = ((bf16[64,4,256]{2,1,0:T(4,128)(2,1)}), bf16[64,4,256]{2,1,0:T(4,128)(2,1)S(1)}, u32[]{:S(2)}, u32[]{:S(2)}) async-start(bf16[64,4,256]{2,1,0:T(4,128)(2,1)} %reshape.24), calls=%async_computation.3 | async-start | bytes 262144 | tf_op jit(solution)/shard_map/all_to_all | solution.py:206

commit v4 on v3

--- a/solution.py
+++ b/solution.py
@@ -92,14 +92,14 @@
     )(*pieces, *event)
 
 
-FOUR = (0, 4, -4, 8)
+FOUR = (0, 8, -4, 4)
 EIGHT = [(f, o) for f in FOUR for o in (0, 1)]
 SLOTS = (
     EIGHT
     + [(1 + f, o) for f, o in EIGHT]
     + [(-1 + f, o) for f, o in EIGHT]
-    + [(2 + f, o) for f, o in EIGHT[:4]]
-    + [(-2 + f, o) for f, o in EIGHT[:2] + EIGHT[4:6]]
+    + [(2 + f, o) for f in (0, 4) for o in (0, 1)]
+    + [(-2 + f, o) for f in (0, -4) for o in (0, 1)]
 )
 
 
@@ -190,11 +190,11 @@
     partial = row_part(row_query[0], row_key[0], row_value[0], out_weight, heads)
     pair = pack(w, theirs)
     parts = lax.all_to_all(touch(partial, pair[1, 0, :16, :128]), HD, 0, 0, tiled=True)
-    up4, down4, up8 = shift(pair, 4), shift(pair, -4), shift(pair, 8)
+    up8, down4, up4 = shift(pair, 8), shift(pair, -4), shift(pair, 4)
     stream = stream_in[0].astype(jnp.float32) + jnp.sum(parts.astype(jnp.float32), axis=0)
     stream_out = stream.astype(jnp.bfloat16)
     columns = lax.all_to_all(stream_out.reshape(seq, here, local), SEQ, 0, 0, tiled=True)
-    eight = pack(pair, up4, down4, up8, event=(stream_out,))
+    eight = pack(pair, up8, down4, up4, event=(stream_out,))
     first, second = pack(pair, up4, event=(stream_out,)), pack(pair, down4, event=(stream_out,))
     up1, down1, up2, down2 = shift(eight, 1), shift(eight, -1), shift(first, 2), shift(second, -2)
     columns = columns.reshape(seq * here, local)

time: 140 us -> 140 us (level)
  waiting for transfers between devices: 47.1 us -> 45.3 us
  starting transfers between devices: 79.3 us -> 81.1 us
    ppermute x1, starting transfers between devices: 2.81 us -> 5.61 us  [on_device(): other = lax.ppermute(own, 'c', [(0, 1), (1, 0)])]
    all_to_all x1, waiting for transfers between devices: 5.55 us -> 3.33 us  [on_device(): lax.all_to_all(stream_out.reshape(seq, here, local), SEQ, 0, 0, tiled=True)]
  transfers between devices with their start and end apart: 13 -> 13, of which waited for: 5 -> 6; matrix products, arithmetic and copies ran while one was open for 2% -> 2% of each run, Pallas kernels for 3% -> 2%
where the time goes in v4:
time: 140 us; the launch traced here: 139 us
  starting transfers between devices  81.1 us (58%)
  waiting for transfers between devices  45.3 us (32%)
  Pallas kernels  7.26 us (5%)
  local copies, waits for them, and re-layouts  3.23 us (2%)
  other arithmetic  1.66 us (1%)
    ppermute x7, starting transfers between devices, shift(): return lax.ppermute(x, 'z', [((i + d) % 16, i) for i in range(16)])  37.3 us
    all_to_all x1, waiting for transfers between devices, on_device(): lax.all_to_all(mixed.reshape(seq, here, local), SEQ, 0, 0, tiled=True)  17.9 us
    all_to_all x1, waiting for transfers between devices, on_device(): lax.all_to_all(jnp.broadcast_to(columns[None], (heads,) + columns.shape),...  15.5 us
    all_to_all x1, starting transfers between devices, on_device(): lax.all_to_all(mixed.reshape(seq, here, local), SEQ, 0, 0, tiled=True)  13.1 us
    all_to_all x1, starting transfers between devices, on_device(): lax.all_to_all(stream_out.reshape(seq, here, local), SEQ, 0, 0, tiled=True)  10 us
    ppermute x7, waiting for transfers between devices, shift(): return lax.ppermute(x, 'z', [((i + d) % 16, i) for i in range(16)])  8.54 us
    ppermute x1, starting transfers between devices, on_device(): theirs = lax.ppermute(w, 'xh', [(0, 1), (1, 0)])  5.61 us
    ppermute x1, starting transfers between devices, on_device(): other = lax.ppermute(own, 'c', [(0, 1), (1, 0)])  5.61 us
  transfers between devices with their start and end apart: 13, of which 6 were waited for; matrix products, arithmetic and copies ran while one was open for 2% of the time, Pallas kernels for 2%

profile of v4, /device:TPU:1, one launch (start us, length us, event | category | flops | bytes accessed | tf_op | source)
XLA Modules:
  0.0 139.4 jit_solution(10837187878725813794)
XLA Ops:
  0.6 0.0 copy-start
  0.6 5.6 %collective-permute-start = (bf16[1,3,32,256]{3,2,1,0:T(8,128)(2,1)}, bf16[1,3,32,256]{3,2,1,0:T(8,128)(2,1)S(1)}, u32[]{:S(2)}, u32[]{:S(2)}) collective-permute-start(bf16[1,3,32,256]{3,2,1,0:T(8,128)(2,1)} %bitcast.20), channel_id=1, source_target_pairs={{0,16},{16,0},{1,17},{17,1},{2,18},{18,2},{3,19},{19,3},{4,20},{20... | collective-permute-start | bytes 147464 | tf_op jit(solution)/shard_map/ppermute | solution.py:189
  6.3 3.4 %row_attention.1.x_ref = bf16[8,256,256]{2,1,0:T(8,128)(2,1)} custom-call(bf16[256,256]{1,0:T(8,128)(2,1)} %bitcast.23, bf16[256,256]{1,0:T(8,128)(2,1)} %bitcast.24, bf16[256,256]{1,0:T(8,128)(2,1)} %bitcast.25, bf16[256,2048]{1,0:T(8,128)(2,1)} %w_hbm.1), custom_call_target="tpu_custom_call" | custom-call | flops 335544320 | bytes 3145728 | tf_op jit(solution)/shard_map/row_attention/pallas_call | solution.py:54
  9.7 0.0 collective-permute-done.refs_1_
  9.7 0.0 copy-done
  9.7 0.6 slice_bitcast_fusion.event_ref
  10.3 0.0 copy-start.2
  10.3 4.3 %all-to-all-start = ((bf16[8,256,256]{2,1,0:T(8,128)(2,1)}), bf16[8,256,256]{2,1,0:T(8,128)(2,1)S(1)}, u32[]{:S(2)}, u32[]{:S(2)}) async-start(bf16[8,256,256]{2,1,0:T(8,128)(2,1)} %touch.1), calls=%async_computation | async-start | bytes 2097152 | tf_op jit(solution)/shard_map/all_to_all | solution.py:192
  14.7 0.0 copy-done.2
  14.7 0.1 reshape.26
  14.8 12.5 %collective-permute-start.3 = (bf16[2,3,32,256]{3,2,1,0:T(8,128)(2,1)S(1)}, bf16[2,3,32,256]{3,2,1,0:T(8,128)(2,1)S(1)}, u32[]{:S(2)}, u32[]{:S(2)}) collective-permute-start(bf16[2,3,32,256]{3,2,1,0:T(8,128)(2,1)S(1)} %pack.5.refs_0_), channel_id=1, source_target_pairs={{128,0},{160,32},{192,64},{224,96},{256,128},{288,160},{320,192},{... | collective-permute-start | bytes 294920 | tf_op jit(solution)/shard_map/ppermute | solution.py:179
  27.2 1.9 %collective-permute-start.2 = (bf16[2,3,32,256]{3,2,1,0:T(8,128)(2,1)S(1)}, bf16[2,3,32,256]{3,2,1,0:T(8,128)(2,1)S(1)}, u32[]{:S(2)}, u32[]{:S(2)}) collective-permute-start(bf16[2,3,32,256]{3,2,1,0:T(8,128)(2,1)S(1)} %pack.5.refs_0_), channel_id=1, source_target_pairs={{384,0},{416,32},{448,64},{480,96},{0,128},{32,160},{64,192},{96,2... | collective-permute-start | bytes 294920 | tf_op jit(solution)/shard_map/ppermute | solution.py:179
  29.2 10.3 %collective-permute-start.1 = (bf16[2,3,32,256]{3,2,1,0:T(8,128)(2,1)S(1)}, bf16[2,3,32,256]{3,2,1,0:T(8,128)(2,1)S(1)}, u32[]{:S(2)}, u32[]{:S(2)}) collective-permute-start(bf16[2,3,32,256]{3,2,1,0:T(8,128)(2,1)S(1)} %pack.5.refs_0_), channel_id=1, source_target_pairs={{256,0},{288,32},{320,64},{352,96},{384,128},{416,160},{448,192},{... | collective-permute-start | bytes 294920 | tf_op jit(solution)/shard_map/ppermute | solution.py:179
  39.4 0.0 all-to-all-done
  39.4 0.1 convert_reduce_fusion
  39.6 0.1 reduce_sum.15
  39.7 0.7 add_convert_fusion
  40.4 10.0 %all-to-all-start.1 = ((bf16[64,4,256]{2,1,0:T(4,128)(2,1)}), bf16[64,4,256]{2,1,0:T(4,128)(2,1)S(1)}, u32[]{:S(2)}, u32[]{:S(2)}) async-start(bf16[64,4,256]{2,1,0:T(4,128)(2,1)} %add_convert_fusion), calls=%async_computation.1 | async-start | bytes 262144 | tf_op jit(solution)/shard_map/all_to_all | solution.py:196
  50.4 0.0 collective-permute-done.3.refs_3_.refs_1_
  50.5 0.0 collective-permute-done.2.refs_2_.refs_1_
  50.5 2.7 %collective-permute-done.1.refs_1_ = bf16[2,3,32,256]{3,2,1,0:T(8,128)(2,1)S(1)} collective-permute-done((bf16[2,3,32,256]{3,2,1,0:T(8,128)(2,1)S(1)}, bf16[2,3,32,256]{3,2,1,0:T(8,128)(2,1)S(1)}, u32[]{:S(2)}, u32[]{:S(2)}) %collective-permute-start.1) | collective-permute-done | bytes 98336 | tf_op jit(solution)/shard_map/ppermute | solution.py:179
  53.2 1.9 %collective-permute-start.5 = (bf16[8,3,32,256]{3,2,1,0:T(8,128)(2,1)S(1)}, bf16[8,3,32,256]{3,2,1,0:T(8,128)(2,1)S(1)}, u32[]{:S(2)}, u32[]{:S(2)}) collective-permute-start(bf16[8,3,32,256]{3,2,1,0:T(8,128)(2,1)S(1)} %pack.6.refs_0_), channel_id=1, source_target_pairs={{480,0},{0,32},{32,64},{64,96},{96,128},{128,160},{160,192},{192,2... | collective-permute-start | bytes 1179656 | tf_op jit(solution)/shard_map/ppermute | solution.py:179
  55.2 4.6 %collective-permute-start.4 = (bf16[8,3,32,256]{3,2,1,0:T(8,128)(2,1)S(1)}, bf16[8,3,32,256]{3,2,1,0:T(8,128)(2,1)S(1)}, u32[]{:S(2)}, u32[]{:S(2)}) collective-permute-start(bf16[8,3,32,256]{3,2,1,0:T(8,128)(2,1)S(1)} %pack.6.refs_0_), channel_id=1, source_target_pairs={{32,0},{64,32},{96,64},{128,96},{160,128},{192,160},{224,192},{256... | collective-permute-start | bytes 1179656 | tf_op jit(solution)/shard_map/ppermute | solution.py:179
  59.8 1.9 %collective-permute-start.6 = (bf16[4,3,32,256]{3,2,1,0:T(8,128)(2,1)S(1)}, bf16[4,3,32,256]{3,2,1,0:T(8,128)(2,1)S(1)}, u32[]{:S(2)}, u32[]{:S(2)}) collective-permute-start(bf16[4,3,32,256]{3,2,1,0:T(8,128)(2,1)S(1)} %pack.7), channel_id=1, source_target_pairs={{64,0},{96,32},{128,64},{160,96},{192,128},{224,160},{256,192},{28... | collective-permute-start | bytes 589832 | tf_op jit(solution)/shard_map/ppermute | solution.py:179
  61.7 4.3 %collective-permute-start.7 = (bf16[4,3,32,256]{3,2,1,0:T(8,128)(2,1)S(1)}, bf16[4,3,32,256]{3,2,1,0:T(8,128)(2,1)S(1)}, u32[]{:S(2)}, u32[]{:S(2)}) collective-permute-start(bf16[4,3,32,256]{3,2,1,0:T(8,128)(2,1)S(1)} %pack.8), channel_id=1, source_target_pairs={{448,0},{480,32},{0,64},{32,96},{64,128},{96,160},{128,192},{160,2... | collective-permute-start | bytes 589832 | tf_op jit(solution)/shard_map/ppermute | solution.py:179
  66.0 3.3 %all-to-all-done.1 = bf16[64,4,256]{2,1,0:T(4,128)(2,1)S(1)} async-done(((bf16[64,4,256]{2,1,0:T(4,128)(2,1)}), bf16[64,4,256]{2,1,0:T(4,128)(2,1)S(1)}, u32[]{:S(2)}, u32[]{:S(2)}) %all-to-all-start.1) | async-done | bytes 131104 | tf_op jit(solution)/shard_map/all_to_all | solution.py:196
  69.3 5.4 %collective-permute-done.6.refs_3_ = bf16[4,3,32,256]{3,2,1,0:T(8,128)(2,1)S(1)} collective-permute-done((bf16[4,3,32,256]{3,2,1,0:T(8,128)(2,1)S(1)}, bf16[4,3,32,256]{3,2,1,0:T(8,128)(2,1)S(1)}, u32[]{:S(2)}, u32[]{:S(2)}) %collective-permute-start.6) | collective-permute-done | bytes 196640 | tf_op jit(solution)/shard_map/ppermute | solution.py:179
  74.8 0.4 collective-permute-done.7.refs_4_
  75.1 0.0 collective-permute-done.5.refs_2_
  75.1 0.0 collective-permute-done.4.refs_1_
  75.1 0.1 pack.9.own_ref
  75.3 0.0 copy-start.1
  75.3 5.6 %collective-permute-start.8 = (bf16[32,3,32,256]{3,2,1,0:T(8,128)(2,1)S(1)}, bf16[32,3,32,256]{3,2,1,0:T(8,128)(2,1)}, u32[]{:S(2)}, u32[]{:S(2)}) collective-permute-start(bf16[32,3,32,256]{3,2,1,0:T(8,128)(2,1)S(1)} %pack.9.own_ref), channel_id=1, source_target_pairs={{0,8},{8,0},{1,9},{9,1},{2,10},{10,2},{3,11},{11,3},{4,12},{12,4},... | collective-permute-start | bytes 4718600 | tf_op jit(solution)/shard_map/ppermute | solution.py:203
  80.9 1.1 broadcast_in_dim.13
  81.9 5.1 %all-to-all-start.2 = ((bf16[8,256,256]{2,1,0:T(8,128)(2,1)}), bf16[8,256,256]{2,1,0:T(8,128)(2,1)S(1)}, u32[]{:S(2)}, u32[]{:S(2)}) async-start(bf16[8,256,256]{2,1,0:T(8,128)(2,1)} %broadcast_in_dim.13), calls=%async_computation.2 | async-start | bytes 2097152 | tf_op jit(solution)/shard_map/all_to_all | solution.py:201
  87.0 0.1 pad_add_fusion.where_ref
  87.1 15.5 %all-to-all-done.2.x_ref = bf16[8,256,256]{2,1,0:T(8,128)(2,1)S(1)} async-done(((bf16[8,256,256]{2,1,0:T(8,128)(2,1)}), bf16[8,256,256]{2,1,0:T(8,128)(2,1)S(1)}, u32[]{:S(2)}, u32[]{:S(2)}) %all-to-all-start.2) | async-done | bytes 1048608 | tf_op jit(solution)/shard_map/all_to_all | solution.py:201
  102.6 0.0 collective-permute-done.8.other_ref
  102.6 0.0 copy-done.1
  102.6 0.0 copy-start.3
  102.6 3.7 %column_attention.1 = bf16[256,256]{1,0:T(8,128)(2,1)S(1)} custom-call(s32[3]{0:T(128)S(1)} %pad_add_fusion.where_ref, bf16[8,256,256]{2,1,0:T(8,128)(2,1)S(1)} %all-to-all-done.2.x_ref, f32[1,2048]{1,0:T(1,128)S(1)} %bitcast.22, bf16[32,3,32,256]{3,2,1,0:T(8,128)(2,1)S(1)} %pack.9.own_ref, bf16[32,3,32,256]{3,2,1,0:T(8,128)(2,1)} %collective-permute-done.8.other_ref), custom_call_target="tpu_custom_call" | custom-call | flops 805306368 | bytes 5242880 | tf_op jit(solution)/shard_map/column_attention/pallas_call | solution.py:161
  106.3 0.7 reshape.24
  107.0 13.1 %all-to-all-start.3 = ((bf16[64,4,256]{2,1,0:T(4,128)(2,1)}), bf16[64,4,256]{2,1,0:T(4,128)(2,1)S(1)}, u32[]{:S(2)}, u32[]{:S(2)}) async-start(bf16[64,4,256]{2,1,0:T(4,128)(2,1)} %reshape.24), calls=%async_computation.3 | async-start | bytes 262144 | tf_op jit(solution)/shard_map/all_to_all | solution.py:206
  120.1 0.0 copy-done.3
  120.1 0.7 fusion.1
  120.8 17.9 %all-to-all-done.3 = bf16[64,4,256]{2,1,0:T(4,128)(2,1)S(1)} async-done(((bf16[64,4,256]{2,1,0:T(4,128)(2,1)}), bf16[64,4,256]{2,1,0:T(4,128)(2,1)S(1)}, u32[]{:S(2)}, u32[]{:S(2)}) %all-to-all-start.3) | async-done | bytes 131104 | tf_op jit(solution)/shard_map/all_to_all | solution.py:206
  138.7 0.7 reshape.25
  (7 shorter events, 0.1 us)
Async XLA Ops:
  0.6 9.1 %copy-start = (bf16[32,3,256]{2,0,1:T(8,128)(2,1)S(1)}, bf16[32,3,256]{2,0,1:T(8,128)(2,1)}, u32[]{:S(2)}) copy-start(bf16[32,3,256]{2,0,1:T(8,128)(2,1)} %param.13) | copy-start | bytes 147460
  0.6 9.1 %collective-permute-start = (bf16[1,3,32,256]{3,2,1,0:T(8,128)(2,1)}, bf16[1,3,32,256]{3,2,1,0:T(8,128)(2,1)S(1)}, u32[]{:S(2)}, u32[]{:S(2)}) collective-permute-start(bf16[1,3,32,256]{3,2,1,0:T(8,128)(2,1)} %bitcast.20), channel_id=1, source_target_pairs={{0,16},{16,0},{1,17},{17,1},{2,18},{18,2},{3,19},{19,3},{4,20},{20... | collective-permute-start | bytes 147464 | tf_op jit(solution)/shard_map/ppermute | solution.py:189
  10.3 4.4 %copy-start.2 = (bf16[1,256,256]{2,1,0:T(8,128)(2,1)S(1)}, bf16[1,256,256]{2,1,0:T(8,128)(2,1)}, u32[]{:S(2)}) copy-start(bf16[1,256,256]{2,1,0:T(8,128)(2,1)} %param.7) | copy-start | bytes 393220
  10.3 29.1 %all-to-all-start = ((bf16[8,256,256]{2,1,0:T(8,128)(2,1)}), bf16[8,256,256]{2,1,0:T(8,128)(2,1)S(1)}, u32[]{:S(2)}, u32[]{:S(2)}) async-start(bf16[8,256,256]{2,1,0:T(8,128)(2,1)} %touch.1), calls=%async_computation | async-start | bytes 2097152 | tf_op jit(solution)/shard_map/all_to_all | solution.py:192
  14.8 35.7 %collective-permute-start.3 = (bf16[2,3,32,256]{3,2,1,0:T(8,128)(2,1)S(1)}, bf16[2,3,32,256]{3,2,1,0:T(8,128)(2,1)S(1)}, u32[]{:S(2)}, u32[]{:S(2)}) collective-permute-start(bf16[2,3,32,256]{3,2,1,0:T(8,128)(2,1)S(1)} %pack.5.refs_0_), channel_id=1, source_target_pairs={{128,0},{160,32},{192,64},{224,96},{256,128},{288,160},{320,192},{... | collective-permute-start | bytes 294920 | tf_op jit(solution)/shard_map/ppermute | solution.py:179
  27.2 23.2 %collective-permute-start.2 = (bf16[2,3,32,256]{3,2,1,0:T(8,128)(2,1)S(1)}, bf16[2,3,32,256]{3,2,1,0:T(8,128)(2,1)S(1)}, u32[]{:S(2)}, u32[]{:S(2)}) collective-permute-start(bf16[2,3,32,256]{3,2,1,0:T(8,128)(2,1)S(1)} %pack.5.refs_0_), channel_id=1, source_target_pairs={{384,0},{416,32},{448,64},{480,96},{0,128},{32,160},{64,192},{96,2... | collective-permute-start | bytes 294920 | tf_op jit(solution)/shard_map/ppermute | solution.py:179
  29.2 24.0 %collective-permute-start.1 = (bf16[2,3,32,256]{3,2,1,0:T(8,128)(2,1)S(1)}, bf16[2,3,32,256]{3,2,1,0:T(8,128)(2,1)S(1)}, u32[]{:S(2)}, u32[]{:S(2)}) collective-permute-start(bf16[2,3,32,256]{3,2,1,0:T(8,128)(2,1)S(1)} %pack.5.refs_0_), channel_id=1, source_target_pairs={{256,0},{288,32},{320,64},{352,96},{384,128},{416,160},{448,192},{... | collective-permute-start | bytes 294920 | tf_op jit(solution)/shard_map/ppermute | solution.py:179
  40.4 28.9 %all-to-all-start.1 = ((bf16[64,4,256]{2,1,0:T(4,128)(2,1)}), bf16[64,4,256]{2,1,0:T(4,128)(2,1)S(1)}, u32[]{:S(2)}, u32[]{:S(2)}) async-start(bf16[64,4,256]{2,1,0:T(4,128)(2,1)} %add_convert_fusion), calls=%async_computation.1 | async-start | bytes 262144 | tf_op jit(solution)/shard_map/all_to_all | solution.py:196
  53.2 21.9 %collective-permute-start.5 = (bf16[8,3,32,256]{3,2,1,0:T(8,128)(2,1)S(1)}, bf16[8,3,32,256]{3,2,1,0:T(8,128)(2,1)S(1)}, u32[]{:S(2)}, u32[]{:S(2)}) collective-permute-start(bf16[8,3,32,256]{3,2,1,0:T(8,128)(2,1)S(1)} %pack.6.refs_0_), channel_id=1, source_target_pairs={{480,0},{0,32},{32,64},{64,96},{96,128},{128,160},{160,192},{192,2... | collective-permute-start | bytes 1179656 | tf_op jit(solution)/shard_map/ppermute | solution.py:179
  55.2 20.0 %collective-permute-start.4 = (bf16[8,3,32,256]{3,2,1,0:T(8,128)(2,1)S(1)}, bf16[8,3,32,256]{3,2,1,0:T(8,128)(2,1)S(1)}, u32[]{:S(2)}, u32[]{:S(2)}) collective-permute-start(bf16[8,3,32,256]{3,2,1,0:T(8,128)(2,1)S(1)} %pack.6.refs_0_), channel_id=1, source_target_pairs={{32,0},{64,32},{96,64},{128,96},{160,128},{192,160},{224,192},{256... | collective-permute-start | bytes 1179656 | tf_op jit(solution)/shard_map/ppermute | solution.py:179
  59.8 15.0 %collective-permute-start.6 = (bf16[4,3,32,256]{3,2,1,0:T(8,128)(2,1)S(1)}, bf16[4,3,32,256]{3,2,1,0:T(8,128)(2,1)S(1)}, u32[]{:S(2)}, u32[]{:S(2)}) collective-permute-start(bf16[4,3,32,256]{3,2,1,0:T(8,128)(2,1)S(1)} %pack.7), channel_id=1, source_target_pairs={{64,0},{96,32},{128,64},{160,96},{192,128},{224,160},{256,192},{28... | collective-permute-start | bytes 589832 | tf_op jit(solution)/shard_map/ppermute | solution.py:179
  61.7 13.4 %collective-permute-start.7 = (bf16[4,3,32,256]{3,2,1,0:T(8,128)(2,1)S(1)}, bf16[4,3,32,256]{3,2,1,0:T(8,128)(2,1)S(1)}, u32[]{:S(2)}, u32[]{:S(2)}) collective-permute-start(bf16[4,3,32,256]{3,2,1,0:T(8,128)(2,1)S(1)} %pack.8), channel_id=1, source_target_pairs={{448,0},{480,32},{0,64},{32,96},{64,128},{96,160},{128,192},{160,2... | collective-permute-start | bytes 589832 | tf_op jit(solution)/shard_map/ppermute | solution.py:179
  75.3 27.4 %copy-start.1 = (f32[2048]{0:T(1024)S(1)}, f32[2048]{0:T(1024)}, u32[]{:S(2)}) copy-start(f32[2048]{0:T(1024)} %param.12) | copy-start | bytes 24580
  75.3 27.4 %collective-permute-start.8 = (bf16[32,3,32,256]{3,2,1,0:T(8,128)(2,1)S(1)}, bf16[32,3,32,256]{3,2,1,0:T(8,128)(2,1)}, u32[]{:S(2)}, u32[]{:S(2)}) collective-permute-start(bf16[32,3,32,256]{3,2,1,0:T(8,128)(2,1)S(1)} %pack.9.own_ref), channel_id=1, source_target_pairs={{0,8},{8,0},{1,9},{9,1},{2,10},{10,2},{3,11},{11,3},{4,12},{12,4},... | collective-permute-start | bytes 4718600 | tf_op jit(solution)/shard_map/ppermute | solution.py:203
  81.9 20.7 %all-to-all-start.2 = ((bf16[8,256,256]{2,1,0:T(8,128)(2,1)}), bf16[8,256,256]{2,1,0:T(8,128)(2,1)S(1)}, u32[]{:S(2)}, u32[]{:S(2)}) async-start(bf16[8,256,256]{2,1,0:T(8,128)(2,1)} %broadcast_in_dim.13), calls=%async_computation.2 | async-start | bytes 2097152 | tf_op jit(solution)/shard_map/all_to_all | solution.py:201
  102.6 17.5 %copy-start.3 = (bf16[1,256,256]{2,1,0:T(8,128)(2,1)S(1)}, bf16[1,256,256]{2,1,0:T(8,128)(2,1)}, u32[]{:S(2)}) copy-start(bf16[1,256,256]{2,1,0:T(8,128)(2,1)} %param.7) | copy-start | bytes 393220
  107.0 31.7 %all-to-all-start.3 = ((bf16[64,4,256]{2,1,0:T(4,128)(2,1)}), bf16[64,4,256]{2,1,0:T(4,128)(2,1)S(1)}, u32[]{:S(2)}, u32[]{:S(2)}) async-start(bf16[64,4,256]{2,1,0:T(4,128)(2,1)} %reshape.24), calls=%async_computation.3 | async-start | bytes 262144 | tf_op jit(solution)/shard_map/all_to_all | solution.py:206

commit v5 on v4

--- a/solution.py
+++ b/solution.py
@@ -74,7 +74,7 @@
         at += ref.shape[0]
 
 
-def pack(*pieces, event=()):
+def pack(*pieces, event=(), weight=0):
     total = sum(p.shape[0] for p in pieces)
     shape = (total,) + pieces[0].shape[1:]
     size = 4
@@ -86,8 +86,8 @@
         out_shape=jax.ShapeDtypeStruct(shape, pieces[0].dtype),
         in_specs=[vm] * (len(pieces) + len(event)),
         out_specs=vm,
-        compiler_params=pltpu.CompilerParams(vmem_limit_bytes=16 * 1024 * 1024),
-        cost_estimate=pl.CostEstimate(flops=0, bytes_accessed=size, transcendentals=0),
+        compiler_params=pltpu.CompilerParams(vmem_limit_bytes=4 * 1024 * 1024),
+        cost_estimate=pl.CostEstimate(flops=weight, bytes_accessed=size, transcendentals=0),
         name="pack",
     )(*pieces, *event)
 
@@ -120,15 +120,19 @@
     )(x, event)
 
 
-def column_kernel(where_ref, x_ref, gain_ref, own_ref, other_ref, out_ref, w_ref, normed_ref):
+def column_kernel(count, where_ref, x_ref, gain_ref, *refs):
+    pieces, (out_ref, w_ref, normed_ref) = refs[: 2 * count], refs[2 * count :]
     z, xh, core = where_ref[0], where_ref[1], where_ref[2]
-    for side, ref in enumerate((own_ref, other_ref)):
+    for side in (0, 1):
         c = core if side == 0 else 1 - core
-        for i, (off, flip) in enumerate(SLOTS):
-            zi = lax.rem(z + (off + 16), 16)
-            xi = 1 - xh if flip else xh
-            for j in range(3):
-                w_ref[j, zi, xi, c] = ref[i, j]
+        slots = iter(SLOTS)
+        for ref in pieces[side * count : (side + 1) * count]:
+            for i in range(ref.shape[0]):
+                off, flip = next(slots)
+                zi = lax.rem(z + (off + 16), 16)
+                xi = 1 - xh if flip else xh
+                for j in range(3):
+                    w_ref[j, zi, xi, c] = ref[i, j]
     heads, n, local = x_ref.shape
     total = jnp.zeros((n, 1), jnp.float32)
     for h in range(heads):
@@ -155,24 +159,25 @@
 
 
 def column_part(where, x, gain, own, other):
+    count = len(own)
     heads, n, local = x.shape
-    rows = own.shape[2]
+    rows = own[0].shape[2]
     vm = pl.BlockSpec(memory_space=pltpu.VMEM)
     return pl.pallas_call(
-        column_kernel,
+        functools.partial(column_kernel, count),
         out_shape=jax.ShapeDtypeStruct((n, local), jnp.bfloat16),
-        in_specs=[pl.BlockSpec(memory_space=pltpu.SMEM), vm, vm, vm, vm],
+        in_specs=[pl.BlockSpec(memory_space=pltpu.SMEM)] + [vm] * (2 + 2 * count),
         out_specs=vm,
         scratch_shapes=[
             pltpu.VMEM((3, 16, 2, 2, rows, local), jnp.bfloat16),
             pltpu.VMEM((n, heads * local), jnp.bfloat16),
         ],
-        compiler_params=pltpu.CompilerParams(vmem_limit_bytes=40 * 1024 * 1024),
+        compiler_params=pltpu.CompilerParams(vmem_limit_bytes=20 * 1024 * 1024),
         cost_estimate=pl.CostEstimate(
             flops=2 * n * heads * local * 3 * local, bytes_accessed=5 * 2**20, transcendentals=2 * n * n
         ),
         name="column_attention",
-    )(where, x, gain, own, other)
+    )(where, x, gain, *own, *other)
 
 
 def shift(x, d):
@@ -194,13 +199,13 @@
     stream = stream_in[0].astype(jnp.float32) + jnp.sum(parts.astype(jnp.float32), axis=0)
     stream_out = stream.astype(jnp.bfloat16)
     columns = lax.all_to_all(stream_out.reshape(seq, here, local), SEQ, 0, 0, tiled=True)
-    eight = pack(pair, up8, down4, up4, event=(stream_out,))
+    eight = pack(pair, up8, down4, up4, event=(stream_out,), weight=1000000000)
     first, second = pack(pair, up4, event=(stream_out,)), pack(pair, down4, event=(stream_out,))
     up1, down1, up2, down2 = shift(eight, 1), shift(eight, -1), shift(first, 2), shift(second, -2)
     columns = columns.reshape(seq * here, local)
     x = lax.all_to_all(jnp.broadcast_to(columns[None], (heads,) + columns.shape), HD, 0, 0, tiled=True)
-    own = pack(eight, up1, down1, up2, down2, event=(columns,))
-    other = lax.ppermute(own, "c", [(0, 1), (1, 0)])
+    own = (pack(eight, up1), pack(down1, up2, down2))
+    other = [lax.ppermute(piece, "c", [(0, 1), (1, 0)]) for piece in own]
     where = jnp.stack([lax.axis_index("z"), lax.axis_index("xh"), lax.axis_index("c")]).astype(jnp.int32)
     mixed = column_part(where, x, norm_gain.reshape(1, -1), own, other)
     back = lax.all_to_all(mixed.reshape(seq, here, local), SEQ, 0, 0, tiled=True)

time: 140 us -> 126 us (0.900)
  waiting for transfers between devices: 45.3 us -> 28.7 us
  starting transfers between devices: 81.1 us -> 78.2 us
  Pallas kernels: 7.26 us -> 9.3 us
  local copies, waits for them, and re-layouts: 3.23 us -> 4.98 us
    all_to_all x1, waiting for transfers between devices: 15.5 us -> 5.22 us  [on_device(): lax.all_to_all(jnp.broadcast_to(columns[None], (heads,) + columns.shape),...]
    ppermute x7, waiting for transfers between devices: 8.54 us -> 0.02 us  [shift(): return lax.ppermute(x, 'z', [((i + d) % 16, i) for i in range(16)])]
    pallas_call x5 -> x6, Pallas kernels: 0.17 us -> 2.55 us  [pack(): pl.pallas_call(functools.partial(pack_kernel, len(pieces)), out_shape=jax...]
    ppermute x1 -> x2, waiting for transfers between devices: 0.01 us -> 2.3 us  [on_device(): other = [lax.ppermute(piece, 'c', [(0, 1), (1, 0)]) for piece in own]]
    unnamed x8 -> x12, local copies, waits for them, and re-layouts: 0.02 us -> 1.77 us
    all_to_all x1, starting transfers between devices: 13.1 us -> 11.5 us  [on_device(): lax.all_to_all(mixed.reshape(seq, here, local), SEQ, 0, 0, tiled=True)]
    ppermute x1 -> x2, starting transfers between devices: 5.61 us -> 4.54 us  [on_device(): other = [lax.ppermute(piece, 'c', [(0, 1), (1, 0)]) for piece in own]]
  transfers between devices with their start and end apart: 13 -> 14, of which waited for: 6 -> 4; matrix products, arithmetic and copies ran while one was open for 2% -> 3% of each run, Pallas kernels for 2% -> 5%
where the time goes in v5:
time: 126 us; the launch traced here: 125 us
  starting transfers between devices  78.2 us (62%)
  waiting for transfers between devices  28.7 us (23%)
  Pallas kernels  9.3 us (7%)
  local copies, waits for them, and re-layouts  4.98 us (4%)
  other arithmetic  2.65 us (2%)
    ppermute x7, starting transfers between devices, shift(): return lax.ppermute(x, 'z', [((i + d) % 16, i) for i in range(16)])  37.5 us
    all_to_all x1, waiting for transfers between devices, on_device(): lax.all_to_all(mixed.reshape(seq, here, local), SEQ, 0, 0, tiled=True)  16.9 us
    all_to_all x1, starting transfers between devices, on_device(): lax.all_to_all(mixed.reshape(seq, here, local), SEQ, 0, 0, tiled=True)  11.5 us
    all_to_all x1, starting transfers between devices, on_device(): lax.all_to_all(stream_out.reshape(seq, here, local), SEQ, 0, 0, tiled=True)  9.99 us
    ppermute x1, starting transfers between devices, on_device(): theirs = lax.ppermute(w, 'xh', [(0, 1), (1, 0)])  5.48 us
    all_to_all x1, waiting for transfers between devices, on_device(): lax.all_to_all(jnp.broadcast_to(columns[None], (heads,) + columns.shape),...  5.22 us
    all_to_all x1, starting transfers between devices, on_device(): lax.all_to_all(jnp.broadcast_to(columns[None], (heads,) + columns.shape),...  4.81 us
    ppermute x2, starting transfers between devices, on_device(): other = [lax.ppermute(piece, 'c', [(0, 1), (1, 0)]) for piece in own]  4.54 us
  transfers between devices with their start and end apart: 14, of which 4 were waited for; matrix products, arithmetic and copies ran while one was open for 3% of the time, Pallas kernels for 5%

profile of v5, /device:TPU:1, one launch (start us, length us, event | category | flops | bytes accessed | tf_op | source)
XLA Modules:
  0.0 124.8 jit_solution(4855589080792425844)
XLA Ops:
  0.6 5.5 %collective-permute-start = (bf16[1,3,32,256]{3,2,1,0:T(8,128)(2,1)}, bf16[1,3,32,256]{3,2,1,0:T(8,128)(2,1)S(1)}, u32[]{:S(2)}, u32[]{:S(2)}) collective-permute-start(bf16[1,3,32,256]{3,2,1,0:T(8,128)(2,1)} %bitcast.20), channel_id=1, source_target_pairs={{0,16},{16,0},{1,17},{17,1},{2,18},{18,2},{3,19},{19,3},{4,20},{20... | collective-permute-start | bytes 147464 | tf_op jit(solution)/shard_map/ppermute | solution.py:194
  6.1 3.4 %row_attention.1.x_ref = bf16[8,256,256]{2,1,0:T(8,128)(2,1)} custom-call(bf16[256,256]{1,0:T(8,128)(2,1)} %bitcast.23, bf16[256,256]{1,0:T(8,128)(2,1)} %bitcast.24, bf16[256,256]{1,0:T(8,128)(2,1)} %bitcast.25, bf16[256,2048]{1,0:T(8,128)(2,1)} %w_hbm.1), custom_call_target="tpu_custom_call" | custom-call | flops 335544320 | bytes 3145728 | tf_op jit(solution)/shard_map/row_attention/pallas_call | solution.py:54
  9.6 0.0 collective-permute-done.refs_1_
  9.6 0.6 slice_bitcast_fusion.event_ref
  10.2 4.3 %all-to-all-start = ((bf16[8,256,256]{2,1,0:T(8,128)(2,1)}), bf16[8,256,256]{2,1,0:T(8,128)(2,1)S(1)}, u32[]{:S(2)}, u32[]{:S(2)}) async-start(bf16[8,256,256]{2,1,0:T(8,128)(2,1)} %touch.1), calls=%async_computation | async-start | bytes 2097152 | tf_op jit(solution)/shard_map/all_to_all | solution.py:197
  14.6 0.0 copy-done.5
  14.6 0.1 reshape.25
  14.6 15.4 %collective-permute-start.1 = (bf16[2,3,32,256]{3,2,1,0:T(8,128)(2,1)S(1)}, bf16[2,3,32,256]{3,2,1,0:T(8,128)(2,1)S(1)}, u32[]{:S(2)}, u32[]{:S(2)}) collective-permute-start(bf16[2,3,32,256]{3,2,1,0:T(8,128)(2,1)S(1)} %pack.6.refs_0_), channel_id=1, source_target_pairs={{256,0},{288,32},{320,64},{352,96},{384,128},{416,160},{448,192},{... | collective-permute-start | bytes 294920 | tf_op jit(solution)/shard_map/ppermute | solution.py:184
  30.1 4.0 %collective-permute-start.2 = (bf16[2,3,32,256]{3,2,1,0:T(8,128)(2,1)S(1)}, bf16[2,3,32,256]{3,2,1,0:T(8,128)(2,1)S(1)}, u32[]{:S(2)}, u32[]{:S(2)}) collective-permute-start(bf16[2,3,32,256]{3,2,1,0:T(8,128)(2,1)S(1)} %pack.6.refs_0_), channel_id=1, source_target_pairs={{384,0},{416,32},{448,64},{480,96},{0,128},{32,160},{64,192},{96,2... | collective-permute-start | bytes 294920 | tf_op jit(solution)/shard_map/ppermute | solution.py:184
  34.1 5.2 %collective-permute-start.3 = (bf16[2,3,32,256]{3,2,1,0:T(8,128)(2,1)S(1)}, bf16[2,3,32,256]{3,2,1,0:T(8,128)(2,1)S(1)}, u32[]{:S(2)}, u32[]{:S(2)}) collective-permute-start(bf16[2,3,32,256]{3,2,1,0:T(8,128)(2,1)S(1)} %pack.6.refs_0_), channel_id=1, source_target_pairs={{128,0},{160,32},{192,64},{224,96},{256,128},{288,160},{320,192},{... | collective-permute-start | bytes 294920 | tf_op jit(solution)/shard_map/ppermute | solution.py:184
  39.3 0.0 all-to-all-done
  39.3 0.1 convert_reduce_fusion
  39.5 0.1 reduce_sum.15
  39.5 0.7 add_convert_fusion
  40.3 10.0 %all-to-all-start.1 = ((bf16[64,4,256]{2,1,0:T(4,128)(2,1)}), bf16[64,4,256]{2,1,0:T(4,128)(2,1)S(1)}, u32[]{:S(2)}, u32[]{:S(2)}) async-start(bf16[64,4,256]{2,1,0:T(4,128)(2,1)} %add_convert_fusion), calls=%async_computation.1 | async-start | bytes 262144 | tf_op jit(solution)/shard_map/all_to_all | solution.py:201
  50.3 0.0 collective-permute-done.1.refs_1_
  50.3 0.0 collective-permute-done.2.refs_2_.refs_1_
  50.3 0.0 collective-permute-done.3.refs_3_.refs_1_
  50.4 4.8 %collective-permute-start.4 = (bf16[8,3,32,256]{3,2,1,0:T(8,128)(2,1)S(1)}, bf16[8,3,32,256]{3,2,1,0:T(8,128)(2,1)S(1)}, u32[]{:S(2)}, u32[]{:S(2)}) collective-permute-start(bf16[8,3,32,256]{3,2,1,0:T(8,128)(2,1)S(1)} %pack.7.refs_0_), channel_id=1, source_target_pairs={{32,0},{64,32},{96,64},{128,96},{160,128},{192,160},{224,192},{256... | collective-permute-start | bytes 1179656 | tf_op jit(solution)/shard_map/ppermute | solution.py:184
  55.2 1.9 %collective-permute-start.5 = (bf16[8,3,32,256]{3,2,1,0:T(8,128)(2,1)S(1)}, bf16[8,3,32,256]{3,2,1,0:T(8,128)(2,1)S(1)}, u32[]{:S(2)}, u32[]{:S(2)}) collective-permute-start(bf16[8,3,32,256]{3,2,1,0:T(8,128)(2,1)S(1)} %pack.7.refs_0_), channel_id=1, source_target_pairs={{480,0},{0,32},{32,64},{64,96},{96,128},{128,160},{160,192},{192,2... | collective-permute-start | bytes 1179656 | tf_op jit(solution)/shard_map/ppermute | solution.py:184
  57.1 0.7 pack.9
  57.8 4.2 %collective-permute-start.6 = (bf16[4,3,32,256]{3,2,1,0:T(8,128)(2,1)}, bf16[4,3,32,256]{3,2,1,0:T(8,128)(2,1)}, u32[]{:S(2)}, u32[]{:S(2)}) collective-permute-start(bf16[4,3,32,256]{3,2,1,0:T(8,128)(2,1)} %pack.9), channel_id=1, source_target_pairs={{64,0},{96,32},{128,64},{160,96},{192,128},{224,160},{256,192},{28... | collective-permute-start | bytes 589832 | tf_op jit(solution)/shard_map/ppermute | solution.py:184
  62.1 0.7 pack.10
  62.7 1.9 %collective-permute-start.7 = (bf16[4,3,32,256]{3,2,1,0:T(8,128)(2,1)}, bf16[4,3,32,256]{3,2,1,0:T(8,128)(2,1)}, u32[]{:S(2)}, u32[]{:S(2)}) collective-permute-start(bf16[4,3,32,256]{3,2,1,0:T(8,128)(2,1)} %pack.10), channel_id=1, source_target_pairs={{448,0},{480,32},{0,64},{32,96},{64,128},{96,160},{128,192},{160,2... | collective-permute-start | bytes 589832 | tf_op jit(solution)/shard_map/ppermute | solution.py:184
  64.7 4.2 %all-to-all-done.1 = bf16[64,4,256]{2,1,0:T(4,128)(2,1)S(1)} async-done(((bf16[64,4,256]{2,1,0:T(4,128)(2,1)}), bf16[64,4,256]{2,1,0:T(4,128)(2,1)S(1)}, u32[]{:S(2)}, u32[]{:S(2)}) %all-to-all-start.1) | async-done | bytes 131104 | tf_op jit(solution)/shard_map/all_to_all | solution.py:201
  68.9 1.1 broadcast_in_dim.13
  70.0 4.8 %all-to-all-start.2 = ((bf16[8,256,256]{2,1,0:T(8,128)(2,1)}), bf16[8,256,256]{2,1,0:T(8,128)(2,1)S(1)}, u32[]{:S(2)}, u32[]{:S(2)}) async-start(bf16[8,256,256]{2,1,0:T(8,128)(2,1)} %broadcast_in_dim.13), calls=%async_computation.2 | async-start | bytes 2097152 | tf_op jit(solution)/shard_map/all_to_all | solution.py:206
  74.8 0.0 collective-permute-done.4.refs_1_
  74.8 0.0 copy-start.3
  74.8 0.1 pack.8.refs_0_
  74.9 2.6 %collective-permute-start.8 = (bf16[16,3,32,256]{3,2,1,0:T(8,128)(2,1)S(1)}, bf16[16,3,32,256]{3,2,1,0:T(8,128)(2,1)S(1)}, u32[]{:S(2)}, u32[]{:S(2)}) collective-permute-start(bf16[16,3,32,256]{3,2,1,0:T(8,128)(2,1)S(1)} %pack.8.refs_0_), channel_id=1, source_target_pairs={{0,8},{8,0},{1,9},{9,1},{2,10},{10,2},{3,11},{11,3},{4,12},{12,4},... | collective-permute-start | bytes 2359304 | tf_op jit(solution)/shard_map/ppermute | solution.py:208
  77.5 0.0 collective-permute-done.6.refs_1_
  77.5 0.0 collective-permute-done.7.refs_2_
  77.5 0.0 collective-permute-done.5.refs_0_
  77.5 0.8 copy-done
  78.3 1.0 copy-done.1
  79.3 1.1 pack.11.refs_1_
  80.4 1.9 %collective-permute-start.9 = (bf16[16,3,32,256]{3,2,1,0:T(8,128)(2,1)S(1)}, bf16[16,3,32,256]{3,2,1,0:T(8,128)(2,1)}, u32[]{:S(2)}, u32[]{:S(2)}) collective-permute-start(bf16[16,3,32,256]{3,2,1,0:T(8,128)(2,1)S(1)} %pack.11.refs_1_), channel_id=1, source_target_pairs={{0,8},{8,0},{1,9},{9,1},{2,10},{10,2},{3,11},{11,3},{4,12},{12,4},... | collective-permute-start | bytes 2359304 | tf_op jit(solution)/shard_map/ppermute | solution.py:208
  82.3 0.1 pad_add_fusion.where_ref
  82.4 0.0 collective-permute-done.8.refs_2_
  82.4 2.3 %collective-permute-done.9.refs_3_ = bf16[16,3,32,256]{3,2,1,0:T(8,128)(2,1)} collective-permute-done((bf16[16,3,32,256]{3,2,1,0:T(8,128)(2,1)S(1)}, bf16[16,3,32,256]{3,2,1,0:T(8,128)(2,1)}, u32[]{:S(2)}, u32[]{:S(2)}) %collective-permute-start.9) | collective-permute-done | bytes 786464 | tf_op jit(solution)/shard_map/ppermute | solution.py:208
  84.7 5.2 %all-to-all-done.2.x_ref = bf16[8,256,256]{2,1,0:T(8,128)(2,1)S(1)} async-done(((bf16[8,256,256]{2,1,0:T(8,128)(2,1)}), bf16[8,256,256]{2,1,0:T(8,128)(2,1)S(1)}, u32[]{:S(2)}, u32[]{:S(2)}) %all-to-all-start.2) | async-done | bytes 1048608 | tf_op jit(solution)/shard_map/all_to_all | solution.py:206
  89.9 3.3 %column_attention.1 = bf16[256,256]{1,0:T(8,128)(2,1)S(1)} custom-call(s32[3]{0:T(128)S(1)} %pad_add_fusion.where_ref, bf16[8,256,256]{2,1,0:T(8,128)(2,1)S(1)} %all-to-all-done.2.x_ref, f32[1,2048]{1,0:T(1,128)S(1)} %bitcast.22, bf16[16,3,32,256]{3,2,1,0:T(8,128)(2,1)S(1)} %pack.8.refs_0_, bf16[16,3,32,256]{3,2,1,0:T(8,128)(2,1)S(1)} %pack.11.refs_1_, ...), custom_call_target="tpu_custom_call" | custom-call | flops 805306368 | bytes 5242880 | tf_op jit(solution)/shard_map/column_attention/pallas_call | solution.py:166
  93.2 0.7 reshape.23
  93.9 11.5 %all-to-all-start.3 = ((bf16[64,4,256]{2,1,0:T(4,128)(2,1)}), bf16[64,4,256]{2,1,0:T(4,128)(2,1)S(1)}, u32[]{:S(2)}, u32[]{:S(2)}) async-start(bf16[64,4,256]{2,1,0:T(4,128)(2,1)} %reshape.23), calls=%async_computation.3 | async-start | bytes 262144 | tf_op jit(solution)/shard_map/all_to_all | solution.py:211
  105.5 1.7 %fusion.1 = bf16[1,256,256]{2,1,0:T(8,128)(2,1)} fusion(f32[256,256]{1,0:T(8,128)} %copy-done.4, bf16[1,256,256]{2,1,0:T(8,128)(2,1)} %param.7), kind=kLoop, calls=%fused_computation.4 | loop fusion | flops 196608 | bytes 524288 | tf_op jit(solution)/shard_map/convert_element_type | solution.py:200
  107.1 16.9 %all-to-all-done.3 = bf16[64,4,256]{2,1,0:T(4,128)(2,1)S(1)} async-done(((bf16[64,4,256]{2,1,0:T(4,128)(2,1)}), bf16[64,4,256]{2,1,0:T(4,128)(2,1)S(1)}, u32[]{:S(2)}, u32[]{:S(2)}) %all-to-all-start.3) | async-done | bytes 131104 | tf_op jit(solution)/shard_map/all_to_all | solution.py:211
  124.1 0.7 reshape.24
  (13 shorter events, 0.1 us)
Async XLA Ops:
  0.6 9.0 %collective-permute-start = (bf16[1,3,32,256]{3,2,1,0:T(8,128)(2,1)}, bf16[1,3,32,256]{3,2,1,0:T(8,128)(2,1)S(1)}, u32[]{:S(2)}, u32[]{:S(2)}) collective-permute-start(bf16[1,3,32,256]{3,2,1,0:T(8,128)(2,1)} %bitcast.20), channel_id=1, source_target_pairs={{0,16},{16,0},{1,17},{17,1},{2,18},{18,2},{3,19},{19,3},{4,20},{20... | collective-permute-start | bytes 147464 | tf_op jit(solution)/shard_map/ppermute | solution.py:194
  6.1 3.5 %copy-start.2 = (bf16[32,3,256]{2,0,1:T(8,128)(2,1)S(1)}, bf16[32,3,256]{2,0,1:T(8,128)(2,1)}, u32[]{:S(2)}) copy-start(bf16[32,3,256]{2,0,1:T(8,128)(2,1)} %param.13) | copy-start | bytes 147460
  10.2 4.4 %copy-start.5 = (bf16[1,256,256]{2,1,0:T(8,128)(2,1)S(1)}, bf16[1,256,256]{2,1,0:T(8,128)(2,1)}, u32[]{:S(2)}) copy-start(bf16[1,256,256]{2,1,0:T(8,128)(2,1)} %param.7) | copy-start | bytes 393220
  10.2 29.1 %all-to-all-start = ((bf16[8,256,256]{2,1,0:T(8,128)(2,1)}), bf16[8,256,256]{2,1,0:T(8,128)(2,1)S(1)}, u32[]{:S(2)}, u32[]{:S(2)}) async-start(bf16[8,256,256]{2,1,0:T(8,128)(2,1)} %touch.1), calls=%async_computation | async-start | bytes 2097152 | tf_op jit(solution)/shard_map/all_to_all | solution.py:197
  14.6 35.7 %collective-permute-start.1 = (bf16[2,3,32,256]{3,2,1,0:T(8,128)(2,1)S(1)}, bf16[2,3,32,256]{3,2,1,0:T(8,128)(2,1)S(1)}, u32[]{:S(2)}, u32[]{:S(2)}) collective-permute-start(bf16[2,3,32,256]{3,2,1,0:T(8,128)(2,1)S(1)} %pack.6.refs_0_), channel_id=1, source_target_pairs={{256,0},{288,32},{320,64},{352,96},{384,128},{416,160},{448,192},{... | collective-permute-start | bytes 294920 | tf_op jit(solution)/shard_map/ppermute | solution.py:184
  30.1 20.2 %collective-permute-start.2 = (bf16[2,3,32,256]{3,2,1,0:T(8,128)(2,1)S(1)}, bf16[2,3,32,256]{3,2,1,0:T(8,128)(2,1)S(1)}, u32[]{:S(2)}, u32[]{:S(2)}) collective-permute-start(bf16[2,3,32,256]{3,2,1,0:T(8,128)(2,1)S(1)} %pack.6.refs_0_), channel_id=1, source_target_pairs={{384,0},{416,32},{448,64},{480,96},{0,128},{32,160},{64,192},{96,2... | collective-permute-start | bytes 294920 | tf_op jit(solution)/shard_map/ppermute | solution.py:184
  34.1 16.2 %collective-permute-start.3 = (bf16[2,3,32,256]{3,2,1,0:T(8,128)(2,1)S(1)}, bf16[2,3,32,256]{3,2,1,0:T(8,128)(2,1)S(1)}, u32[]{:S(2)}, u32[]{:S(2)}) collective-permute-start(bf16[2,3,32,256]{3,2,1,0:T(8,128)(2,1)S(1)} %pack.6.refs_0_), channel_id=1, source_target_pairs={{128,0},{160,32},{192,64},{224,96},{256,128},{288,160},{320,192},{... | collective-permute-start | bytes 294920 | tf_op jit(solution)/shard_map/ppermute | solution.py:184
  39.5 10.9 %copy-start.4 = (f32[256,256]{1,0:T(8,128)}, f32[256,256]{1,0:T(8,128)S(1)}, u32[]{:S(2)}) copy-start(f32[256,256]{1,0:T(8,128)S(1)} %convert_reduce_fusion) | copy-start | bytes 786436
  40.3 28.6 %all-to-all-start.1 = ((bf16[64,4,256]{2,1,0:T(4,128)(2,1)}), bf16[64,4,256]{2,1,0:T(4,128)(2,1)S(1)}, u32[]{:S(2)}, u32[]{:S(2)}) async-start(bf16[64,4,256]{2,1,0:T(4,128)(2,1)} %add_convert_fusion), calls=%async_computation.1 | async-start | bytes 262144 | tf_op jit(solution)/shard_map/all_to_all | solution.py:201
  50.4 24.4 %collective-permute-start.4 = (bf16[8,3,32,256]{3,2,1,0:T(8,128)(2,1)S(1)}, bf16[8,3,32,256]{3,2,1,0:T(8,128)(2,1)S(1)}, u32[]{:S(2)}, u32[]{:S(2)}) collective-permute-start(bf16[8,3,32,256]{3,2,1,0:T(8,128)(2,1)S(1)} %pack.7.refs_0_), channel_id=1, source_target_pairs={{32,0},{64,32},{96,64},{128,96},{160,128},{192,160},{224,192},{256... | collective-permute-start | bytes 1179656 | tf_op jit(solution)/shard_map/ppermute | solution.py:184
  55.2 22.3 %collective-permute-start.5 = (bf16[8,3,32,256]{3,2,1,0:T(8,128)(2,1)S(1)}, bf16[8,3,32,256]{3,2,1,0:T(8,128)(2,1)S(1)}, u32[]{:S(2)}, u32[]{:S(2)}) collective-permute-start(bf16[8,3,32,256]{3,2,1,0:T(8,128)(2,1)S(1)} %pack.7.refs_0_), channel_id=1, source_target_pairs={{480,0},{0,32},{32,64},{64,96},{96,128},{128,160},{160,192},{192,2... | collective-permute-start | bytes 1179656 | tf_op jit(solution)/shard_map/ppermute | solution.py:184
  57.8 19.7 %collective-permute-start.6 = (bf16[4,3,32,256]{3,2,1,0:T(8,128)(2,1)}, bf16[4,3,32,256]{3,2,1,0:T(8,128)(2,1)}, u32[]{:S(2)}, u32[]{:S(2)}) collective-permute-start(bf16[4,3,32,256]{3,2,1,0:T(8,128)(2,1)} %pack.9), channel_id=1, source_target_pairs={{64,0},{96,32},{128,64},{160,96},{192,128},{224,160},{256,192},{28... | collective-permute-start | bytes 589832 | tf_op jit(solution)/shard_map/ppermute | solution.py:184
  62.7 14.8 %collective-permute-start.7 = (bf16[4,3,32,256]{3,2,1,0:T(8,128)(2,1)}, bf16[4,3,32,256]{3,2,1,0:T(8,128)(2,1)}, u32[]{:S(2)}, u32[]{:S(2)}) collective-permute-start(bf16[4,3,32,256]{3,2,1,0:T(8,128)(2,1)} %pack.10), channel_id=1, source_target_pairs={{448,0},{480,32},{0,64},{32,96},{64,128},{96,160},{128,192},{160,2... | collective-permute-start | bytes 589832 | tf_op jit(solution)/shard_map/ppermute | solution.py:184
  70.0 19.9 %all-to-all-start.2 = ((bf16[8,256,256]{2,1,0:T(8,128)(2,1)}), bf16[8,256,256]{2,1,0:T(8,128)(2,1)S(1)}, u32[]{:S(2)}, u32[]{:S(2)}) async-start(bf16[8,256,256]{2,1,0:T(8,128)(2,1)} %broadcast_in_dim.13), calls=%async_computation.2 | async-start | bytes 2097152 | tf_op jit(solution)/shard_map/all_to_all | solution.py:206
  74.8 15.1 %copy-start.3 = (f32[2048]{0:T(1024)S(1)}, f32[2048]{0:T(1024)}, u32[]{:S(2)}) copy-start(f32[2048]{0:T(1024)} %param.12) | copy-start | bytes 24580
  74.9 7.5 %collective-permute-start.8 = (bf16[16,3,32,256]{3,2,1,0:T(8,128)(2,1)S(1)}, bf16[16,3,32,256]{3,2,1,0:T(8,128)(2,1)S(1)}, u32[]{:S(2)}, u32[]{:S(2)}) collective-permute-start(bf16[16,3,32,256]{3,2,1,0:T(8,128)(2,1)S(1)} %pack.8.refs_0_), channel_id=1, source_target_pairs={{0,8},{8,0},{1,9},{9,1},{2,10},{10,2},{3,11},{11,3},{4,12},{12,4},... | collective-permute-start | bytes 2359304 | tf_op jit(solution)/shard_map/ppermute | solution.py:208
  77.5 0.8 copy-start
  78.3 1.0 copy-start.1
  80.4 4.3 %collective-permute-start.9 = (bf16[16,3,32,256]{3,2,1,0:T(8,128)(2,1)S(1)}, bf16[16,3,32,256]{3,2,1,0:T(8,128)(2,1)}, u32[]{:S(2)}, u32[]{:S(2)}) collective-permute-start(bf16[16,3,32,256]{3,2,1,0:T(8,128)(2,1)S(1)} %pack.11.refs_1_), channel_id=1, source_target_pairs={{0,8},{8,0},{1,9},{9,1},{2,10},{10,2},{3,11},{11,3},{4,12},{12,4},... | collective-permute-start | bytes 2359304 | tf_op jit(solution)/shard_map/ppermute | solution.py:208
  93.9 30.2 %all-to-all-start.3 = ((bf16[64,4,256]{2,1,0:T(4,128)(2,1)}), bf16[64,4,256]{2,1,0:T(4,128)(2,1)S(1)}, u32[]{:S(2)}, u32[]{:S(2)}) async-start(bf16[64,4,256]{2,1,0:T(4,128)(2,1)} %reshape.23), calls=%async_computation.3 | async-start | bytes 262144 | tf_op jit(solution)/shard_map/all_to_all | solution.py:211

commit v6 on v5

--- a/solution.py
+++ b/solution.py
@@ -65,8 +65,8 @@
     )(q, k, v, w)
 
 
-def pack_kernel(count, *refs):
-    pieces, out_ref = refs[:count], refs[-1]
+def pack_kernel(*refs):
+    pieces, out_ref = refs[:-1], refs[-1]
     at = 0
     for ref in pieces:
         for i in range(ref.shape[0]):
@@ -74,7 +74,7 @@
         at += ref.shape[0]
 
 
-def pack(*pieces, event=(), weight=0):
+def pack(*pieces, weight=0):
     total = sum(p.shape[0] for p in pieces)
     shape = (total,) + pieces[0].shape[1:]
     size = 4
@@ -82,14 +82,39 @@
         size *= d
     vm = pl.BlockSpec(memory_space=pltpu.VMEM)
     return pl.pallas_call(
-        functools.partial(pack_kernel, len(pieces)),
+        pack_kernel,
         out_shape=jax.ShapeDtypeStruct(shape, pieces[0].dtype),
-        in_specs=[vm] * (len(pieces) + len(event)),
+        in_specs=[vm] * len(pieces),
         out_specs=vm,
         compiler_params=pltpu.CompilerParams(vmem_limit_bytes=4 * 1024 * 1024),
         cost_estimate=pl.CostEstimate(flops=weight, bytes_accessed=size, transcendentals=0),
         name="pack",
-    )(*pieces, *event)
+    )(*pieces)
+
+
+def group_kernel(pair_ref, up8_ref, down4_ref, up4_ref, event_ref, eight_ref, first_ref, second_ref):
+    for i, ref in enumerate((pair_ref, up8_ref, down4_ref, up4_ref)):
+        for o in (0, 1):
+            eight_ref[2 * i + o] = ref[o]
+    for o in (0, 1):
+        first_ref[o] = pair_ref[o]
+        first_ref[2 + o] = up4_ref[o]
+        second_ref[o] = pair_ref[o]
+        second_ref[2 + o] = down4_ref[o]
+
+
+def group(pair, up8, down4, up4, event, weight):
+    vm = pl.BlockSpec(memory_space=pltpu.VMEM)
+    shape = pair.shape[1:]
+    return pl.pallas_call(
+        group_kernel,
+        out_shape=[jax.ShapeDtypeStruct((n,) + shape, pair.dtype) for n in (8, 4, 4)],
+        in_specs=[vm] * 5,
+        out_specs=[vm] * 3,
+        compiler_params=pltpu.CompilerParams(vmem_limit_bytes=4 * 1024 * 1024),
+        cost_estimate=pl.CostEstimate(flops=weight, bytes_accessed=16 * pair.size, transcendentals=0),
+        name="group",
+    )(pair, up8, down4, up4, event)
 
 
 FOUR = (0, 8, -4, 4)
@@ -101,23 +126,6 @@
     + [(2 + f, o) for f in (0, 4) for o in (0, 1)]
     + [(-2 + f, o) for f in (0, -4) for o in (0, 1)]
 )
-
-
-def touch_kernel(x_ref, event_ref, out_ref):
-    pass
-
-
-def touch(x, event):
-    anyspace = pl.BlockSpec(memory_space=pl.ANY)
-    return pl.pallas_call(
-        touch_kernel,
-        out_shape=jax.ShapeDtypeStruct(x.shape, x.dtype),
-        in_specs=[anyspace, anyspace],
-        out_specs=anyspace,
-        input_output_aliases={0: 0},
-        compiler_params=pltpu.CompilerParams(vmem_limit_bytes=VMEM_BYTES),
-        name="touch",
-    )(x, event)
 
 
 def column_kernel(count, where_ref, x_ref, gain_ref, *refs):
@@ -193,14 +201,13 @@
     w = jnp.transpose(qkv_weight, (1, 0, 2))[None]
     theirs = lax.ppermute(w, "xh", [(0, 1), (1, 0)])
     partial = row_part(row_query[0], row_key[0], row_value[0], out_weight, heads)
-    pair = pack(w, theirs)
-    parts = lax.all_to_all(touch(partial, pair[1, 0, :16, :128]), HD, 0, 0, tiled=True)
+    pair = pack(w, theirs, weight=10**10)
+    parts = lax.all_to_all(partial, HD, 0, 0, tiled=True)
     up8, down4, up4 = shift(pair, 8), shift(pair, -4), shift(pair, 4)
     stream = stream_in[0].astype(jnp.float32) + jnp.sum(parts.astype(jnp.float32), axis=0)
     stream_out = stream.astype(jnp.bfloat16)
     columns = lax.all_to_all(stream_out.reshape(seq, here, local), SEQ, 0, 0, tiled=True)
-    eight = pack(pair, up8, down4, up4, event=(stream_out,), weight=1000000000)
-    first, second = pack(pair, up4, event=(stream_out,)), pack(pair, down4, event=(stream_out,))
+    eight, first, second = group(pair, up8, down4, up4, stream_out, 10**9)
     up1, down1, up2, down2 = shift(eight, 1), shift(eight, -1), shift(first, 2), shift(second, -2)
     columns = columns.reshape(seq * here, local)
     x = lax.all_to_all(jnp.broadcast_to(columns[None], (heads,) + columns.shape), HD, 0, 0, tiled=True)

time: 126 us -> 123 us (0.976)
  starting transfers between devices: 78.2 us -> 76.9 us
    pallas_call x7 -> x4, Pallas kernels: 2.55 us -> 1.94 us  [the longest x3 1.13 us: pack(): pl.pallas_call(pack_kernel, out_shape=jax.ShapeDtypeStruct(shape, pieces[...]
  transfers between devices with their start and end apart: 14 -> 14, of which waited for: 4 -> 4; matrix products, arithmetic and copies ran while one was open for 3% -> 3% of each run, Pallas kernels for 5% -> 4%
where the time goes in v6:
time: 123 us
  starting transfers between devices  76.9 us (63%)
  waiting for transfers between devices  29.2 us (24%)
  Pallas kernels  8.69 us (7%)
  local copies, waits for them, and re-layouts  4.41 us (4%)
  other arithmetic  2.64 us (2%)
    ppermute x7, starting transfers between devices, shift(): return lax.ppermute(x, 'z', [((i + d) % 16, i) for i in range(16)])  37.5 us
    all_to_all x1, waiting for transfers between devices, on_device(): lax.all_to_all(mixed.reshape(seq, here, local), SEQ, 0, 0, tiled=True)  16.9 us
    all_to_all x1, starting transfers between devices, on_device(): lax.all_to_all(mixed.reshape(seq, here, local), SEQ, 0, 0, tiled=True)  10.9 us
    all_to_all x1, starting transfers between devices, on_device(): lax.all_to_all(stream_out.reshape(seq, here, local), SEQ, 0, 0, tiled=True)  9.1 us
    ppermute x1, starting transfers between devices, on_device(): theirs = lax.ppermute(w, 'xh', [(0, 1), (1, 0)])  5.48 us
    all_to_all x1, waiting for transfers between devices, on_device(): lax.all_to_all(jnp.broadcast_to(columns[None], (heads,) + columns.shape),...  5.26 us
    all_to_all x1, starting transfers between devices, on_device(): lax.all_to_all(jnp.broadcast_to(columns[None], (heads,) + columns.shape),...  4.81 us
    all_to_all x1, waiting for transfers between devices, on_device(): lax.all_to_all(stream_out.reshape(seq, here, local), SEQ, 0, 0, tiled=True)  4.81 us
  transfers between devices with their start and end apart: 14, of which 4 were waited for; matrix products, arithmetic and copies ran while one was open for 3% of the time, Pallas kernels for 4%

profile of v6, /device:TPU:1, one launch (start us, length us, event | category | flops | bytes accessed | tf_op | source)
XLA Modules:
  0.0 122.7 jit_solution(8061529551741386780)
XLA Ops:
  0.6 5.5 %collective-permute-start = (bf16[1,3,32,256]{3,2,1,0:T(8,128)(2,1)}, bf16[1,3,32,256]{3,2,1,0:T(8,128)(2,1)S(1)}, u32[]{:S(2)}, u32[]{:S(2)}) collective-permute-start(bf16[1,3,32,256]{3,2,1,0:T(8,128)(2,1)} %bitcast.19), channel_id=1, source_target_pairs={{0,16},{16,0},{1,17},{17,1},{2,18},{18,2},{3,19},{19,3},{4,20},{20... | collective-permute-start | bytes 147464 | tf_op jit(solution)/shard_map/ppermute | solution.py:202
  6.1 3.4 %row_attention.1 = bf16[8,256,256]{2,1,0:T(8,128)(2,1)} custom-call(bf16[256,256]{1,0:T(8,128)(2,1)} %bitcast.21, bf16[256,256]{1,0:T(8,128)(2,1)} %bitcast.22, bf16[256,256]{1,0:T(8,128)(2,1)} %bitcast.23, bf16[256,2048]{1,0:T(8,128)(2,1)} %w_hbm.1), custom_call_target="tpu_custom_call" | custom-call | flops 335544320 | bytes 3145728 | tf_op jit(solution)/shard_map/row_attention/pallas_call | solution.py:54
  9.6 0.0 copy-start.5
  9.6 0.0 copy-start.3
  9.6 4.4 %all-to-all-start = ((bf16[8,256,256]{2,1,0:T(8,128)(2,1)}), bf16[8,256,256]{2,1,0:T(8,128)(2,1)S(1)}, u32[]{:S(2)}, u32[]{:S(2)}) async-start(bf16[8,256,256]{2,1,0:T(8,128)(2,1)} %row_attention.1), calls=%async_computation | async-start | bytes 2097152 | tf_op jit(solution)/shard_map/all_to_all | solution.py:205
  14.0 0.1 reshape.25
  14.0 0.0 collective-permute-done.refs_1_
  14.1 15.4 %collective-permute-start.1 = (bf16[2,3,32,256]{3,2,1,0:T(8,128)(2,1)S(1)}, bf16[2,3,32,256]{3,2,1,0:T(8,128)(2,1)S(1)}, u32[]{:S(2)}, u32[]{:S(2)}) collective-permute-start(bf16[2,3,32,256]{3,2,1,0:T(8,128)(2,1)S(1)} %pack.3.pair_ref), channel_id=1, source_target_pairs={{256,0},{288,32},{320,64},{352,96},{384,128},{416,160},{448,192},{... | collective-permute-start | bytes 294920 | tf_op jit(solution)/shard_map/ppermute | solution.py:192
  29.5 4.0 %collective-permute-start.2 = (bf16[2,3,32,256]{3,2,1,0:T(8,128)(2,1)S(1)}, bf16[2,3,32,256]{3,2,1,0:T(8,128)(2,1)S(1)}, u32[]{:S(2)}, u32[]{:S(2)}) collective-permute-start(bf16[2,3,32,256]{3,2,1,0:T(8,128)(2,1)S(1)} %pack.3.pair_ref), channel_id=1, source_target_pairs={{384,0},{416,32},{448,64},{480,96},{0,128},{32,160},{64,192},{96,2... | collective-permute-start | bytes 294920 | tf_op jit(solution)/shard_map/ppermute | solution.py:192
  33.5 5.2 %collective-permute-start.3 = (bf16[2,3,32,256]{3,2,1,0:T(8,128)(2,1)S(1)}, bf16[2,3,32,256]{3,2,1,0:T(8,128)(2,1)S(1)}, u32[]{:S(2)}, u32[]{:S(2)}) collective-permute-start(bf16[2,3,32,256]{3,2,1,0:T(8,128)(2,1)S(1)} %pack.3.pair_ref), channel_id=1, source_target_pairs={{128,0},{160,32},{192,64},{224,96},{256,128},{288,160},{320,192},{... | collective-permute-start | bytes 294920 | tf_op jit(solution)/shard_map/ppermute | solution.py:192
  38.7 0.0 all-to-all-done
  38.7 0.1 convert_reduce_fusion
  38.9 0.1 reduce_sum.15
  39.0 0.7 add_convert_fusion
  39.7 9.1 %all-to-all-start.1 = ((bf16[64,4,256]{2,1,0:T(4,128)(2,1)}), bf16[64,4,256]{2,1,0:T(4,128)(2,1)S(1)}, u32[]{:S(2)}, u32[]{:S(2)}) async-start(bf16[64,4,256]{2,1,0:T(4,128)(2,1)} %add_convert_fusion), calls=%async_computation.1 | async-start | bytes 262144 | tf_op jit(solution)/shard_map/all_to_all | solution.py:209
  48.8 0.0 collective-permute-done.1.up8_ref
  48.9 0.0 collective-permute-done.2.down4_ref
  48.9 0.0 collective-permute-done.3.up4_ref
  48.9 0.8 group.1
  49.7 4.8 %collective-permute-start.4 = (bf16[8,3,32,256]{3,2,1,0:T(8,128)(2,1)S(1)}, bf16[8,3,32,256]{3,2,1,0:T(8,128)(2,1)S(1)}, u32[]{:S(2)}, u32[]{:S(2)}) collective-permute-start(bf16[8,3,32,256]{3,2,1,0:T(8,128)(2,1)S(1)} %get-tuple-element.5.refs_0_), channel_id=1, source_target_pairs={{32,0},{64,32},{96,64},{128,96},{160,128},{192,160},{224,192},{256... | collective-permute-start | bytes 1179656 | tf_op jit(solution)/shard_map/ppermute | solution.py:192
  54.5 1.9 %collective-permute-start.5 = (bf16[8,3,32,256]{3,2,1,0:T(8,128)(2,1)S(1)}, bf16[8,3,32,256]{3,2,1,0:T(8,128)(2,1)S(1)}, u32[]{:S(2)}, u32[]{:S(2)}) collective-permute-start(bf16[8,3,32,256]{3,2,1,0:T(8,128)(2,1)S(1)} %get-tuple-element.5.refs_0_), channel_id=1, source_target_pairs={{480,0},{0,32},{32,64},{64,96},{96,128},{128,160},{160,192},{192,2... | collective-permute-start | bytes 1179656 | tf_op jit(solution)/shard_map/ppermute | solution.py:192
  56.4 4.2 %collective-permute-start.6 = (bf16[4,3,32,256]{3,2,1,0:T(8,128)(2,1)}, bf16[4,3,32,256]{3,2,1,0:T(8,128)(2,1)}, u32[]{:S(2)}, u32[]{:S(2)}) collective-permute-start(bf16[4,3,32,256]{3,2,1,0:T(8,128)(2,1)} %get-tuple-element.6), channel_id=1, source_target_pairs={{64,0},{96,32},{128,64},{160,96},{192,128},{224,160},{256,192},{28... | collective-permute-start | bytes 589832 | tf_op jit(solution)/shard_map/ppermute | solution.py:192
  60.7 1.9 %collective-permute-start.7 = (bf16[4,3,32,256]{3,2,1,0:T(8,128)(2,1)}, bf16[4,3,32,256]{3,2,1,0:T(8,128)(2,1)}, u32[]{:S(2)}, u32[]{:S(2)}) collective-permute-start(bf16[4,3,32,256]{3,2,1,0:T(8,128)(2,1)} %get-tuple-element.7), channel_id=1, source_target_pairs={{448,0},{480,32},{0,64},{32,96},{64,128},{96,160},{128,192},{160,2... | collective-permute-start | bytes 589832 | tf_op jit(solution)/shard_map/ppermute | solution.py:192
  62.6 4.8 %all-to-all-done.1 = bf16[64,4,256]{2,1,0:T(4,128)(2,1)S(1)} async-done(((bf16[64,4,256]{2,1,0:T(4,128)(2,1)}), bf16[64,4,256]{2,1,0:T(4,128)(2,1)S(1)}, u32[]{:S(2)}, u32[]{:S(2)}) %all-to-all-start.1) | async-done | bytes 131104 | tf_op jit(solution)/shard_map/all_to_all | solution.py:209
  67.5 1.1 broadcast_in_dim.12
  68.5 4.8 %all-to-all-start.2 = ((bf16[8,256,256]{2,1,0:T(8,128)(2,1)}), bf16[8,256,256]{2,1,0:T(8,128)(2,1)S(1)}, u32[]{:S(2)}, u32[]{:S(2)}) async-start(bf16[8,256,256]{2,1,0:T(8,128)(2,1)} %broadcast_in_dim.12), calls=%async_computation.2 | async-start | bytes 2097152 | tf_op jit(solution)/shard_map/all_to_all | solution.py:213
  73.3 0.0 collective-permute-done.4.refs_1_
  73.3 0.0 copy-start.2
  73.4 0.1 pack.4.refs_0_
  73.4 2.6 %collective-permute-start.8 = (bf16[16,3,32,256]{3,2,1,0:T(8,128)(2,1)S(1)}, bf16[16,3,32,256]{3,2,1,0:T(8,128)(2,1)S(1)}, u32[]{:S(2)}, u32[]{:S(2)}) collective-permute-start(bf16[16,3,32,256]{3,2,1,0:T(8,128)(2,1)S(1)} %pack.4.refs_0_), channel_id=1, source_target_pairs={{0,8},{8,0},{1,9},{9,1},{2,10},{10,2},{3,11},{11,3},{4,12},{12,4},... | collective-permute-start | bytes 2359304 | tf_op jit(solution)/shard_map/ppermute | solution.py:215
  76.0 0.0 collective-permute-done.6.refs_1_
  76.0 0.0 collective-permute-done.7.refs_2_
  76.0 0.0 collective-permute-done.5.refs_0_
  76.1 0.8 copy-done
  76.8 1.0 copy-done.1
  77.8 1.1 pack.5.refs_1_
  78.9 2.1 %collective-permute-start.9 = (bf16[16,3,32,256]{3,2,1,0:T(8,128)(2,1)S(1)}, bf16[16,3,32,256]{3,2,1,0:T(8,128)(2,1)}, u32[]{:S(2)}, u32[]{:S(2)}) collective-permute-start(bf16[16,3,32,256]{3,2,1,0:T(8,128)(2,1)S(1)} %pack.5.refs_1_), channel_id=1, source_target_pairs={{0,8},{8,0},{1,9},{9,1},{2,10},{10,2},{3,11},{11,3},{4,12},{12,4},... | collective-permute-start | bytes 2359304 | tf_op jit(solution)/shard_map/ppermute | solution.py:215
  81.0 0.1 pad_add_fusion.where_ref
  81.1 0.0 collective-permute-done.8.refs_2_
  81.1 2.1 %collective-permute-done.9.refs_3_ = bf16[16,3,32,256]{3,2,1,0:T(8,128)(2,1)} collective-permute-done((bf16[16,3,32,256]{3,2,1,0:T(8,128)(2,1)S(1)}, bf16[16,3,32,256]{3,2,1,0:T(8,128)(2,1)}, u32[]{:S(2)}, u32[]{:S(2)}) %collective-permute-start.9) | collective-permute-done | bytes 786464 | tf_op jit(solution)/shard_map/ppermute | solution.py:215
  83.2 5.3 %all-to-all-done.2.x_ref = bf16[8,256,256]{2,1,0:T(8,128)(2,1)S(1)} async-done(((bf16[8,256,256]{2,1,0:T(8,128)(2,1)}), bf16[8,256,256]{2,1,0:T(8,128)(2,1)S(1)}, u32[]{:S(2)}, u32[]{:S(2)}) %all-to-all-start.2) | async-done | bytes 1048608 | tf_op jit(solution)/shard_map/all_to_all | solution.py:213
  88.5 0.0 copy-done.2
  88.5 3.3 %column_attention.1 = bf16[256,256]{1,0:T(8,128)(2,1)S(1)} custom-call(s32[3]{0:T(128)S(1)} %pad_add_fusion.where_ref, bf16[8,256,256]{2,1,0:T(8,128)(2,1)S(1)} %all-to-all-done.2.x_ref, f32[1,2048]{1,0:T(1,128)S(1)} %bitcast.18, bf16[16,3,32,256]{3,2,1,0:T(8,128)(2,1)S(1)} %pack.4.refs_0_, bf16[16,3,32,256]{3,2,1,0:T(8,128)(2,1)S(1)} %pack.5.refs_1_, ...), custom_call_target="tpu_custom_call" | custom-call | flops 805306368 | bytes 5242880 | tf_op jit(solution)/shard_map/column_attention/pallas_call | solution.py:174
  91.8 0.7 reshape.23
  92.5 10.9 %all-to-all-start.3 = ((bf16[64,4,256]{2,1,0:T(4,128)(2,1)}), bf16[64,4,256]{2,1,0:T(4,128)(2,1)S(1)}, u32[]{:S(2)}, u32[]{:S(2)}) async-start(bf16[64,4,256]{2,1,0:T(4,128)(2,1)} %reshape.23), calls=%async_computation.3 | async-start | bytes 262144 | tf_op jit(solution)/shard_map/all_to_all | solution.py:218
  103.4 1.7 %fusion.1 = bf16[1,256,256]{2,1,0:T(8,128)(2,1)} fusion(f32[256,256]{1,0:T(8,128)} %copy-done.4, bf16[1,256,256]{2,1,0:T(8,128)(2,1)} %param.7), kind=kLoop, calls=%fused_computation.4 | loop fusion | flops 196608 | bytes 524288 | tf_op jit(solution)/shard_map/convert_element_type | solution.py:208
  105.1 16.9 %all-to-all-done.3 = bf16[64,4,256]{2,1,0:T(4,128)(2,1)S(1)} async-done(((bf16[64,4,256]{2,1,0:T(4,128)(2,1)}), bf16[64,4,256]{2,1,0:T(4,128)(2,1)S(1)}, u32[]{:S(2)}, u32[]{:S(2)}) %all-to-all-start.3) | async-done | bytes 131104 | tf_op jit(solution)/shard_map/all_to_all | solution.py:218
  122.0 0.7 reshape.24
  (9 shorter events, 0.1 us)
Async XLA Ops:
  0.6 13.4 %collective-permute-start = (bf16[1,3,32,256]{3,2,1,0:T(8,128)(2,1)}, bf16[1,3,32,256]{3,2,1,0:T(8,128)(2,1)S(1)}, u32[]{:S(2)}, u32[]{:S(2)}) collective-permute-start(bf16[1,3,32,256]{3,2,1,0:T(8,128)(2,1)} %bitcast.19), channel_id=1, source_target_pairs={{0,16},{16,0},{1,17},{17,1},{2,18},{18,2},{3,19},{19,3},{4,20},{20... | collective-permute-start | bytes 147464 | tf_op jit(solution)/shard_map/ppermute | solution.py:202
  9.6 4.4 %copy-start.5 = (bf16[1,256,256]{2,1,0:T(8,128)(2,1)S(1)}, bf16[1,256,256]{2,1,0:T(8,128)(2,1)}, u32[]{:S(2)}) copy-start(bf16[1,256,256]{2,1,0:T(8,128)(2,1)} %param.7) | copy-start | bytes 393220
  9.6 4.5 %copy-start.3 = (bf16[32,3,256]{2,0,1:T(8,128)(2,1)S(1)}, bf16[32,3,256]{2,0,1:T(8,128)(2,1)}, u32[]{:S(2)}) copy-start(bf16[32,3,256]{2,0,1:T(8,128)(2,1)} %param.13) | copy-start | bytes 147460
  9.6 29.1 %all-to-all-start = ((bf16[8,256,256]{2,1,0:T(8,128)(2,1)}), bf16[8,256,256]{2,1,0:T(8,128)(2,1)S(1)}, u32[]{:S(2)}, u32[]{:S(2)}) async-start(bf16[8,256,256]{2,1,0:T(8,128)(2,1)} %row_attention.1), calls=%async_computation | async-start | bytes 2097152 | tf_op jit(solution)/shard_map/all_to_all | solution.py:205
  14.1 34.8 %collective-permute-start.1 = (bf16[2,3,32,256]{3,2,1,0:T(8,128)(2,1)S(1)}, bf16[2,3,32,256]{3,2,1,0:T(8,128)(2,1)S(1)}, u32[]{:S(2)}, u32[]{:S(2)}) collective-permute-start(bf16[2,3,32,256]{3,2,1,0:T(8,128)(2,1)S(1)} %pack.3.pair_ref), channel_id=1, source_target_pairs={{256,0},{288,32},{320,64},{352,96},{384,128},{416,160},{448,192},{... | collective-permute-start | bytes 294920 | tf_op jit(solution)/shard_map/ppermute | solution.py:192
  29.5 19.3 %collective-permute-start.2 = (bf16[2,3,32,256]{3,2,1,0:T(8,128)(2,1)S(1)}, bf16[2,3,32,256]{3,2,1,0:T(8,128)(2,1)S(1)}, u32[]{:S(2)}, u32[]{:S(2)}) collective-permute-start(bf16[2,3,32,256]{3,2,1,0:T(8,128)(2,1)S(1)} %pack.3.pair_ref), channel_id=1, source_target_pairs={{384,0},{416,32},{448,64},{480,96},{0,128},{32,160},{64,192},{96,2... | collective-permute-start | bytes 294920 | tf_op jit(solution)/shard_map/ppermute | solution.py:192
  33.5 15.3 %collective-permute-start.3 = (bf16[2,3,32,256]{3,2,1,0:T(8,128)(2,1)S(1)}, bf16[2,3,32,256]{3,2,1,0:T(8,128)(2,1)S(1)}, u32[]{:S(2)}, u32[]{:S(2)}) collective-permute-start(bf16[2,3,32,256]{3,2,1,0:T(8,128)(2,1)S(1)} %pack.3.pair_ref), channel_id=1, source_target_pairs={{128,0},{160,32},{192,64},{224,96},{256,128},{288,160},{320,192},{... | collective-permute-start | bytes 294920 | tf_op jit(solution)/shard_map/ppermute | solution.py:192
  38.9 10.8 %copy-start.4 = (f32[256,256]{1,0:T(8,128)}, f32[256,256]{1,0:T(8,128)S(1)}, u32[]{:S(2)}) copy-start(f32[256,256]{1,0:T(8,128)S(1)} %convert_reduce_fusion) | copy-start | bytes 786436
  39.7 27.7 %all-to-all-start.1 = ((bf16[64,4,256]{2,1,0:T(4,128)(2,1)}), bf16[64,4,256]{2,1,0:T(4,128)(2,1)S(1)}, u32[]{:S(2)}, u32[]{:S(2)}) async-start(bf16[64,4,256]{2,1,0:T(4,128)(2,1)} %add_convert_fusion), calls=%async_computation.1 | async-start | bytes 262144 | tf_op jit(solution)/shard_map/all_to_all | solution.py:209
  49.7 23.6 %collective-permute-start.4 = (bf16[8,3,32,256]{3,2,1,0:T(8,128)(2,1)S(1)}, bf16[8,3,32,256]{3,2,1,0:T(8,128)(2,1)S(1)}, u32[]{:S(2)}, u32[]{:S(2)}) collective-permute-start(bf16[8,3,32,256]{3,2,1,0:T(8,128)(2,1)S(1)} %get-tuple-element.5.refs_0_), channel_id=1, source_target_pairs={{32,0},{64,32},{96,64},{128,96},{160,128},{192,160},{224,192},{256... | collective-permute-start | bytes 1179656 | tf_op jit(solution)/shard_map/ppermute | solution.py:192
  54.5 21.6 %collective-permute-start.5 = (bf16[8,3,32,256]{3,2,1,0:T(8,128)(2,1)S(1)}, bf16[8,3,32,256]{3,2,1,0:T(8,128)(2,1)S(1)}, u32[]{:S(2)}, u32[]{:S(2)}) collective-permute-start(bf16[8,3,32,256]{3,2,1,0:T(8,128)(2,1)S(1)} %get-tuple-element.5.refs_0_), channel_id=1, source_target_pairs={{480,0},{0,32},{32,64},{64,96},{96,128},{128,160},{160,192},{192,2... | collective-permute-start | bytes 1179656 | tf_op jit(solution)/shard_map/ppermute | solution.py:192
  56.4 19.6 %collective-permute-start.6 = (bf16[4,3,32,256]{3,2,1,0:T(8,128)(2,1)}, bf16[4,3,32,256]{3,2,1,0:T(8,128)(2,1)}, u32[]{:S(2)}, u32[]{:S(2)}) collective-permute-start(bf16[4,3,32,256]{3,2,1,0:T(8,128)(2,1)} %get-tuple-element.6), channel_id=1, source_target_pairs={{64,0},{96,32},{128,64},{160,96},{192,128},{224,160},{256,192},{28... | collective-permute-start | bytes 589832 | tf_op jit(solution)/shard_map/ppermute | solution.py:192
  60.7 15.4 %collective-permute-start.7 = (bf16[4,3,32,256]{3,2,1,0:T(8,128)(2,1)}, bf16[4,3,32,256]{3,2,1,0:T(8,128)(2,1)}, u32[]{:S(2)}, u32[]{:S(2)}) collective-permute-start(bf16[4,3,32,256]{3,2,1,0:T(8,128)(2,1)} %get-tuple-element.7), channel_id=1, source_target_pairs={{448,0},{480,32},{0,64},{32,96},{64,128},{96,160},{128,192},{160,2... | collective-permute-start | bytes 589832 | tf_op jit(solution)/shard_map/ppermute | solution.py:192
  68.5 19.9 %all-to-all-start.2 = ((bf16[8,256,256]{2,1,0:T(8,128)(2,1)}), bf16[8,256,256]{2,1,0:T(8,128)(2,1)S(1)}, u32[]{:S(2)}, u32[]{:S(2)}) async-start(bf16[8,256,256]{2,1,0:T(8,128)(2,1)} %broadcast_in_dim.12), calls=%async_computation.2 | async-start | bytes 2097152 | tf_op jit(solution)/shard_map/all_to_all | solution.py:213
  73.3 15.1 %copy-start.2 = (f32[2048]{0:T(1024)S(1)}, f32[2048]{0:T(1024)}, u32[]{:S(2)}) copy-start(f32[2048]{0:T(1024)} %param.12) | copy-start | bytes 24580
  73.4 7.6 %collective-permute-start.8 = (bf16[16,3,32,256]{3,2,1,0:T(8,128)(2,1)S(1)}, bf16[16,3,32,256]{3,2,1,0:T(8,128)(2,1)S(1)}, u32[]{:S(2)}, u32[]{:S(2)}) collective-permute-start(bf16[16,3,32,256]{3,2,1,0:T(8,128)(2,1)S(1)} %pack.4.refs_0_), channel_id=1, source_target_pairs={{0,8},{8,0},{1,9},{9,1},{2,10},{10,2},{3,11},{11,3},{4,12},{12,4},... | collective-permute-start | bytes 2359304 | tf_op jit(solution)/shard_map/ppermute | solution.py:215
  76.1 0.8 copy-start
  76.8 1.0 copy-start.1
  78.9 4.3 %collective-permute-start.9 = (bf16[16,3,32,256]{3,2,1,0:T(8,128)(2,1)S(1)}, bf16[16,3,32,256]{3,2,1,0:T(8,128)(2,1)}, u32[]{:S(2)}, u32[]{:S(2)}) collective-permute-start(bf16[16,3,32,256]{3,2,1,0:T(8,128)(2,1)S(1)} %pack.5.refs_1_), channel_id=1, source_target_pairs={{0,8},{8,0},{1,9},{9,1},{2,10},{10,2},{3,11},{11,3},{4,12},{12,4},... | collective-permute-start | bytes 2359304 | tf_op jit(solution)/shard_map/ppermute | solution.py:215
  92.5 29.5 %all-to-all-start.3 = ((bf16[64,4,256]{2,1,0:T(4,128)(2,1)}), bf16[64,4,256]{2,1,0:T(4,128)(2,1)S(1)}, u32[]{:S(2)}, u32[]{:S(2)}) async-start(bf16[64,4,256]{2,1,0:T(4,128)(2,1)} %reshape.23), calls=%async_computation.3 | async-start | bytes 262144 | tf_op jit(solution)/shard_map/all_to_all | solution.py:218

commit v7 on v6

--- a/solution.py
+++ b/solution.py
@@ -23,7 +23,7 @@
     return jnp.dot(w, v, preferred_element_type=jnp.float32).astype(jnp.bfloat16)
 
 
-def row_kernel(q_hbm, k_hbm, v_hbm, w_hbm, out_ref, q_ref, k_ref, v_ref, w_ref, sems):
+def row_kernel(q_hbm, k_hbm, v_hbm, w_hbm, out_hbm, q_ref, k_ref, v_ref, w_ref, out_ref, sems, out_sems):
     copies = [
         pltpu.make_async_copy(src, dst, sems.at[i])
         for i, (src, dst) in enumerate(((q_hbm, q_ref), (k_hbm, k_ref), (v_hbm, v_ref), (w_hbm, w_ref)))
@@ -41,10 +41,15 @@
     mixed = jnp.concatenate(mixed, axis=1)
     copies[3].wait()
     width = out_ref.shape[2]
+    parts = []
     for part in range(out_ref.shape[0]):
         out_ref[part] = jnp.dot(
             mixed, w_ref[:, part * width : (part + 1) * width], preferred_element_type=jnp.float32
         ).astype(jnp.bfloat16)
+        parts.append(pltpu.make_async_copy(out_ref.at[part], out_hbm.at[part], out_sems.at[part]))
+        parts[-1].start()
+    for copy in parts:
+        copy.wait()
 
 
 def row_part(q, k, v, w, heads):
@@ -55,8 +60,16 @@
         row_kernel,
         out_shape=jax.ShapeDtypeStruct((heads, n, width), jnp.bfloat16),
         in_specs=[pl.BlockSpec(memory_space=pltpu.HBM)] * 4,
-        out_specs=pl.BlockSpec(memory_space=pltpu.VMEM),
-        scratch_shapes=[tile, tile, tile, pltpu.VMEM(w.shape, jnp.bfloat16), pltpu.SemaphoreType.DMA((4,))],
+        out_specs=pl.BlockSpec(memory_space=pltpu.HBM),
+        scratch_shapes=[
+            tile,
+            tile,
+            tile,
+            pltpu.VMEM(w.shape, jnp.bfloat16),
+            pltpu.VMEM((heads, n, width), jnp.bfloat16),
+            pltpu.SemaphoreType.DMA((4,)),
+            pltpu.SemaphoreType.DMA((heads,)),
+        ],
         compiler_params=pltpu.CompilerParams(vmem_limit_bytes=VMEM_BYTES),
         cost_estimate=pl.CostEstimate(
             flops=2 * n * local * (n * 2 + w.shape[1]), bytes_accessed=3 * 2**20, transcendentals=2 * n * n
@@ -129,18 +142,27 @@
 
 
 def column_kernel(count, where_ref, x_ref, gain_ref, *refs):
-    pieces, (out_ref, w_ref, normed_ref) = refs[: 2 * count], refs[2 * count :]
+    own, other = refs[:count], refs[count : 2 * count]
+    out_ref, w_ref, normed_ref, sems = refs[2 * count :]
     z, xh, core = where_ref[0], where_ref[1], where_ref[2]
-    for side in (0, 1):
-        c = core if side == 0 else 1 - core
-        slots = iter(SLOTS)
-        for ref in pieces[side * count : (side + 1) * count]:
-            for i in range(ref.shape[0]):
-                off, flip = next(slots)
-                zi = lax.rem(z + (off + 16), 16)
-                xi = 1 - xh if flip else xh
-                for j in range(3):
-                    w_ref[j, zi, xi, c] = ref[i, j]
+    places = [
+        (lax.rem(z + (off + 16), 16), 1 - xh if flip else xh) for off, flip in SLOTS
+    ]
+    copies = []
+    for ref in other:
+        for i in range(ref.shape[0]):
+            zi, xi = places[len(copies)]
+            copies.append(
+                pltpu.make_async_copy(ref.at[i], w_ref.at[:, zi, xi, 1 - core], sems.at[len(copies)])
+            )
+            copies[-1].start()
+    at = 0
+    for ref in own:
+        for i in range(ref.shape[0]):
+            zi, xi = places[at]
+            at += 1
+            for j in range(3):
+                w_ref[j, zi, xi, core] = ref[i, j]
     heads, n, local = x_ref.shape
     total = jnp.zeros((n, 1), jnp.float32)
     for h in range(heads):
@@ -150,6 +172,8 @@
     for h in range(heads):
         cols = slice(h * local, (h + 1) * local)
         normed_ref[:, cols] = (x_ref[h].astype(jnp.float32) * scale * gain_ref[:, cols]).astype(jnp.bfloat16)
+    for copy in copies:
+        copy.wait()
     parts = []
     for j in range(3):
         w = w_ref[j].reshape(heads * local, local)
@@ -174,11 +198,12 @@
     return pl.pallas_call(
         functools.partial(column_kernel, count),
         out_shape=jax.ShapeDtypeStruct((n, local), jnp.bfloat16),
-        in_specs=[pl.BlockSpec(memory_space=pltpu.SMEM)] + [vm] * (2 + 2 * count),
+        in_specs=[pl.BlockSpec(memory_space=pltpu.SMEM)] + [vm] * (2 + count) + [pl.BlockSpec(memory_space=pl.ANY)] * count,
         out_specs=vm,
         scratch_shapes=[
             pltpu.VMEM((3, 16, 2, 2, rows, local), jnp.bfloat16),
             pltpu.VMEM((n, heads * local), jnp.bfloat16),
+            pltpu.SemaphoreType.DMA((len(SLOTS),)),
         ],
         compiler_params=pltpu.CompilerParams(vmem_limit_bytes=20 * 1024 * 1024),
         cost_estimate=pl.CostEstimate(

time: 123 us -> 124 us (level)
  no operation moved by 1% of the time
where the time goes in v7:
time: 124 us; the launch traced here: 123 us
  starting transfers between devices  76.9 us (62%)
  waiting for transfers between devices  29.2 us (24%)
  Pallas kernels  9.35 us (8%)
  local copies, waits for them, and re-layouts  4.4 us (4%)
  other arithmetic  2.64 us (2%)
    ppermute x7, starting transfers between devices, shift(): return lax.ppermute(x, 'z', [((i + d) % 16, i) for i in range(16)])  37.5 us
    all_to_all x1, waiting for transfers between devices, on_device(): lax.all_to_all(mixed.reshape(seq, here, local), SEQ, 0, 0, tiled=True)  16.9 us
    all_to_all x1, starting transfers between devices, on_device(): lax.all_to_all(mixed.reshape(seq, here, local), SEQ, 0, 0, tiled=True)  10.9 us
    all_to_all x1, starting transfers between devices, on_device(): lax.all_to_all(stream_out.reshape(seq, here, local), SEQ, 0, 0, tiled=True)  9.1 us
    ppermute x1, starting transfers between devices, on_device(): theirs = lax.ppermute(w, 'xh', [(0, 1), (1, 0)])  5.48 us
    all_to_all x1, waiting for transfers between devices, on_device(): lax.all_to_all(jnp.broadcast_to(columns[None], (heads,) + columns.shape),...  5.26 us
    all_to_all x1, starting transfers between devices, on_device(): lax.all_to_all(jnp.broadcast_to(columns[None], (heads,) + columns.shape),...  4.81 us
    all_to_all x1, waiting for transfers between devices, on_device(): lax.all_to_all(stream_out.reshape(seq, here, local), SEQ, 0, 0, tiled=True)  4.81 us
  transfers between devices with their start and end apart: 14, of which 4 were waited for; matrix products, arithmetic and copies ran while one was open for 3% of the time, Pallas kernels for 4%

profile of v7, /device:TPU:1, one launch (start us, length us, event | category | flops | bytes accessed | tf_op | source)
XLA Modules:
  0.0 123.4 jit_solution(8922599662615110451)
XLA Ops:
  0.6 5.5 %collective-permute-start = (bf16[1,3,32,256]{3,2,1,0:T(8,128)(2,1)}, bf16[1,3,32,256]{3,2,1,0:T(8,128)(2,1)S(1)}, u32[]{:S(2)}, u32[]{:S(2)}) collective-permute-start(bf16[1,3,32,256]{3,2,1,0:T(8,128)(2,1)} %bitcast.19), channel_id=1, source_target_pairs={{0,16},{16,0},{1,17},{17,1},{2,18},{18,2},{3,19},{19,3},{4,20},{20... | collective-permute-start | bytes 147464 | tf_op jit(solution)/shard_map/ppermute | solution.py:227
  6.1 3.3 %row_attention.1 = bf16[8,256,256]{2,1,0:T(8,128)(2,1)} custom-call(bf16[256,256]{1,0:T(8,128)(2,1)} %bitcast.21, bf16[256,256]{1,0:T(8,128)(2,1)} %bitcast.22, bf16[256,256]{1,0:T(8,128)(2,1)} %bitcast.23, bf16[256,2048]{1,0:T(8,128)(2,1)} %w_hbm.1), custom_call_target="tpu_custom_call" | custom-call | flops 335544320 | bytes 3145728 | tf_op jit(solution)/shard_map/row_attention/pallas_call | solution.py:59
  9.4 0.0 copy-start.5
  9.4 0.0 copy-start.3
  9.5 4.4 %all-to-all-start = ((bf16[8,256,256]{2,1,0:T(8,128)(2,1)}), bf16[8,256,256]{2,1,0:T(8,128)(2,1)S(1)}, u32[]{:S(2)}, u32[]{:S(2)}) async-start(bf16[8,256,256]{2,1,0:T(8,128)(2,1)} %row_attention.1), calls=%async_computation | async-start | bytes 2097152 | tf_op jit(solution)/shard_map/all_to_all | solution.py:230
  13.8 0.0 copy-done.5
  13.8 0.1 reshape.25
  13.9 0.0 collective-permute-done.refs_1_
  13.9 15.4 %collective-permute-start.1 = (bf16[2,3,32,256]{3,2,1,0:T(8,128)(2,1)S(1)}, bf16[2,3,32,256]{3,2,1,0:T(8,128)(2,1)S(1)}, u32[]{:S(2)}, u32[]{:S(2)}) collective-permute-start(bf16[2,3,32,256]{3,2,1,0:T(8,128)(2,1)S(1)} %pack.3.pair_ref), channel_id=1, source_target_pairs={{256,0},{288,32},{320,64},{352,96},{384,128},{416,160},{448,192},{... | collective-permute-start | bytes 294920 | tf_op jit(solution)/shard_map/ppermute | solution.py:217
  29.4 4.0 %collective-permute-start.2 = (bf16[2,3,32,256]{3,2,1,0:T(8,128)(2,1)S(1)}, bf16[2,3,32,256]{3,2,1,0:T(8,128)(2,1)S(1)}, u32[]{:S(2)}, u32[]{:S(2)}) collective-permute-start(bf16[2,3,32,256]{3,2,1,0:T(8,128)(2,1)S(1)} %pack.3.pair_ref), channel_id=1, source_target_pairs={{384,0},{416,32},{448,64},{480,96},{0,128},{32,160},{64,192},{96,2... | collective-permute-start | bytes 294920 | tf_op jit(solution)/shard_map/ppermute | solution.py:217
  33.4 5.2 %collective-permute-start.3 = (bf16[2,3,32,256]{3,2,1,0:T(8,128)(2,1)S(1)}, bf16[2,3,32,256]{3,2,1,0:T(8,128)(2,1)S(1)}, u32[]{:S(2)}, u32[]{:S(2)}) collective-permute-start(bf16[2,3,32,256]{3,2,1,0:T(8,128)(2,1)S(1)} %pack.3.pair_ref), channel_id=1, source_target_pairs={{128,0},{160,32},{192,64},{224,96},{256,128},{288,160},{320,192},{... | collective-permute-start | bytes 294920 | tf_op jit(solution)/shard_map/ppermute | solution.py:217
  38.6 0.0 all-to-all-done
  38.6 0.1 convert_reduce_fusion
  38.8 0.1 reduce_sum.15
  38.8 0.7 add_convert_fusion
  39.6 9.1 %all-to-all-start.1 = ((bf16[64,4,256]{2,1,0:T(4,128)(2,1)}), bf16[64,4,256]{2,1,0:T(4,128)(2,1)S(1)}, u32[]{:S(2)}, u32[]{:S(2)}) async-start(bf16[64,4,256]{2,1,0:T(4,128)(2,1)} %add_convert_fusion), calls=%async_computation.1 | async-start | bytes 262144 | tf_op jit(solution)/shard_map/all_to_all | solution.py:234
  48.7 0.0 collective-permute-done.1.up8_ref
  48.7 0.0 collective-permute-done.2.down4_ref
  48.7 0.0 collective-permute-done.3.up4_ref
  48.7 0.8 group.1
  49.5 4.8 %collective-permute-start.4 = (bf16[8,3,32,256]{3,2,1,0:T(8,128)(2,1)S(1)}, bf16[8,3,32,256]{3,2,1,0:T(8,128)(2,1)S(1)}, u32[]{:S(2)}, u32[]{:S(2)}) collective-permute-start(bf16[8,3,32,256]{3,2,1,0:T(8,128)(2,1)S(1)} %get-tuple-element.5.refs_0_), channel_id=1, source_target_pairs={{32,0},{64,32},{96,64},{128,96},{160,128},{192,160},{224,192},{256... | collective-permute-start | bytes 1179656 | tf_op jit(solution)/shard_map/ppermute | solution.py:217
  54.3 1.9 %collective-permute-start.5 = (bf16[8,3,32,256]{3,2,1,0:T(8,128)(2,1)S(1)}, bf16[8,3,32,256]{3,2,1,0:T(8,128)(2,1)S(1)}, u32[]{:S(2)}, u32[]{:S(2)}) collective-permute-start(bf16[8,3,32,256]{3,2,1,0:T(8,128)(2,1)S(1)} %get-tuple-element.5.refs_0_), channel_id=1, source_target_pairs={{480,0},{0,32},{32,64},{64,96},{96,128},{128,160},{160,192},{192,2... | collective-permute-start | bytes 1179656 | tf_op jit(solution)/shard_map/ppermute | solution.py:217
  56.3 4.2 %collective-permute-start.6 = (bf16[4,3,32,256]{3,2,1,0:T(8,128)(2,1)}, bf16[4,3,32,256]{3,2,1,0:T(8,128)(2,1)}, u32[]{:S(2)}, u32[]{:S(2)}) collective-permute-start(bf16[4,3,32,256]{3,2,1,0:T(8,128)(2,1)} %get-tuple-element.6), channel_id=1, source_target_pairs={{64,0},{96,32},{128,64},{160,96},{192,128},{224,160},{256,192},{28... | collective-permute-start | bytes 589832 | tf_op jit(solution)/shard_map/ppermute | solution.py:217
  60.5 1.9 %collective-permute-start.7 = (bf16[4,3,32,256]{3,2,1,0:T(8,128)(2,1)}, bf16[4,3,32,256]{3,2,1,0:T(8,128)(2,1)}, u32[]{:S(2)}, u32[]{:S(2)}) collective-permute-start(bf16[4,3,32,256]{3,2,1,0:T(8,128)(2,1)} %get-tuple-element.7), channel_id=1, source_target_pairs={{448,0},{480,32},{0,64},{32,96},{64,128},{96,160},{128,192},{160,2... | collective-permute-start | bytes 589832 | tf_op jit(solution)/shard_map/ppermute | solution.py:217
  62.5 4.8 %all-to-all-done.1 = bf16[64,4,256]{2,1,0:T(4,128)(2,1)S(1)} async-done(((bf16[64,4,256]{2,1,0:T(4,128)(2,1)}), bf16[64,4,256]{2,1,0:T(4,128)(2,1)S(1)}, u32[]{:S(2)}, u32[]{:S(2)}) %all-to-all-start.1) | async-done | bytes 131104 | tf_op jit(solution)/shard_map/all_to_all | solution.py:234
  67.3 1.1 broadcast_in_dim.12
  68.4 4.8 %all-to-all-start.2 = ((bf16[8,256,256]{2,1,0:T(8,128)(2,1)}), bf16[8,256,256]{2,1,0:T(8,128)(2,1)S(1)}, u32[]{:S(2)}, u32[]{:S(2)}) async-start(bf16[8,256,256]{2,1,0:T(8,128)(2,1)} %broadcast_in_dim.12), calls=%async_computation.2 | async-start | bytes 2097152 | tf_op jit(solution)/shard_map/all_to_all | solution.py:238
  73.2 0.0 collective-permute-done.4.refs_1_
  73.2 0.0 copy-start.2
  73.2 0.1 pack.4.refs_0_
  73.3 2.6 %collective-permute-start.8 = (bf16[16,3,32,256]{3,2,1,0:T(8,128)(2,1)S(1)}, bf16[16,3,32,256]{3,2,1,0:T(8,128)(2,1)S(1)}, u32[]{:S(2)}, u32[]{:S(2)}) collective-permute-start(bf16[16,3,32,256]{3,2,1,0:T(8,128)(2,1)S(1)} %pack.4.refs_0_), channel_id=1, source_target_pairs={{0,8},{8,0},{1,9},{9,1},{2,10},{10,2},{3,11},{11,3},{4,12},{12,4},... | collective-permute-start | bytes 2359304 | tf_op jit(solution)/shard_map/ppermute | solution.py:240
  75.9 0.0 collective-permute-done.6.refs_1_
  75.9 0.0 collective-permute-done.7.refs_2_
  75.9 0.0 collective-permute-done.5.refs_0_
  75.9 0.8 copy-done
  76.7 1.0 copy-done.1
  77.7 1.1 pack.5.refs_1_
  78.8 2.1 %collective-permute-start.9 = (bf16[16,3,32,256]{3,2,1,0:T(8,128)(2,1)S(1)}, bf16[16,3,32,256]{3,2,1,0:T(8,128)(2,1)}, u32[]{:S(2)}, u32[]{:S(2)}) collective-permute-start(bf16[16,3,32,256]{3,2,1,0:T(8,128)(2,1)S(1)} %pack.5.refs_1_), channel_id=1, source_target_pairs={{0,8},{8,0},{1,9},{9,1},{2,10},{10,2},{3,11},{11,3},{4,12},{12,4},... | collective-permute-start | bytes 2359304 | tf_op jit(solution)/shard_map/ppermute | solution.py:240
  80.8 0.1 pad_add_fusion.where_ref
  80.9 0.0 collective-permute-done.8.refs_2_
  80.9 2.1 %collective-permute-done.9.refs_3_ = bf16[16,3,32,256]{3,2,1,0:T(8,128)(2,1)} collective-permute-done((bf16[16,3,32,256]{3,2,1,0:T(8,128)(2,1)S(1)}, bf16[16,3,32,256]{3,2,1,0:T(8,128)(2,1)}, u32[]{:S(2)}, u32[]{:S(2)}) %collective-permute-start.9) | collective-permute-done | bytes 786464 | tf_op jit(solution)/shard_map/ppermute | solution.py:240
  83.1 5.3 %all-to-all-done.2.x_ref = bf16[8,256,256]{2,1,0:T(8,128)(2,1)S(1)} async-done(((bf16[8,256,256]{2,1,0:T(8,128)(2,1)}), bf16[8,256,256]{2,1,0:T(8,128)(2,1)S(1)}, u32[]{:S(2)}, u32[]{:S(2)}) %all-to-all-start.2) | async-done | bytes 1048608 | tf_op jit(solution)/shard_map/all_to_all | solution.py:238
  88.3 4.1 %column_attention.1 = bf16[256,256]{1,0:T(8,128)(2,1)S(1)} custom-call(s32[3]{0:T(128)S(1)} %pad_add_fusion.where_ref, bf16[8,256,256]{2,1,0:T(8,128)(2,1)S(1)} %all-to-all-done.2.x_ref, f32[1,2048]{1,0:T(1,128)S(1)} %bitcast.18, bf16[16,3,32,256]{3,2,1,0:T(8,128)(2,1)S(1)} %pack.4.refs_0_, bf16[16,3,32,256]{3,2,1,0:T(8,128)(2,1)S(1)} %pack.5.refs_1_, ...), custom_call_target="tpu_custom_call" | custom-call | flops 805306368 | bytes 5242880 | tf_op jit(solution)/shard_map/column_attention/pallas_call | solution.py:198
  92.4 0.7 reshape.23
  93.1 10.9 %all-to-all-start.3 = ((bf16[64,4,256]{2,1,0:T(4,128)(2,1)}), bf16[64,4,256]{2,1,0:T(4,128)(2,1)S(1)}, u32[]{:S(2)}, u32[]{:S(2)}) async-start(bf16[64,4,256]{2,1,0:T(4,128)(2,1)} %reshape.23), calls=%async_computation.3 | async-start | bytes 262144 | tf_op jit(solution)/shard_map/all_to_all | solution.py:243
  104.1 1.7 %fusion.1 = bf16[1,256,256]{2,1,0:T(8,128)(2,1)} fusion(f32[256,256]{1,0:T(8,128)} %copy-done.4, bf16[1,256,256]{2,1,0:T(8,128)(2,1)} %param.7), kind=kLoop, calls=%fused_computation.4 | loop fusion | flops 196608 | bytes 524288 | tf_op jit(solution)/shard_map/convert_element_type | solution.py:233
  105.7 16.9 %all-to-all-done.3 = bf16[64,4,256]{2,1,0:T(4,128)(2,1)S(1)} async-done(((bf16[64,4,256]{2,1,0:T(4,128)(2,1)}), bf16[64,4,256]{2,1,0:T(4,128)(2,1)S(1)}, u32[]{:S(2)}, u32[]{:S(2)}) %all-to-all-start.3) | async-done | bytes 131104 | tf_op jit(solution)/shard_map/all_to_all | solution.py:243
  122.7 0.7 reshape.24
  (9 shorter events, 0.1 us)
Async XLA Ops:
  0.6 13.3 %collective-permute-start = (bf16[1,3,32,256]{3,2,1,0:T(8,128)(2,1)}, bf16[1,3,32,256]{3,2,1,0:T(8,128)(2,1)S(1)}, u32[]{:S(2)}, u32[]{:S(2)}) collective-permute-start(bf16[1,3,32,256]{3,2,1,0:T(8,128)(2,1)} %bitcast.19), channel_id=1, source_target_pairs={{0,16},{16,0},{1,17},{17,1},{2,18},{18,2},{3,19},{19,3},{4,20},{20... | collective-permute-start | bytes 147464 | tf_op jit(solution)/shard_map/ppermute | solution.py:227
  9.4 4.4 %copy-start.5 = (bf16[1,256,256]{2,1,0:T(8,128)(2,1)S(1)}, bf16[1,256,256]{2,1,0:T(8,128)(2,1)}, u32[]{:S(2)}) copy-start(bf16[1,256,256]{2,1,0:T(8,128)(2,1)} %param.7) | copy-start | bytes 393220
  9.4 4.5 %copy-start.3 = (bf16[32,3,256]{2,0,1:T(8,128)(2,1)S(1)}, bf16[32,3,256]{2,0,1:T(8,128)(2,1)}, u32[]{:S(2)}) copy-start(bf16[32,3,256]{2,0,1:T(8,128)(2,1)} %param.13) | copy-start | bytes 147460
  9.5 29.1 %all-to-all-start = ((bf16[8,256,256]{2,1,0:T(8,128)(2,1)}), bf16[8,256,256]{2,1,0:T(8,128)(2,1)S(1)}, u32[]{:S(2)}, u32[]{:S(2)}) async-start(bf16[8,256,256]{2,1,0:T(8,128)(2,1)} %row_attention.1), calls=%async_computation | async-start | bytes 2097152 | tf_op jit(solution)/shard_map/all_to_all | solution.py:230
  13.9 34.8 %collective-permute-start.1 = (bf16[2,3,32,256]{3,2,1,0:T(8,128)(2,1)S(1)}, bf16[2,3,32,256]{3,2,1,0:T(8,128)(2,1)S(1)}, u32[]{:S(2)}, u32[]{:S(2)}) collective-permute-start(bf16[2,3,32,256]{3,2,1,0:T(8,128)(2,1)S(1)} %pack.3.pair_ref), channel_id=1, source_target_pairs={{256,0},{288,32},{320,64},{352,96},{384,128},{416,160},{448,192},{... | collective-permute-start | bytes 294920 | tf_op jit(solution)/shard_map/ppermute | solution.py:217
  29.4 19.3 %collective-permute-start.2 = (bf16[2,3,32,256]{3,2,1,0:T(8,128)(2,1)S(1)}, bf16[2,3,32,256]{3,2,1,0:T(8,128)(2,1)S(1)}, u32[]{:S(2)}, u32[]{:S(2)}) collective-permute-start(bf16[2,3,32,256]{3,2,1,0:T(8,128)(2,1)S(1)} %pack.3.pair_ref), channel_id=1, source_target_pairs={{384,0},{416,32},{448,64},{480,96},{0,128},{32,160},{64,192},{96,2... | collective-permute-start | bytes 294920 | tf_op jit(solution)/shard_map/ppermute | solution.py:217
  33.4 15.3 %collective-permute-start.3 = (bf16[2,3,32,256]{3,2,1,0:T(8,128)(2,1)S(1)}, bf16[2,3,32,256]{3,2,1,0:T(8,128)(2,1)S(1)}, u32[]{:S(2)}, u32[]{:S(2)}) collective-permute-start(bf16[2,3,32,256]{3,2,1,0:T(8,128)(2,1)S(1)} %pack.3.pair_ref), channel_id=1, source_target_pairs={{128,0},{160,32},{192,64},{224,96},{256,128},{288,160},{320,192},{... | collective-permute-start | bytes 294920 | tf_op jit(solution)/shard_map/ppermute | solution.py:217
  38.7 10.8 %copy-start.4 = (f32[256,256]{1,0:T(8,128)}, f32[256,256]{1,0:T(8,128)S(1)}, u32[]{:S(2)}) copy-start(f32[256,256]{1,0:T(8,128)S(1)} %convert_reduce_fusion) | copy-start | bytes 786436
  39.6 27.7 %all-to-all-start.1 = ((bf16[64,4,256]{2,1,0:T(4,128)(2,1)}), bf16[64,4,256]{2,1,0:T(4,128)(2,1)S(1)}, u32[]{:S(2)}, u32[]{:S(2)}) async-start(bf16[64,4,256]{2,1,0:T(4,128)(2,1)} %add_convert_fusion), calls=%async_computation.1 | async-start | bytes 262144 | tf_op jit(solution)/shard_map/all_to_all | solution.py:234
  49.5 23.6 %collective-permute-start.4 = (bf16[8,3,32,256]{3,2,1,0:T(8,128)(2,1)S(1)}, bf16[8,3,32,256]{3,2,1,0:T(8,128)(2,1)S(1)}, u32[]{:S(2)}, u32[]{:S(2)}) collective-permute-start(bf16[8,3,32,256]{3,2,1,0:T(8,128)(2,1)S(1)} %get-tuple-element.5.refs_0_), channel_id=1, source_target_pairs={{32,0},{64,32},{96,64},{128,96},{160,128},{192,160},{224,192},{256... | collective-permute-start | bytes 1179656 | tf_op jit(solution)/shard_map/ppermute | solution.py:217
  54.3 21.6 %collective-permute-start.5 = (bf16[8,3,32,256]{3,2,1,0:T(8,128)(2,1)S(1)}, bf16[8,3,32,256]{3,2,1,0:T(8,128)(2,1)S(1)}, u32[]{:S(2)}, u32[]{:S(2)}) collective-permute-start(bf16[8,3,32,256]{3,2,1,0:T(8,128)(2,1)S(1)} %get-tuple-element.5.refs_0_), channel_id=1, source_target_pairs={{480,0},{0,32},{32,64},{64,96},{96,128},{128,160},{160,192},{192,2... | collective-permute-start | bytes 1179656 | tf_op jit(solution)/shard_map/ppermute | solution.py:217
  56.3 19.6 %collective-permute-start.6 = (bf16[4,3,32,256]{3,2,1,0:T(8,128)(2,1)}, bf16[4,3,32,256]{3,2,1,0:T(8,128)(2,1)}, u32[]{:S(2)}, u32[]{:S(2)}) collective-permute-start(bf16[4,3,32,256]{3,2,1,0:T(8,128)(2,1)} %get-tuple-element.6), channel_id=1, source_target_pairs={{64,0},{96,32},{128,64},{160,96},{192,128},{224,160},{256,192},{28... | collective-permute-start | bytes 589832 | tf_op jit(solution)/shard_map/ppermute | solution.py:217
  60.5 15.4 %collective-permute-start.7 = (bf16[4,3,32,256]{3,2,1,0:T(8,128)(2,1)}, bf16[4,3,32,256]{3,2,1,0:T(8,128)(2,1)}, u32[]{:S(2)}, u32[]{:S(2)}) collective-permute-start(bf16[4,3,32,256]{3,2,1,0:T(8,128)(2,1)} %get-tuple-element.7), channel_id=1, source_target_pairs={{448,0},{480,32},{0,64},{32,96},{64,128},{96,160},{128,192},{160,2... | collective-permute-start | bytes 589832 | tf_op jit(solution)/shard_map/ppermute | solution.py:217
  68.4 19.9 %all-to-all-start.2 = ((bf16[8,256,256]{2,1,0:T(8,128)(2,1)}), bf16[8,256,256]{2,1,0:T(8,128)(2,1)S(1)}, u32[]{:S(2)}, u32[]{:S(2)}) async-start(bf16[8,256,256]{2,1,0:T(8,128)(2,1)} %broadcast_in_dim.12), calls=%async_computation.2 | async-start | bytes 2097152 | tf_op jit(solution)/shard_map/all_to_all | solution.py:238
  73.2 15.1 %copy-start.2 = (f32[2048]{0:T(1024)S(1)}, f32[2048]{0:T(1024)}, u32[]{:S(2)}) copy-start(f32[2048]{0:T(1024)} %param.12) | copy-start | bytes 24580
  73.3 7.6 %collective-permute-start.8 = (bf16[16,3,32,256]{3,2,1,0:T(8,128)(2,1)S(1)}, bf16[16,3,32,256]{3,2,1,0:T(8,128)(2,1)S(1)}, u32[]{:S(2)}, u32[]{:S(2)}) collective-permute-start(bf16[16,3,32,256]{3,2,1,0:T(8,128)(2,1)S(1)} %pack.4.refs_0_), channel_id=1, source_target_pairs={{0,8},{8,0},{1,9},{9,1},{2,10},{10,2},{3,11},{11,3},{4,12},{12,4},... | collective-permute-start | bytes 2359304 | tf_op jit(solution)/shard_map/ppermute | solution.py:240
  75.9 0.8 copy-start
  76.7 1.0 copy-start.1
  78.8 4.3 %collective-permute-start.9 = (bf16[16,3,32,256]{3,2,1,0:T(8,128)(2,1)S(1)}, bf16[16,3,32,256]{3,2,1,0:T(8,128)(2,1)}, u32[]{:S(2)}, u32[]{:S(2)}) collective-permute-start(bf16[16,3,32,256]{3,2,1,0:T(8,128)(2,1)S(1)} %pack.5.refs_1_), channel_id=1, source_target_pairs={{0,8},{8,0},{1,9},{9,1},{2,10},{10,2},{3,11},{11,3},{4,12},{12,4},... | collective-permute-start | bytes 2359304 | tf_op jit(solution)/shard_map/ppermute | solution.py:240
  93.1 29.5 %all-to-all-start.3 = ((bf16[64,4,256]{2,1,0:T(4,128)(2,1)}), bf16[64,4,256]{2,1,0:T(4,128)(2,1)S(1)}, u32[]{:S(2)}, u32[]{:S(2)}) async-start(bf16[64,4,256]{2,1,0:T(4,128)(2,1)} %reshape.23), calls=%async_computation.3 | async-start | bytes 262144 | tf_op jit(solution)/shard_map/all_to_all | solution.py:243

commit v8 on v6

--- a/solution.py
+++ b/solution.py
@@ -13,6 +13,7 @@
 VMEM_BYTES = 60 * 1024 * 1024
 SEQ = ("z", "xh", "c")
 HD = ("y", "xl")
+TURN = 32
 
 
 def softmax_mix(q, k, v, mask):
@@ -20,10 +21,10 @@
     s = jnp.where(mask, s * (HEAD ** -0.5), NEG)
     p = jnp.exp(s - jnp.max(s, axis=-1, keepdims=True))
     w = (p / jnp.sum(p, axis=-1, keepdims=True)).astype(jnp.bfloat16)
-    return jnp.dot(w, v, preferred_element_type=jnp.float32).astype(jnp.bfloat16)
-
-
-def row_kernel(q_hbm, k_hbm, v_hbm, w_hbm, out_ref, q_ref, k_ref, v_ref, w_ref, sems):
+    return jnp.dot(w, v, preferred_element_type=jnp.float32)
+
+
+def row_kernel(q_hbm, k_hbm, v_hbm, w_hbm, out_hbm, q_ref, k_ref, v_ref, w_ref, out_ref, sems, out_sems):
     copies = [
         pltpu.make_async_copy(src, dst, sems.at[i])
         for i, (src, dst) in enumerate(((q_hbm, q_ref), (k_hbm, k_ref), (v_hbm, v_ref), (w_hbm, w_ref)))
@@ -37,14 +38,19 @@
     mixed = []
     for h in range(q_ref.shape[1] // HEAD):
         cols = slice(h * HEAD, (h + 1) * HEAD)
-        mixed.append(softmax_mix(q_ref[:, cols], k_ref[:, cols], v_ref[:, cols], mask))
+        mixed.append(softmax_mix(q_ref[:, cols], k_ref[:, cols], v_ref[:, cols], mask).astype(jnp.bfloat16))
     mixed = jnp.concatenate(mixed, axis=1)
     copies[3].wait()
     width = out_ref.shape[2]
+    parts = []
     for part in range(out_ref.shape[0]):
         out_ref[part] = jnp.dot(
             mixed, w_ref[:, part * width : (part + 1) * width], preferred_element_type=jnp.float32
         ).astype(jnp.bfloat16)
+        parts.append(pltpu.make_async_copy(out_ref.at[part], out_hbm.at[part], out_sems.at[part]))
+        parts[-1].start()
+    for copy in parts:
+        copy.wait()
 
 
 def row_part(q, k, v, w, heads):
@@ -55,8 +61,16 @@
         row_kernel,
         out_shape=jax.ShapeDtypeStruct((heads, n, width), jnp.bfloat16),
         in_specs=[pl.BlockSpec(memory_space=pltpu.HBM)] * 4,
-        out_specs=pl.BlockSpec(memory_space=pltpu.VMEM),
-        scratch_shapes=[tile, tile, tile, pltpu.VMEM(w.shape, jnp.bfloat16), pltpu.SemaphoreType.DMA((4,))],
+        out_specs=pl.BlockSpec(memory_space=pltpu.HBM),
+        scratch_shapes=[
+            tile,
+            tile,
+            tile,
+            pltpu.VMEM(w.shape, jnp.bfloat16),
+            pltpu.VMEM((heads, n, width), jnp.bfloat16),
+            pltpu.SemaphoreType.DMA((4,)),
+            pltpu.SemaphoreType.DMA((heads,)),
+        ],
         compiler_params=pltpu.CompilerParams(vmem_limit_bytes=VMEM_BYTES),
         cost_estimate=pl.CostEstimate(
             flops=2 * n * local * (n * 2 + w.shape[1]), bytes_accessed=3 * 2**20, transcendentals=2 * n * n
@@ -161,9 +175,15 @@
     t1 = lax.broadcasted_iota(jnp.int32, (n, n), 1)
     cols_here = 4
     mask = (t0 >= t1) & ((t0 & (cols_here - 1)) == (t1 & (cols_here - 1)))
+    mixed = []
     for h in range(local // HEAD):
         cols = slice(h * HEAD, (h + 1) * HEAD)
-        out_ref[:, cols] = softmax_mix(q[:, cols], k[:, cols], v[:, cols], mask)
+        one = softmax_mix(q[:, cols], k[:, cols], v[:, cols], mask)
+        mixed.append(one.reshape(n // cols_here, cols_here, HEAD))
+    mixed = jnp.concatenate(mixed, axis=1).astype(jnp.bfloat16)
+    rows = mixed.shape[0]
+    out_ref[: rows - TURN] = mixed[TURN:]
+    out_ref[rows - TURN :] = mixed[:TURN]
 
 
 def column_part(where, x, gain, own, other):
@@ -173,7 +193,7 @@
     vm = pl.BlockSpec(memory_space=pltpu.VMEM)
     return pl.pallas_call(
         functools.partial(column_kernel, count),
-        out_shape=jax.ShapeDtypeStruct((n, local), jnp.bfloat16),
+        out_shape=jax.ShapeDtypeStruct((n // 4, 4 * local // HEAD, HEAD), jnp.bfloat16),
         in_specs=[pl.BlockSpec(memory_space=pltpu.SMEM)] + [vm] * (2 + 2 * count),
         out_specs=vm,
         scratch_shapes=[
@@ -211,11 +231,14 @@
     up1, down1, up2, down2 = shift(eight, 1), shift(eight, -1), shift(first, 2), shift(second, -2)
     columns = columns.reshape(seq * here, local)
     x = lax.all_to_all(jnp.broadcast_to(columns[None], (heads,) + columns.shape), HD, 0, 0, tiled=True)
-    own = (pack(eight, up1), pack(down1, up2, down2))
+    own = (pack(eight, up1), pack(down1, weight=3000000000), pack(up2, down2, weight=1000000000))
     other = [lax.ppermute(piece, "c", [(0, 1), (1, 0)]) for piece in own]
     where = jnp.stack([lax.axis_index("z"), lax.axis_index("xh"), lax.axis_index("c")]).astype(jnp.int32)
     mixed = column_part(where, x, norm_gain.reshape(1, -1), own, other)
-    back = lax.all_to_all(mixed.reshape(seq, here, local), SEQ, 0, 0, tiled=True)
+    turned = [[(i + TURN) % seq for i in range(seq)]]
+    back = lax.all_to_all(mixed, SEQ, 0, 0, tiled=True, axis_index_groups=turned)
+    back = jnp.concatenate([back[seq - TURN :], back[: seq - TURN]], axis=0)
+    back = back.reshape(seq, local // HEAD, here, HEAD).transpose(0, 2, 1, 3)
     return (stream_out[None], back.reshape(1, steps, local))
 
 

time: 123 us -> 117 us (0.951)
  waiting for transfers between devices: 29.2 us -> 17.5 us
  starting transfers between devices: 76.9 us -> 82.3 us
  local copies, waits for them, and re-layouts: 4.41 us -> 2.12 us
  Pallas kernels: 8.69 us -> 10.9 us
    all_to_all x1, waiting for transfers between devices: 16.9 us -> 7.5 us  [on_device(): lax.all_to_all(mixed, SEQ, 0, 0, tiled=True, axis_index_groups=turned)]
    all_to_all x1, starting transfers between devices: 10.9 us -> 14.1 us  [on_device(): lax.all_to_all(mixed, SEQ, 0, 0, tiled=True, axis_index_groups=turned)]
    ppermute x2 -> x3, starting transfers between devices: 4.67 us -> 6.91 us  [on_device(): other = [lax.ppermute(piece, 'c', [(0, 1), (1, 0)]) for piece in own]]
    unnamed x12 -> x8, local copies, waits for them, and re-layouts: 1.78 us -> 0.02 us
    pallas_call x3 -> x4, Pallas kernels: 1.13 us -> 2.87 us  [pack(): pl.pallas_call(pack_kernel, out_shape=jax.ShapeDtypeStruct(shape, pieces[...]
    all_to_all x1, waiting for transfers between devices: 5.26 us -> 3.61 us  [on_device(): lax.all_to_all(jnp.broadcast_to(columns[None], (heads,) + columns.shape),...]
  transfers between devices with their start and end apart: 14 -> 15, of which waited for: 4 -> 4; matrix products, arithmetic and copies ran while one was open for 3% -> 3% of each run, Pallas kernels for 4% -> 6%
where the time goes in v8:
time: 117 us; the launch traced here: 116 us
  starting transfers between devices  82.3 us (70%)
  waiting for transfers between devices  17.5 us (15%)
  Pallas kernels  10.9 us (9%)
  other arithmetic  2.63 us (2%)
  local copies, waits for them, and re-layouts  2.12 us (2%)
    ppermute x7, starting transfers between devices, shift(): return lax.ppermute(x, 'z', [((i + d) % 16, i) for i in range(16)])  37.5 us
    all_to_all x1, starting transfers between devices, on_device(): lax.all_to_all(mixed, SEQ, 0, 0, tiled=True, axis_index_groups=turned)  14.1 us
    all_to_all x1, starting transfers between devices, on_device(): lax.all_to_all(stream_out.reshape(seq, here, local), SEQ, 0, 0, tiled=True)  9.1 us
    all_to_all x1, waiting for transfers between devices, on_device(): lax.all_to_all(mixed, SEQ, 0, 0, tiled=True, axis_index_groups=turned)  7.5 us
    ppermute x3, starting transfers between devices, on_device(): other = [lax.ppermute(piece, 'c', [(0, 1), (1, 0)]) for piece in own]  6.91 us
    ppermute x1, starting transfers between devices, on_device(): theirs = lax.ppermute(w, 'xh', [(0, 1), (1, 0)])  5.48 us
    all_to_all x1, starting transfers between devices, on_device(): lax.all_to_all(jnp.broadcast_to(columns[None], (heads,) + columns.shape),...  4.81 us
    all_to_all x1, waiting for transfers between devices, on_device(): lax.all_to_all(stream_out.reshape(seq, here, local), SEQ, 0, 0, tiled=True)  4.8 us
  transfers between devices with their start and end apart: 15, of which 4 were waited for; matrix products, arithmetic and copies ran while one was open for 3% of the time, Pallas kernels for 6%

profile of v8, /device:TPU:1, one launch (start us, length us, event | category | flops | bytes accessed | tf_op | source)
XLA Modules:
  0.0 116.4 jit_solution(12192030774414553528)
XLA Ops:
  0.6 5.5 %collective-permute-start = (bf16[1,3,32,256]{3,2,1,0:T(8,128)(2,1)}, bf16[1,3,32,256]{3,2,1,0:T(8,128)(2,1)S(1)}, u32[]{:S(2)}, u32[]{:S(2)}) collective-permute-start(bf16[1,3,32,256]{3,2,1,0:T(8,128)(2,1)} %bitcast.22), channel_id=1, source_target_pairs={{0,16},{16,0},{1,17},{17,1},{2,18},{18,2},{3,19},{19,3},{4,20},{20... | collective-permute-start | bytes 147464 | tf_op jit(solution)/shard_map/ppermute | solution.py:222
  6.1 3.3 %row_attention.1 = bf16[8,256,256]{2,1,0:T(8,128)(2,1)} custom-call(bf16[256,256]{1,0:T(8,128)(2,1)} %bitcast.25, bf16[256,256]{1,0:T(8,128)(2,1)} %bitcast.26, bf16[256,256]{1,0:T(8,128)(2,1)} %bitcast.27, bf16[256,2048]{1,0:T(8,128)(2,1)} %w_hbm.1), custom_call_target="tpu_custom_call" | custom-call | flops 335544320 | bytes 3145728 | tf_op jit(solution)/shard_map/row_attention/pallas_call | solution.py:60
  9.4 0.0 copy-start.3
  9.4 0.0 copy-start.1
  9.5 4.4 %all-to-all-start = ((bf16[8,256,256]{2,1,0:T(8,128)(2,1)}), bf16[8,256,256]{2,1,0:T(8,128)(2,1)S(1)}, u32[]{:S(2)}, u32[]{:S(2)}) async-start(bf16[8,256,256]{2,1,0:T(8,128)(2,1)} %row_attention.1), calls=%async_computation | async-start | bytes 2097152 | tf_op jit(solution)/shard_map/all_to_all | solution.py:225
  13.8 0.1 reshape.25
  13.9 0.0 collective-permute-done.refs_1_
  13.9 15.4 %collective-permute-start.1 = (bf16[2,3,32,256]{3,2,1,0:T(8,128)(2,1)S(1)}, bf16[2,3,32,256]{3,2,1,0:T(8,128)(2,1)S(1)}, u32[]{:S(2)}, u32[]{:S(2)}) collective-permute-start(bf16[2,3,32,256]{3,2,1,0:T(8,128)(2,1)S(1)} %pack.4.pair_ref), channel_id=1, source_target_pairs={{256,0},{288,32},{320,64},{352,96},{384,128},{416,160},{448,192},{... | collective-permute-start | bytes 294920 | tf_op jit(solution)/shard_map/ppermute | solution.py:212
  29.4 4.0 %collective-permute-start.2 = (bf16[2,3,32,256]{3,2,1,0:T(8,128)(2,1)S(1)}, bf16[2,3,32,256]{3,2,1,0:T(8,128)(2,1)S(1)}, u32[]{:S(2)}, u32[]{:S(2)}) collective-permute-start(bf16[2,3,32,256]{3,2,1,0:T(8,128)(2,1)S(1)} %pack.4.pair_ref), channel_id=1, source_target_pairs={{384,0},{416,32},{448,64},{480,96},{0,128},{32,160},{64,192},{96,2... | collective-permute-start | bytes 294920 | tf_op jit(solution)/shard_map/ppermute | solution.py:212
  33.4 5.2 %collective-permute-start.3 = (bf16[2,3,32,256]{3,2,1,0:T(8,128)(2,1)S(1)}, bf16[2,3,32,256]{3,2,1,0:T(8,128)(2,1)S(1)}, u32[]{:S(2)}, u32[]{:S(2)}) collective-permute-start(bf16[2,3,32,256]{3,2,1,0:T(8,128)(2,1)S(1)} %pack.4.pair_ref), channel_id=1, source_target_pairs={{128,0},{160,32},{192,64},{224,96},{256,128},{288,160},{320,192},{... | collective-permute-start | bytes 294920 | tf_op jit(solution)/shard_map/ppermute | solution.py:212
  38.6 0.0 all-to-all-done
  38.6 0.1 convert_reduce_fusion
  38.7 0.0 copy-start.2
  38.8 0.1 reduce_sum.15
  38.8 0.7 add_convert_fusion
  39.6 9.1 %all-to-all-start.1 = ((bf16[64,4,256]{2,1,0:T(4,128)(2,1)}), bf16[64,4,256]{2,1,0:T(4,128)(2,1)S(1)}, u32[]{:S(2)}, u32[]{:S(2)}) async-start(bf16[64,4,256]{2,1,0:T(4,128)(2,1)} %add_convert_fusion), calls=%async_computation.1 | async-start | bytes 262144 | tf_op jit(solution)/shard_map/all_to_all | solution.py:229
  48.7 0.0 collective-permute-done.1.up8_ref
  48.7 0.0 collective-permute-done.2.down4_ref
  48.7 0.0 collective-permute-done.3.up4_ref
  48.7 0.8 group.1
  49.6 4.8 %collective-permute-start.4 = (bf16[8,3,32,256]{3,2,1,0:T(8,128)(2,1)}, bf16[8,3,32,256]{3,2,1,0:T(8,128)(2,1)S(1)}, u32[]{:S(2)}, u32[]{:S(2)}) collective-permute-start(bf16[8,3,32,256]{3,2,1,0:T(8,128)(2,1)} %get-tuple-element.5.refs_0_), channel_id=1, source_target_pairs={{32,0},{64,32},{96,64},{128,96},{160,128},{192,160},{224,192},{256... | collective-permute-start | bytes 1179656 | tf_op jit(solution)/shard_map/ppermute | solution.py:212
  54.4 1.9 %collective-permute-start.5 = (bf16[8,3,32,256]{3,2,1,0:T(8,128)(2,1)}, bf16[8,3,32,256]{3,2,1,0:T(8,128)(2,1)}, u32[]{:S(2)}, u32[]{:S(2)}) collective-permute-start(bf16[8,3,32,256]{3,2,1,0:T(8,128)(2,1)} %get-tuple-element.5.refs_0_), channel_id=1, source_target_pairs={{480,0},{0,32},{32,64},{64,96},{96,128},{128,160},{160,192},{192,2... | collective-permute-start | bytes 1179656 | tf_op jit(solution)/shard_map/ppermute | solution.py:212
  56.3 4.2 %collective-permute-start.6 = (bf16[4,3,32,256]{3,2,1,0:T(8,128)(2,1)S(1)}, bf16[4,3,32,256]{3,2,1,0:T(8,128)(2,1)S(1)}, u32[]{:S(2)}, u32[]{:S(2)}) collective-permute-start(bf16[4,3,32,256]{3,2,1,0:T(8,128)(2,1)S(1)} %get-tuple-element.6), channel_id=1, source_target_pairs={{64,0},{96,32},{128,64},{160,96},{192,128},{224,160},{256,192},{28... | collective-permute-start | bytes 589832 | tf_op jit(solution)/shard_map/ppermute | solution.py:212
  60.5 1.9 %collective-permute-start.7 = (bf16[4,3,32,256]{3,2,1,0:T(8,128)(2,1)S(1)}, bf16[4,3,32,256]{3,2,1,0:T(8,128)(2,1)S(1)}, u32[]{:S(2)}, u32[]{:S(2)}) collective-permute-start(bf16[4,3,32,256]{3,2,1,0:T(8,128)(2,1)S(1)} %get-tuple-element.7), channel_id=1, source_target_pairs={{448,0},{480,32},{0,64},{32,96},{64,128},{96,160},{128,192},{160,2... | collective-permute-start | bytes 589832 | tf_op jit(solution)/shard_map/ppermute | solution.py:212
  62.5 4.8 %all-to-all-done.1 = bf16[64,4,256]{2,1,0:T(4,128)(2,1)S(1)} async-done(((bf16[64,4,256]{2,1,0:T(4,128)(2,1)}), bf16[64,4,256]{2,1,0:T(4,128)(2,1)S(1)}, u32[]{:S(2)}, u32[]{:S(2)}) %all-to-all-start.1) | async-done | bytes 131104 | tf_op jit(solution)/shard_map/all_to_all | solution.py:229
  67.3 1.1 broadcast_in_dim.12
  68.4 4.8 %all-to-all-start.2 = ((bf16[8,256,256]{2,1,0:T(8,128)(2,1)}), bf16[8,256,256]{2,1,0:T(8,128)(2,1)S(1)}, u32[]{:S(2)}, u32[]{:S(2)}) async-start(bf16[8,256,256]{2,1,0:T(8,128)(2,1)} %broadcast_in_dim.12), calls=%async_computation.2 | async-start | bytes 2097152 | tf_op jit(solution)/shard_map/all_to_all | solution.py:233
  73.2 0.0 collective-permute-done.4.refs_1_
  73.2 1.0 pack.5.refs_0_
  74.3 2.6 %collective-permute-start.8 = (bf16[16,3,32,256]{3,2,1,0:T(8,128)(2,1)S(1)}, bf16[16,3,32,256]{3,2,1,0:T(8,128)(2,1)S(1)}, u32[]{:S(2)}, u32[]{:S(2)}) collective-permute-start(bf16[16,3,32,256]{3,2,1,0:T(8,128)(2,1)S(1)} %pack.5.refs_0_), channel_id=1, source_target_pairs={{0,8},{8,0},{1,9},{9,1},{2,10},{10,2},{3,11},{11,3},{4,12},{12,4},... | collective-permute-start | bytes 2359304 | tf_op jit(solution)/shard_map/ppermute | solution.py:235
  76.9 0.0 collective-permute-done.6.refs_0_
  76.9 0.0 collective-permute-done.7.refs_1_
  76.9 0.0 copy-start
  76.9 1.9 %collective-permute-start.10 = (bf16[8,3,32,256]{3,2,1,0:T(8,128)(2,1)S(1)}, bf16[8,3,32,256]{3,2,1,0:T(8,128)(2,1)S(1)}, u32[]{:S(2)}, u32[]{:S(2)}) collective-permute-start(bf16[8,3,32,256]{3,2,1,0:T(8,128)(2,1)S(1)} %pack.7.refs_2_), channel_id=1, source_target_pairs={{0,8},{8,0},{1,9},{9,1},{2,10},{10,2},{3,11},{11,3},{4,12},{12,4},... | collective-permute-start | bytes 1179656 | tf_op jit(solution)/shard_map/ppermute | solution.py:235
  78.9 0.0 collective-permute-done.5.refs_0_
  78.9 1.8 %pack.6.refs_1_ = bf16[8,3,32,256]{3,2,1,0:T(8,128)(2,1)} custom-call(bf16[8,3,32,256]{3,2,1,0:T(8,128)(2,1)} %collective-permute-done.5.refs_0_), custom_call_target="tpu_custom_call" | custom-call | flops 3000000000 | bytes 786432 | tf_op jit(solution)/shard_map/pack/pallas_call | solution.py:98
  80.7 2.4 %collective-permute-start.9 = (bf16[8,3,32,256]{3,2,1,0:T(8,128)(2,1)}, bf16[8,3,32,256]{3,2,1,0:T(8,128)(2,1)}, u32[]{:S(2)}, u32[]{:S(2)}) collective-permute-start(bf16[8,3,32,256]{3,2,1,0:T(8,128)(2,1)} %pack.6.refs_1_), channel_id=1, source_target_pairs={{0,8},{8,0},{1,9},{9,1},{2,10},{10,2},{3,11},{11,3},{4,12},{12,4},... | collective-permute-start | bytes 1179656 | tf_op jit(solution)/shard_map/ppermute | solution.py:235
  83.1 0.1 pad_add_fusion.where_ref
  83.1 0.0 collective-permute-done.10.refs_5_
  83.1 1.6 %collective-permute-done.9.refs_4_ = bf16[8,3,32,256]{3,2,1,0:T(8,128)(2,1)} collective-permute-done((bf16[8,3,32,256]{3,2,1,0:T(8,128)(2,1)}, bf16[8,3,32,256]{3,2,1,0:T(8,128)(2,1)}, u32[]{:S(2)}, u32[]{:S(2)}) %collective-permute-start.9) | collective-permute-done | bytes 393248 | tf_op jit(solution)/shard_map/ppermute | solution.py:235
  84.7 0.0 collective-permute-done.8.refs_3_
  84.7 3.6 %all-to-all-done.2.x_ref = bf16[8,256,256]{2,1,0:T(8,128)(2,1)S(1)} async-done(((bf16[8,256,256]{2,1,0:T(8,128)(2,1)}), bf16[8,256,256]{2,1,0:T(8,128)(2,1)S(1)}, u32[]{:S(2)}, u32[]{:S(2)}) %all-to-all-start.2) | async-done | bytes 1048608 | tf_op jit(solution)/shard_map/all_to_all | solution.py:233
  88.3 3.9 %column_attention.1 = bf16[64,8,128]{2,1,0:T(8,128)(2,1)} custom-call(s32[3]{0:T(128)S(1)} %pad_add_fusion.where_ref, bf16[8,256,256]{2,1,0:T(8,128)(2,1)S(1)} %all-to-all-done.2.x_ref, f32[1,2048]{1,0:T(1,128)S(1)} %bitcast.21, bf16[16,3,32,256]{3,2,1,0:T(8,128)(2,1)S(1)} %pack.5.refs_0_, bf16[8,3,32,256]{3,2,1,0:T(8,128)(2,1)} %pack.6.refs_1_, ...), custom_call_target="tpu_custom_call" | custom-call | flops 805306368 | bytes 5242880 | tf_op jit(solution)/shard_map/column_attention/pallas_call | solution.py:194
  92.3 14.1 %all-to-all-start.3 = ((bf16[64,8,128]{2,1,0:T(8,128)(2,1)}), bf16[64,8,128]{2,1,0:T(8,128)(2,1)S(1)}, u32[]{:S(2)}, u32[]{:S(2)}) async-start(bf16[64,8,128]{2,1,0:T(8,128)(2,1)} %column_attention.1), calls=%async_computation.3 | async-start | bytes 262144 | tf_op jit(solution)/shard_map/all_to_all | solution.py:239
  106.4 1.6 %fusion.1 = bf16[1,256,256]{2,1,0:T(8,128)(2,1)} fusion(f32[256,256]{1,0:T(8,128)} %copy-done.2, bf16[1,256,256]{2,1,0:T(8,128)(2,1)S(1)} %copy-done.3), kind=kLoop, calls=%fused_computation.4 | loop fusion | flops 196608 | bytes 524288 | tf_op jit(solution)/shard_map/convert_element_type | solution.py:228
  108.1 7.5 %all-to-all-done.3 = bf16[64,8,128]{2,1,0:T(8,128)(2,1)S(1)} async-done(((bf16[64,8,128]{2,1,0:T(8,128)(2,1)}), bf16[64,8,128]{2,1,0:T(8,128)(2,1)S(1)}, u32[]{:S(2)}, u32[]{:S(2)}) %all-to-all-start.3) | async-done | bytes 131104 | tf_op jit(solution)/shard_map/all_to_all | solution.py:239
  115.6 0.1 copy.9
  115.7 0.7 reshape.24
  (10 shorter events, 0.1 us)
Async XLA Ops:
  0.6 13.3 %collective-permute-start = (bf16[1,3,32,256]{3,2,1,0:T(8,128)(2,1)}, bf16[1,3,32,256]{3,2,1,0:T(8,128)(2,1)S(1)}, u32[]{:S(2)}, u32[]{:S(2)}) collective-permute-start(bf16[1,3,32,256]{3,2,1,0:T(8,128)(2,1)} %bitcast.22), channel_id=1, source_target_pairs={{0,16},{16,0},{1,17},{17,1},{2,18},{18,2},{3,19},{19,3},{4,20},{20... | collective-permute-start | bytes 147464 | tf_op jit(solution)/shard_map/ppermute | solution.py:222
  9.4 4.4 %copy-start.3 = (bf16[1,256,256]{2,1,0:T(8,128)(2,1)S(1)}, bf16[1,256,256]{2,1,0:T(8,128)(2,1)}, u32[]{:S(2)}) copy-start(bf16[1,256,256]{2,1,0:T(8,128)(2,1)} %param.7) | copy-start | bytes 393220
  9.4 4.5 %copy-start.1 = (bf16[32,3,256]{2,0,1:T(8,128)(2,1)S(1)}, bf16[32,3,256]{2,0,1:T(8,128)(2,1)}, u32[]{:S(2)}) copy-start(bf16[32,3,256]{2,0,1:T(8,128)(2,1)} %param.13) | copy-start | bytes 147460
  9.5 29.1 %all-to-all-start = ((bf16[8,256,256]{2,1,0:T(8,128)(2,1)}), bf16[8,256,256]{2,1,0:T(8,128)(2,1)S(1)}, u32[]{:S(2)}, u32[]{:S(2)}) async-start(bf16[8,256,256]{2,1,0:T(8,128)(2,1)} %row_attention.1), calls=%async_computation | async-start | bytes 2097152 | tf_op jit(solution)/shard_map/all_to_all | solution.py:225
  13.9 34.8 %collective-permute-start.1 = (bf16[2,3,32,256]{3,2,1,0:T(8,128)(2,1)S(1)}, bf16[2,3,32,256]{3,2,1,0:T(8,128)(2,1)S(1)}, u32[]{:S(2)}, u32[]{:S(2)}) collective-permute-start(bf16[2,3,32,256]{3,2,1,0:T(8,128)(2,1)S(1)} %pack.4.pair_ref), channel_id=1, source_target_pairs={{256,0},{288,32},{320,64},{352,96},{384,128},{416,160},{448,192},{... | collective-permute-start | bytes 294920 | tf_op jit(solution)/shard_map/ppermute | solution.py:212
  29.4 19.3 %collective-permute-start.2 = (bf16[2,3,32,256]{3,2,1,0:T(8,128)(2,1)S(1)}, bf16[2,3,32,256]{3,2,1,0:T(8,128)(2,1)S(1)}, u32[]{:S(2)}, u32[]{:S(2)}) collective-permute-start(bf16[2,3,32,256]{3,2,1,0:T(8,128)(2,1)S(1)} %pack.4.pair_ref), channel_id=1, source_target_pairs={{384,0},{416,32},{448,64},{480,96},{0,128},{32,160},{64,192},{96,2... | collective-permute-start | bytes 294920 | tf_op jit(solution)/shard_map/ppermute | solution.py:212
  33.4 15.3 %collective-permute-start.3 = (bf16[2,3,32,256]{3,2,1,0:T(8,128)(2,1)S(1)}, bf16[2,3,32,256]{3,2,1,0:T(8,128)(2,1)S(1)}, u32[]{:S(2)}, u32[]{:S(2)}) collective-permute-start(bf16[2,3,32,256]{3,2,1,0:T(8,128)(2,1)S(1)} %pack.4.pair_ref), channel_id=1, source_target_pairs={{128,0},{160,32},{192,64},{224,96},{256,128},{288,160},{320,192},{... | collective-permute-start | bytes 294920 | tf_op jit(solution)/shard_map/ppermute | solution.py:212
  38.7 10.8 %copy-start.2 = (f32[256,256]{1,0:T(8,128)}, f32[256,256]{1,0:T(8,128)S(1)}, u32[]{:S(2)}) copy-start(f32[256,256]{1,0:T(8,128)S(1)} %convert_reduce_fusion) | copy-start | bytes 786436
  39.6 27.7 %all-to-all-start.1 = ((bf16[64,4,256]{2,1,0:T(4,128)(2,1)}), bf16[64,4,256]{2,1,0:T(4,128)(2,1)S(1)}, u32[]{:S(2)}, u32[]{:S(2)}) async-start(bf16[64,4,256]{2,1,0:T(4,128)(2,1)} %add_convert_fusion), calls=%async_computation.1 | async-start | bytes 262144 | tf_op jit(solution)/shard_map/all_to_all | solution.py:229
  49.6 23.6 %collective-permute-start.4 = (bf16[8,3,32,256]{3,2,1,0:T(8,128)(2,1)}, bf16[8,3,32,256]{3,2,1,0:T(8,128)(2,1)S(1)}, u32[]{:S(2)}, u32[]{:S(2)}) collective-permute-start(bf16[8,3,32,256]{3,2,1,0:T(8,128)(2,1)} %get-tuple-element.5.refs_0_), channel_id=1, source_target_pairs={{32,0},{64,32},{96,64},{128,96},{160,128},{192,160},{224,192},{256... | collective-permute-start | bytes 1179656 | tf_op jit(solution)/shard_map/ppermute | solution.py:212
  54.4 24.5 %collective-permute-start.5 = (bf16[8,3,32,256]{3,2,1,0:T(8,128)(2,1)}, bf16[8,3,32,256]{3,2,1,0:T(8,128)(2,1)}, u32[]{:S(2)}, u32[]{:S(2)}) collective-permute-start(bf16[8,3,32,256]{3,2,1,0:T(8,128)(2,1)} %get-tuple-element.5.refs_0_), channel_id=1, source_target_pairs={{480,0},{0,32},{32,64},{64,96},{96,128},{128,160},{160,192},{192,2... | collective-permute-start | bytes 1179656 | tf_op jit(solution)/shard_map/ppermute | solution.py:212
  56.3 20.6 %collective-permute-start.6 = (bf16[4,3,32,256]{3,2,1,0:T(8,128)(2,1)S(1)}, bf16[4,3,32,256]{3,2,1,0:T(8,128)(2,1)S(1)}, u32[]{:S(2)}, u32[]{:S(2)}) collective-permute-start(bf16[4,3,32,256]{3,2,1,0:T(8,128)(2,1)S(1)} %get-tuple-element.6), channel_id=1, source_target_pairs={{64,0},{96,32},{128,64},{160,96},{192,128},{224,160},{256,192},{28... | collective-permute-start | bytes 589832 | tf_op jit(solution)/shard_map/ppermute | solution.py:212
  60.5 16.3 %collective-permute-start.7 = (bf16[4,3,32,256]{3,2,1,0:T(8,128)(2,1)S(1)}, bf16[4,3,32,256]{3,2,1,0:T(8,128)(2,1)S(1)}, u32[]{:S(2)}, u32[]{:S(2)}) collective-permute-start(bf16[4,3,32,256]{3,2,1,0:T(8,128)(2,1)S(1)} %get-tuple-element.7), channel_id=1, source_target_pairs={{448,0},{480,32},{0,64},{32,96},{64,128},{96,160},{128,192},{160,2... | collective-permute-start | bytes 589832 | tf_op jit(solution)/shard_map/ppermute | solution.py:212
  68.4 20.0 %all-to-all-start.2 = ((bf16[8,256,256]{2,1,0:T(8,128)(2,1)}), bf16[8,256,256]{2,1,0:T(8,128)(2,1)S(1)}, u32[]{:S(2)}, u32[]{:S(2)}) async-start(bf16[8,256,256]{2,1,0:T(8,128)(2,1)} %broadcast_in_dim.12), calls=%async_computation.2 | async-start | bytes 2097152 | tf_op jit(solution)/shard_map/all_to_all | solution.py:233
  74.3 10.5 %collective-permute-start.8 = (bf16[16,3,32,256]{3,2,1,0:T(8,128)(2,1)S(1)}, bf16[16,3,32,256]{3,2,1,0:T(8,128)(2,1)S(1)}, u32[]{:S(2)}, u32[]{:S(2)}) collective-permute-start(bf16[16,3,32,256]{3,2,1,0:T(8,128)(2,1)S(1)} %pack.5.refs_0_), channel_id=1, source_target_pairs={{0,8},{8,0},{1,9},{9,1},{2,10},{10,2},{3,11},{11,3},{4,12},{12,4},... | collective-permute-start | bytes 2359304 | tf_op jit(solution)/shard_map/ppermute | solution.py:235
  76.9 11.4 %copy-start = (f32[2048]{0:T(1024)S(1)}, f32[2048]{0:T(1024)}, u32[]{:S(2)}) copy-start(f32[2048]{0:T(1024)} %param.12) | copy-start | bytes 24580
  76.9 6.2 %collective-permute-start.10 = (bf16[8,3,32,256]{3,2,1,0:T(8,128)(2,1)S(1)}, bf16[8,3,32,256]{3,2,1,0:T(8,128)(2,1)S(1)}, u32[]{:S(2)}, u32[]{:S(2)}) collective-permute-start(bf16[8,3,32,256]{3,2,1,0:T(8,128)(2,1)S(1)} %pack.7.refs_2_), channel_id=1, source_target_pairs={{0,8},{8,0},{1,9},{9,1},{2,10},{10,2},{3,11},{11,3},{4,12},{12,4},... | collective-permute-start | bytes 1179656 | tf_op jit(solution)/shard_map/ppermute | solution.py:235
  80.7 4.1 %collective-permute-start.9 = (bf16[8,3,32,256]{3,2,1,0:T(8,128)(2,1)}, bf16[8,3,32,256]{3,2,1,0:T(8,128)(2,1)}, u32[]{:S(2)}, u32[]{:S(2)}) collective-permute-start(bf16[8,3,32,256]{3,2,1,0:T(8,128)(2,1)} %pack.6.refs_1_), channel_id=1, source_target_pairs={{0,8},{8,0},{1,9},{9,1},{2,10},{10,2},{3,11},{11,3},{4,12},{12,4},... | collective-permute-start | bytes 1179656 | tf_op jit(solution)/shard_map/ppermute | solution.py:235
  92.3 23.3 %all-to-all-start.3 = ((bf16[64,8,128]{2,1,0:T(8,128)(2,1)}), bf16[64,8,128]{2,1,0:T(8,128)(2,1)S(1)}, u32[]{:S(2)}, u32[]{:S(2)}) async-start(bf16[64,8,128]{2,1,0:T(8,128)(2,1)} %column_attention.1), calls=%async_computation.3 | async-start | bytes 262144 | tf_op jit(solution)/shard_map/all_to_all | solution.py:239

commit v9 on v8

--- a/solution.py
+++ b/solution.py
@@ -14,6 +14,7 @@
 SEQ = ("z", "xh", "c")
 HD = ("y", "xl")
 TURN = 32
+FIRST = 16
 
 
 def softmax_mix(q, k, v, mask):
@@ -174,6 +175,8 @@
     t0 = lax.broadcasted_iota(jnp.int32, (n, n), 0)
     t1 = lax.broadcasted_iota(jnp.int32, (n, n), 1)
     cols_here = 4
+    shift_by = cols_here * FIRST
+    t0, t1 = (t0 + shift_by) & (n - 1), (t1 + shift_by) & (n - 1)
     mask = (t0 >= t1) & ((t0 & (cols_here - 1)) == (t1 & (cols_here - 1)))
     mixed = []
     for h in range(local // HEAD):
@@ -182,8 +185,12 @@
         mixed.append(one.reshape(n // cols_here, cols_here, HEAD))
     mixed = jnp.concatenate(mixed, axis=1).astype(jnp.bfloat16)
     rows = mixed.shape[0]
-    out_ref[: rows - TURN] = mixed[TURN:]
-    out_ref[rows - TURN :] = mixed[:TURN]
+    turn = (TURN - FIRST) % rows
+    if turn:
+        out_ref[: rows - turn] = mixed[turn:]
+        out_ref[rows - turn :] = mixed[:turn]
+    else:
+        out_ref[...] = mixed
 
 
 def column_part(where, x, gain, own, other):
@@ -221,13 +228,16 @@
     w = jnp.transpose(qkv_weight, (1, 0, 2))[None]
     theirs = lax.ppermute(w, "xh", [(0, 1), (1, 0)])
     partial = row_part(row_query[0], row_key[0], row_value[0], out_weight, heads)
-    pair = pack(w, theirs, weight=10**10)
+    pair = pack(w, theirs, weight=10**11)
     parts = lax.all_to_all(partial, HD, 0, 0, tiled=True)
     up8, down4, up4 = shift(pair, 8), shift(pair, -4), shift(pair, 4)
     stream = stream_in[0].astype(jnp.float32) + jnp.sum(parts.astype(jnp.float32), axis=0)
     stream_out = stream.astype(jnp.bfloat16)
-    columns = lax.all_to_all(stream_out.reshape(seq, here, local), SEQ, 0, 0, tiled=True)
-    eight, first, second = group(pair, up8, down4, up4, stream_out, 10**9)
+    blocks = stream_out.reshape(seq, here, local)
+    blocks = jnp.concatenate([blocks[FIRST:], blocks[:FIRST]], axis=0)
+    turned = [[(i + FIRST) % seq for i in range(seq)]]
+    columns = lax.all_to_all(blocks, SEQ, 0, 0, tiled=True, axis_index_groups=turned)
+    eight, first, second = group(pair, up8, down4, up4, stream_out, 10**10)
     up1, down1, up2, down2 = shift(eight, 1), shift(eight, -1), shift(first, 2), shift(second, -2)
     columns = columns.reshape(seq * here, local)
     x = lax.all_to_all(jnp.broadcast_to(columns[None], (heads,) + columns.shape), HD, 0, 0, tiled=True)

time: 117 us -> 119 us (1.017)
  starting transfers between devices: 82.3 us -> 89 us
  waiting for transfers between devices: 17.5 us -> 11.9 us
    all_to_all x1, starting transfers between devices: 14.1 us -> 18.4 us  [on_device(): lax.all_to_all(mixed, SEQ, 0, 0, tiled=True, axis_index_groups=turned)]
    all_to_all x1, waiting for transfers between devices: 4.8 us -> 0.55 us  [on_device(): lax.all_to_all(blocks, SEQ, 0, 0, tiled=True, axis_index_groups=turned)]
    all_to_all x1, waiting for transfers between devices: 3.61 us -> 0.82 us  [on_device(): lax.all_to_all(jnp.broadcast_to(columns[None], (heads,) + columns.shape),...]
    all_to_all x1, starting transfers between devices: 9.1 us -> 11.1 us  [on_device(): lax.all_to_all(blocks, SEQ, 0, 0, tiled=True, axis_index_groups=turned)]
    convert_element_type x3 -> x2, other arithmetic: 2.39 us -> 1.67 us  [on_device(): stream_out = stream.astype(jnp.bfloat16)]
  transfers between devices with their start and end apart: 15 -> 15, of which waited for: 4 -> 5; matrix products, arithmetic and copies ran while one was open for 3% -> 3% of each run, Pallas kernels for 6% -> 6%
where the time goes in v9:
time: 119 us; the launch traced here: 118 us
  starting transfers between devices  89 us (75%)
  waiting for transfers between devices  11.9 us (10%)
  Pallas kernels  10.9 us (9%)
  local copies, waits for them, and re-layouts  2.73 us (2%)
  other arithmetic  2.65 us (2%)
    ppermute x7, starting transfers between devices, shift(): return lax.ppermute(x, 'z', [((i + d) % 16, i) for i in range(16)])  37.1 us
    all_to_all x1, starting transfers between devices, on_device(): lax.all_to_all(mixed, SEQ, 0, 0, tiled=True, axis_index_groups=turned)  18.4 us
    all_to_all x1, starting transfers between devices, on_device(): lax.all_to_all(blocks, SEQ, 0, 0, tiled=True, axis_index_groups=turned)  11.1 us
    ppermute x3, starting transfers between devices, on_device(): other = [lax.ppermute(piece, 'c', [(0, 1), (1, 0)]) for piece in own]  7.65 us
    all_to_all x1, waiting for transfers between devices, on_device(): lax.all_to_all(mixed, SEQ, 0, 0, tiled=True, axis_index_groups=turned)  7.5 us
    ppermute x1, starting transfers between devices, on_device(): theirs = lax.ppermute(w, 'xh', [(0, 1), (1, 0)])  5.48 us
    all_to_all x1, starting transfers between devices, on_device(): lax.all_to_all(jnp.broadcast_to(columns[None], (heads,) + columns.shape),...  4.81 us
    all_to_all x1, starting transfers between devices, on_device(): parts = lax.all_to_all(partial, HD, 0, 0, tiled=True)  4.36 us
  transfers between devices with their start and end apart: 15, of which 5 were waited for; matrix products, arithmetic and copies ran while one was open for 3% of the time, Pallas kernels for 6%

profile of v9, /device:TPU:1, one launch (start us, length us, event | category | flops | bytes accessed | tf_op | source)
XLA Modules:
  0.0 118.1 jit_solution(2395332465341709551)
XLA Ops:
  0.6 5.5 %collective-permute-start = (bf16[1,3,32,256]{3,2,1,0:T(8,128)(2,1)}, bf16[1,3,32,256]{3,2,1,0:T(8,128)(2,1)S(1)}, u32[]{:S(2)}, u32[]{:S(2)}) collective-permute-start(bf16[1,3,32,256]{3,2,1,0:T(8,128)(2,1)} %bitcast.22), channel_id=1, source_target_pairs={{0,16},{16,0},{1,17},{17,1},{2,18},{18,2},{3,19},{19,3},{4,20},{20... | collective-permute-start | bytes 147464 | tf_op jit(solution)/shard_map/ppermute | solution.py:229
  6.1 3.3 %row_attention.1 = bf16[8,256,256]{2,1,0:T(8,128)(2,1)} custom-call(bf16[256,256]{1,0:T(8,128)(2,1)} %bitcast.25, bf16[256,256]{1,0:T(8,128)(2,1)} %bitcast.26, bf16[256,256]{1,0:T(8,128)(2,1)} %bitcast.27, bf16[256,2048]{1,0:T(8,128)(2,1)} %w_hbm.1), custom_call_target="tpu_custom_call" | custom-call | flops 335544320 | bytes 3145728 | tf_op jit(solution)/shard_map/row_attention/pallas_call | solution.py:61
  9.4 0.0 copy-start.1
  9.4 4.4 %all-to-all-start = ((bf16[8,256,256]{2,1,0:T(8,128)(2,1)}), bf16[8,256,256]{2,1,0:T(8,128)(2,1)S(1)}, u32[]{:S(2)}, u32[]{:S(2)}) async-start(bf16[8,256,256]{2,1,0:T(8,128)(2,1)} %row_attention.1), calls=%async_computation | async-start | bytes 2097152 | tf_op jit(solution)/shard_map/all_to_all | solution.py:232
  13.8 0.0 collective-permute-done.refs_1_
  13.8 0.0 copy-done.1
  13.8 0.0 copy-start.3
  13.9 15.6 %collective-permute-start.1 = (bf16[2,3,32,256]{3,2,1,0:T(8,128)(2,1)S(1)}, bf16[2,3,32,256]{3,2,1,0:T(8,128)(2,1)S(1)}, u32[]{:S(2)}, u32[]{:S(2)}) collective-permute-start(bf16[2,3,32,256]{3,2,1,0:T(8,128)(2,1)S(1)} %pack.4.pair_ref), channel_id=1, source_target_pairs={{256,0},{288,32},{320,64},{352,96},{384,128},{416,160},{448,192},{... | collective-permute-start | bytes 294920 | tf_op jit(solution)/shard_map/ppermute | solution.py:219
  29.4 4.0 %collective-permute-start.2 = (bf16[2,3,32,256]{3,2,1,0:T(8,128)(2,1)S(1)}, bf16[2,3,32,256]{3,2,1,0:T(8,128)(2,1)S(1)}, u32[]{:S(2)}, u32[]{:S(2)}) collective-permute-start(bf16[2,3,32,256]{3,2,1,0:T(8,128)(2,1)S(1)} %pack.4.pair_ref), channel_id=1, source_target_pairs={{384,0},{416,32},{448,64},{480,96},{0,128},{32,160},{64,192},{96,2... | collective-permute-start | bytes 294920 | tf_op jit(solution)/shard_map/ppermute | solution.py:219
  33.5 5.2 %collective-permute-start.3 = (bf16[2,3,32,256]{3,2,1,0:T(8,128)(2,1)S(1)}, bf16[2,3,32,256]{3,2,1,0:T(8,128)(2,1)S(1)}, u32[]{:S(2)}, u32[]{:S(2)}) collective-permute-start(bf16[2,3,32,256]{3,2,1,0:T(8,128)(2,1)S(1)} %pack.4.pair_ref), channel_id=1, source_target_pairs={{128,0},{160,32},{192,64},{224,96},{256,128},{288,160},{320,192},{... | collective-permute-start | bytes 294920 | tf_op jit(solution)/shard_map/ppermute | solution.py:219
  38.6 0.0 all-to-all-done
  38.7 0.1 convert_reduce_fusion
  38.8 0.7 copy-done.2
  39.5 0.0 copy-done.3
  39.6 0.7 pad_maximum_fusion
  40.4 11.1 %all-to-all-start.1 = ((bf16[64,4,256]{2,1,0:T(4,128)(2,1)}), bf16[64,4,256]{2,1,0:T(4,128)(2,1)S(1)}, u32[]{:S(2)}, u32[]{:S(2)}) async-start(bf16[64,4,256]{2,1,0:T(4,128)(2,1)} %pad_maximum_fusion), calls=%async_computation.1 | async-start | bytes 262144 | tf_op jit(solution)/shard_map/all_to_all | solution.py:239
  51.5 0.0 collective-permute-done.1.up8_ref
  51.5 0.0 collective-permute-done.2.down4_ref
  51.5 0.0 collective-permute-done.3.up4_ref
  51.5 0.8 group.1
  52.4 4.3 %collective-permute-start.4 = (bf16[8,3,32,256]{3,2,1,0:T(8,128)(2,1)}, bf16[8,3,32,256]{3,2,1,0:T(8,128)(2,1)S(1)}, u32[]{:S(2)}, u32[]{:S(2)}) collective-permute-start(bf16[8,3,32,256]{3,2,1,0:T(8,128)(2,1)} %get-tuple-element.5.refs_0_), channel_id=1, source_target_pairs={{32,0},{64,32},{96,64},{128,96},{160,128},{192,160},{224,192},{256... | collective-permute-start | bytes 1179656 | tf_op jit(solution)/shard_map/ppermute | solution.py:219
  56.6 1.9 %collective-permute-start.5 = (bf16[8,3,32,256]{3,2,1,0:T(8,128)(2,1)}, bf16[8,3,32,256]{3,2,1,0:T(8,128)(2,1)}, u32[]{:S(2)}, u32[]{:S(2)}) collective-permute-start(bf16[8,3,32,256]{3,2,1,0:T(8,128)(2,1)} %get-tuple-element.5.refs_0_), channel_id=1, source_target_pairs={{480,0},{0,32},{32,64},{64,96},{96,128},{128,160},{160,192},{192,2... | collective-permute-start | bytes 1179656 | tf_op jit(solution)/shard_map/ppermute | solution.py:219
  58.6 4.2 %collective-permute-start.6 = (bf16[4,3,32,256]{3,2,1,0:T(8,128)(2,1)S(1)}, bf16[4,3,32,256]{3,2,1,0:T(8,128)(2,1)S(1)}, u32[]{:S(2)}, u32[]{:S(2)}) collective-permute-start(bf16[4,3,32,256]{3,2,1,0:T(8,128)(2,1)S(1)} %get-tuple-element.6), channel_id=1, source_target_pairs={{64,0},{96,32},{128,64},{160,96},{192,128},{224,160},{256,192},{28... | collective-permute-start | bytes 589832 | tf_op jit(solution)/shard_map/ppermute | solution.py:219
  62.8 1.9 %collective-permute-start.7 = (bf16[4,3,32,256]{3,2,1,0:T(8,128)(2,1)S(1)}, bf16[4,3,32,256]{3,2,1,0:T(8,128)(2,1)S(1)}, u32[]{:S(2)}, u32[]{:S(2)}) collective-permute-start(bf16[4,3,32,256]{3,2,1,0:T(8,128)(2,1)S(1)} %get-tuple-element.7), channel_id=1, source_target_pairs={{448,0},{480,32},{0,64},{32,96},{64,128},{96,160},{128,192},{160,2... | collective-permute-start | bytes 589832 | tf_op jit(solution)/shard_map/ppermute | solution.py:219
  64.7 0.6 all-to-all-done.1
  65.3 1.1 broadcast_in_dim.12
  66.4 4.8 %all-to-all-start.2 = ((bf16[8,256,256]{2,1,0:T(8,128)(2,1)}), bf16[8,256,256]{2,1,0:T(8,128)(2,1)S(1)}, u32[]{:S(2)}, u32[]{:S(2)}) async-start(bf16[8,256,256]{2,1,0:T(8,128)(2,1)} %broadcast_in_dim.12), calls=%async_computation.2 | async-start | bytes 2097152 | tf_op jit(solution)/shard_map/all_to_all | solution.py:243
  71.2 0.0 collective-permute-done.4.refs_1_
  71.2 1.0 pack.5.refs_0_
  72.3 2.9 %collective-permute-start.8 = (bf16[16,3,32,256]{3,2,1,0:T(8,128)(2,1)S(1)}, bf16[16,3,32,256]{3,2,1,0:T(8,128)(2,1)S(1)}, u32[]{:S(2)}, u32[]{:S(2)}) collective-permute-start(bf16[16,3,32,256]{3,2,1,0:T(8,128)(2,1)S(1)} %pack.5.refs_0_), channel_id=1, source_target_pairs={{0,8},{8,0},{1,9},{9,1},{2,10},{10,2},{3,11},{11,3},{4,12},{12,4},... | collective-permute-start | bytes 2359304 | tf_op jit(solution)/shard_map/ppermute | solution.py:245
  75.1 0.0 collective-permute-done.6.refs_0_
  75.1 1.1 collective-permute-done.7.refs_1_
  76.2 0.0 copy-start
  76.3 2.9 %collective-permute-start.10 = (bf16[8,3,32,256]{3,2,1,0:T(8,128)(2,1)S(1)}, bf16[8,3,32,256]{3,2,1,0:T(8,128)(2,1)S(1)}, u32[]{:S(2)}, u32[]{:S(2)}) collective-permute-start(bf16[8,3,32,256]{3,2,1,0:T(8,128)(2,1)S(1)} %pack.7.refs_2_), channel_id=1, source_target_pairs={{0,8},{8,0},{1,9},{9,1},{2,10},{10,2},{3,11},{11,3},{4,12},{12,4},... | collective-permute-start | bytes 1179656 | tf_op jit(solution)/shard_map/ppermute | solution.py:245
  79.1 0.0 collective-permute-done.5.refs_0_
  79.2 1.8 %pack.6.refs_1_ = bf16[8,3,32,256]{3,2,1,0:T(8,128)(2,1)} custom-call(bf16[8,3,32,256]{3,2,1,0:T(8,128)(2,1)} %collective-permute-done.5.refs_0_), custom_call_target="tpu_custom_call" | custom-call | flops 3000000000 | bytes 786432 | tf_op jit(solution)/shard_map/pack/pallas_call | solution.py:99
  80.9 1.9 %collective-permute-start.9 = (bf16[8,3,32,256]{3,2,1,0:T(8,128)(2,1)}, bf16[8,3,32,256]{3,2,1,0:T(8,128)(2,1)}, u32[]{:S(2)}, u32[]{:S(2)}) collective-permute-start(bf16[8,3,32,256]{3,2,1,0:T(8,128)(2,1)} %pack.6.refs_1_), channel_id=1, source_target_pairs={{0,8},{8,0},{1,9},{9,1},{2,10},{10,2},{3,11},{11,3},{4,12},{12,4},... | collective-permute-start | bytes 1179656 | tf_op jit(solution)/shard_map/ppermute | solution.py:245
  82.9 0.1 pad_add_fusion.where_ref
  82.9 0.0 collective-permute-done.10.refs_5_
  83.0 1.9 %collective-permute-done.9.refs_4_ = bf16[8,3,32,256]{3,2,1,0:T(8,128)(2,1)} collective-permute-done((bf16[8,3,32,256]{3,2,1,0:T(8,128)(2,1)}, bf16[8,3,32,256]{3,2,1,0:T(8,128)(2,1)}, u32[]{:S(2)}, u32[]{:S(2)}) %collective-permute-start.9) | collective-permute-done | bytes 393248 | tf_op jit(solution)/shard_map/ppermute | solution.py:245
  84.9 0.0 collective-permute-done.8.refs_3_
  84.9 0.8 all-to-all-done.2.x_ref
  85.7 3.9 %column_attention.1 = bf16[64,8,128]{2,1,0:T(8,128)(2,1)} custom-call(s32[3]{0:T(128)S(1)} %pad_add_fusion.where_ref, bf16[8,256,256]{2,1,0:T(8,128)(2,1)S(1)} %all-to-all-done.2.x_ref, f32[1,2048]{1,0:T(1,128)S(1)} %bitcast.21, bf16[16,3,32,256]{3,2,1,0:T(8,128)(2,1)S(1)} %pack.5.refs_0_, bf16[8,3,32,256]{3,2,1,0:T(8,128)(2,1)} %pack.6.refs_1_, ...), custom_call_target="tpu_custom_call" | custom-call | flops 805306368 | bytes 5242880 | tf_op jit(solution)/shard_map/column_attention/pallas_call | solution.py:201
  89.7 18.4 %all-to-all-start.3 = ((bf16[64,8,128]{2,1,0:T(8,128)(2,1)}), bf16[64,8,128]{2,1,0:T(8,128)(2,1)S(1)}, u32[]{:S(2)}, u32[]{:S(2)}) async-start(bf16[64,8,128]{2,1,0:T(8,128)(2,1)} %column_attention.1), calls=%async_computation.3 | async-start | bytes 262144 | tf_op jit(solution)/shard_map/all_to_all | solution.py:249
  108.1 1.6 %fusion = bf16[1,256,256]{2,1,0:T(8,128)(2,1)} fusion(bf16[1,256,256]{2,1,0:T(8,128)(2,1)S(1)} %copy-done.3, f32[256,256]{1,0:T(8,128)} %copy-done.2), kind=kLoop, calls=%fused_computation.3 | loop fusion | flops 196608 | bytes 524288 | tf_op jit(solution)/shard_map/convert_element_type | solution.py:235
  109.7 7.5 %all-to-all-done.3 = bf16[64,8,128]{2,1,0:T(8,128)(2,1)S(1)} async-done(((bf16[64,8,128]{2,1,0:T(8,128)(2,1)}), bf16[64,8,128]{2,1,0:T(8,128)(2,1)S(1)}, u32[]{:S(2)}, u32[]{:S(2)}) %all-to-all-start.3) | async-done | bytes 131104 | tf_op jit(solution)/shard_map/all_to_all | solution.py:249
  117.3 0.1 copy.9
  117.4 0.7 reshape.22
  (12 shorter events, 0.2 us)
Async XLA Ops:
  0.6 13.2 %collective-permute-start = (bf16[1,3,32,256]{3,2,1,0:T(8,128)(2,1)}, bf16[1,3,32,256]{3,2,1,0:T(8,128)(2,1)S(1)}, u32[]{:S(2)}, u32[]{:S(2)}) collective-permute-start(bf16[1,3,32,256]{3,2,1,0:T(8,128)(2,1)} %bitcast.22), channel_id=1, source_target_pairs={{0,16},{16,0},{1,17},{17,1},{2,18},{18,2},{3,19},{19,3},{4,20},{20... | collective-permute-start | bytes 147464 | tf_op jit(solution)/shard_map/ppermute | solution.py:229
  9.4 4.4 %copy-start.1 = (bf16[32,3,256]{2,0,1:T(8,128)(2,1)S(1)}, bf16[32,3,256]{2,0,1:T(8,128)(2,1)}, u32[]{:S(2)}) copy-start(bf16[32,3,256]{2,0,1:T(8,128)(2,1)} %param.13) | copy-start | bytes 147460
  9.4 29.2 %all-to-all-start = ((bf16[8,256,256]{2,1,0:T(8,128)(2,1)}), bf16[8,256,256]{2,1,0:T(8,128)(2,1)S(1)}, u32[]{:S(2)}, u32[]{:S(2)}) async-start(bf16[8,256,256]{2,1,0:T(8,128)(2,1)} %row_attention.1), calls=%async_computation | async-start | bytes 2097152 | tf_op jit(solution)/shard_map/all_to_all | solution.py:232
  13.8 25.7 %copy-start.3 = (bf16[1,256,256]{2,1,0:T(8,128)(2,1)S(1)}, bf16[1,256,256]{2,1,0:T(8,128)(2,1)}, u32[]{:S(2)}) copy-start(bf16[1,256,256]{2,1,0:T(8,128)(2,1)} %param.7) | copy-start | bytes 393220
  13.9 37.7 %collective-permute-start.1 = (bf16[2,3,32,256]{3,2,1,0:T(8,128)(2,1)S(1)}, bf16[2,3,32,256]{3,2,1,0:T(8,128)(2,1)S(1)}, u32[]{:S(2)}, u32[]{:S(2)}) collective-permute-start(bf16[2,3,32,256]{3,2,1,0:T(8,128)(2,1)S(1)} %pack.4.pair_ref), channel_id=1, source_target_pairs={{256,0},{288,32},{320,64},{352,96},{384,128},{416,160},{448,192},{... | collective-permute-start | bytes 294920 | tf_op jit(solution)/shard_map/ppermute | solution.py:219
  29.4 22.1 %collective-permute-start.2 = (bf16[2,3,32,256]{3,2,1,0:T(8,128)(2,1)S(1)}, bf16[2,3,32,256]{3,2,1,0:T(8,128)(2,1)S(1)}, u32[]{:S(2)}, u32[]{:S(2)}) collective-permute-start(bf16[2,3,32,256]{3,2,1,0:T(8,128)(2,1)S(1)} %pack.4.pair_ref), channel_id=1, source_target_pairs={{384,0},{416,32},{448,64},{480,96},{0,128},{32,160},{64,192},{96,2... | collective-permute-start | bytes 294920 | tf_op jit(solution)/shard_map/ppermute | solution.py:219
  33.5 18.1 %collective-permute-start.3 = (bf16[2,3,32,256]{3,2,1,0:T(8,128)(2,1)S(1)}, bf16[2,3,32,256]{3,2,1,0:T(8,128)(2,1)S(1)}, u32[]{:S(2)}, u32[]{:S(2)}) collective-permute-start(bf16[2,3,32,256]{3,2,1,0:T(8,128)(2,1)S(1)} %pack.4.pair_ref), channel_id=1, source_target_pairs={{128,0},{160,32},{192,64},{224,96},{256,128},{288,160},{320,192},{... | collective-permute-start | bytes 294920 | tf_op jit(solution)/shard_map/ppermute | solution.py:219
  38.8 0.7 copy-start.2
  40.4 24.9 %all-to-all-start.1 = ((bf16[64,4,256]{2,1,0:T(4,128)(2,1)}), bf16[64,4,256]{2,1,0:T(4,128)(2,1)S(1)}, u32[]{:S(2)}, u32[]{:S(2)}) async-start(bf16[64,4,256]{2,1,0:T(4,128)(2,1)} %pad_maximum_fusion), calls=%async_computation.1 | async-start | bytes 262144 | tf_op jit(solution)/shard_map/all_to_all | solution.py:239
  52.4 18.9 %collective-permute-start.4 = (bf16[8,3,32,256]{3,2,1,0:T(8,128)(2,1)}, bf16[8,3,32,256]{3,2,1,0:T(8,128)(2,1)S(1)}, u32[]{:S(2)}, u32[]{:S(2)}) collective-permute-start(bf16[8,3,32,256]{3,2,1,0:T(8,128)(2,1)} %get-tuple-element.5.refs_0_), channel_id=1, source_target_pairs={{32,0},{64,32},{96,64},{128,96},{160,128},{192,160},{224,192},{256... | collective-permute-start | bytes 1179656 | tf_op jit(solution)/shard_map/ppermute | solution.py:219
  56.6 22.5 %collective-permute-start.5 = (bf16[8,3,32,256]{3,2,1,0:T(8,128)(2,1)}, bf16[8,3,32,256]{3,2,1,0:T(8,128)(2,1)}, u32[]{:S(2)}, u32[]{:S(2)}) collective-permute-start(bf16[8,3,32,256]{3,2,1,0:T(8,128)(2,1)} %get-tuple-element.5.refs_0_), channel_id=1, source_target_pairs={{480,0},{0,32},{32,64},{64,96},{96,128},{128,160},{160,192},{192,2... | collective-permute-start | bytes 1179656 | tf_op jit(solution)/shard_map/ppermute | solution.py:219
  58.6 16.6 %collective-permute-start.6 = (bf16[4,3,32,256]{3,2,1,0:T(8,128)(2,1)S(1)}, bf16[4,3,32,256]{3,2,1,0:T(8,128)(2,1)S(1)}, u32[]{:S(2)}, u32[]{:S(2)}) collective-permute-start(bf16[4,3,32,256]{3,2,1,0:T(8,128)(2,1)S(1)} %get-tuple-element.6), channel_id=1, source_target_pairs={{64,0},{96,32},{128,64},{160,96},{192,128},{224,160},{256,192},{28... | collective-permute-start | bytes 589832 | tf_op jit(solution)/shard_map/ppermute | solution.py:219
  62.8 13.4 %collective-permute-start.7 = (bf16[4,3,32,256]{3,2,1,0:T(8,128)(2,1)S(1)}, bf16[4,3,32,256]{3,2,1,0:T(8,128)(2,1)S(1)}, u32[]{:S(2)}, u32[]{:S(2)}) collective-permute-start(bf16[4,3,32,256]{3,2,1,0:T(8,128)(2,1)S(1)} %get-tuple-element.7), channel_id=1, source_target_pairs={{448,0},{480,32},{0,64},{32,96},{64,128},{96,160},{128,192},{160,2... | collective-permute-start | bytes 589832 | tf_op jit(solution)/shard_map/ppermute | solution.py:219
  66.4 19.3 %all-to-all-start.2 = ((bf16[8,256,256]{2,1,0:T(8,128)(2,1)}), bf16[8,256,256]{2,1,0:T(8,128)(2,1)S(1)}, u32[]{:S(2)}, u32[]{:S(2)}) async-start(bf16[8,256,256]{2,1,0:T(8,128)(2,1)} %broadcast_in_dim.12), calls=%async_computation.2 | async-start | bytes 2097152 | tf_op jit(solution)/shard_map/all_to_all | solution.py:243
  72.3 12.6 %collective-permute-start.8 = (bf16[16,3,32,256]{3,2,1,0:T(8,128)(2,1)S(1)}, bf16[16,3,32,256]{3,2,1,0:T(8,128)(2,1)S(1)}, u32[]{:S(2)}, u32[]{:S(2)}) collective-permute-start(bf16[16,3,32,256]{3,2,1,0:T(8,128)(2,1)S(1)} %pack.5.refs_0_), channel_id=1, source_target_pairs={{0,8},{8,0},{1,9},{9,1},{2,10},{10,2},{3,11},{11,3},{4,12},{12,4},... | collective-permute-start | bytes 2359304 | tf_op jit(solution)/shard_map/ppermute | solution.py:245
  76.2 9.5 %copy-start = (f32[2048]{0:T(1024)S(1)}, f32[2048]{0:T(1024)}, u32[]{:S(2)}) copy-start(f32[2048]{0:T(1024)} %param.12) | copy-start | bytes 24580
  76.3 6.7 %collective-permute-start.10 = (bf16[8,3,32,256]{3,2,1,0:T(8,128)(2,1)S(1)}, bf16[8,3,32,256]{3,2,1,0:T(8,128)(2,1)S(1)}, u32[]{:S(2)}, u32[]{:S(2)}) collective-permute-start(bf16[8,3,32,256]{3,2,1,0:T(8,128)(2,1)S(1)} %pack.7.refs_2_), channel_id=1, source_target_pairs={{0,8},{8,0},{1,9},{9,1},{2,10},{10,2},{3,11},{11,3},{4,12},{12,4},... | collective-permute-start | bytes 1179656 | tf_op jit(solution)/shard_map/ppermute | solution.py:245
  80.9 3.9 %collective-permute-start.9 = (bf16[8,3,32,256]{3,2,1,0:T(8,128)(2,1)}, bf16[8,3,32,256]{3,2,1,0:T(8,128)(2,1)}, u32[]{:S(2)}, u32[]{:S(2)}) collective-permute-start(bf16[8,3,32,256]{3,2,1,0:T(8,128)(2,1)} %pack.6.refs_1_), channel_id=1, source_target_pairs={{0,8},{8,0},{1,9},{9,1},{2,10},{10,2},{3,11},{11,3},{4,12},{12,4},... | collective-permute-start | bytes 1179656 | tf_op jit(solution)/shard_map/ppermute | solution.py:245
  89.7 27.6 %all-to-all-start.3 = ((bf16[64,8,128]{2,1,0:T(8,128)(2,1)}), bf16[64,8,128]{2,1,0:T(8,128)(2,1)S(1)}, u32[]{:S(2)}, u32[]{:S(2)}) async-start(bf16[64,8,128]{2,1,0:T(8,128)(2,1)} %column_attention.1), calls=%async_computation.3 | async-start | bytes 262144 | tf_op jit(solution)/shard_map/all_to_all | solution.py:249
